TPU v7x, 32 devices: a whole 2x2x4 slice. The times are simulated.
32 devices in a mesh: pair: 8 (over z, y), virt: 4 (over x, core).
Axes of the slice: x: 2, y: 2, z: 4, core: 2. Of those that a mesh axis runs over, the one named last changes fastest.
Arguments:
- amplitudes: bfloat16 [2, 112, 960, 960], P(None, 'pair', None, 'virt'), may hold values from -6 to 6
- integrals: bfloat16 [112, 960, 2, 960], P('pair', 'virt'), may hold values from -0.02734375 to 0.02734375
Outputs:
- residual_tile: float32 [2, 960, 2, 960], P(None, 'pair', None, 'virt')
All inputs are finite; a program needn't handle non-finite values.
Results may differ from a plain program's by a relative error of at most 0.0003.
Values may be sent and summed in bfloat16 or wider, within the bound.
No kernel may reach another device: no remote copies, remote signals or barrier semaphores. Data moves between devices by JAX's collectives and lax.ppermute only.
A program may use at most 320 MiB of HBM per device.

v0:
```python
import jax
import jax.numpy as jnp
from jax import lax
from jax.sharding import PartitionSpec as P


def shards(amplitudes, integrals):
    regrouped = lax.all_to_all(amplitudes, "pair", split_axis=2, concat_axis=1, tiled=True)
    partial_sum = jnp.einsum(
        "ikac,kcjb->iajb",
        regrouped,
        lax.all_gather(integrals, "pair", axis=0, tiled=True),
        preferred_element_type=jnp.float32,
    )
    mirrored = lax.all_to_all(partial_sum, "pair", split_axis=3, concat_axis=1, tiled=True)
    symmetric = partial_sum + mirrored.transpose(2, 3, 0, 1)
    return lax.psum_scatter(symmetric, "virt", scatter_dimension=3, tiled=True)


def solution(mesh):
    placed = (P(None, "pair", None, "virt"), P("pair", "virt", None, None))
    return jax.shard_map(
        shards, mesh=mesh, in_specs=placed, out_specs=P(None, "pair", None, "virt"), check_vma=False
    )
```

profile of v0, /device:TPU:2, one launch (start us, length us, event | category | flops | bytes accessed | tf_op | source)
XLA Modules:
  0.0 2414.0 jit_solution(8093663452934429012)
XLA Ops:
  6.5 0.0 all-gather.2.cloned.1.call-start
  6.5 14.8 copy.9
  21.3 0.0 all-gather.2.cloned.1.call-update
  21.3 0.0 reduce-scatter.4.cloned.1.call-start
  21.4 20.8 copy.7
  42.2 621.4 %all_to_all.36 = bf16[2,14,960,240]{3,1,0,2:T(8,128)(2,1)S(1)} all-to-all(bf16[2,14,960,240]{3,1,0,2:T(8,128)(2,1)S(1)} %copy.7), channel_id=1, replica_groups=mesh['pair'=8,'virt'=4] {'pair'}, dimensions={2} | all-to-all | bytes 25804800 | tf_op jit(solution)/shard_map/all_to_all | solution.py:8
  663.5 16.9 copy.8
  680.4 1583.9 %all-gather.2.cloned.1.call-done = bf16[112,240,2,960]{3,1,0,2:T(8,128)(2,1)} async-done(((bf16[14,240,2,960]{3,1,0,2:T(8,128)(2,1)}), bf16[112,240,2,960]{3,1,0,2:T(8,128)(2,1)}) %all-gather.2.cloned.1.call-update) | async-done | bytes 103219216 | tf_op jit(solution)/shard_map/all_gather | solution.py:12
  2264.3 44.3 %fusion.2 = f32[2,120,2,960]{3,1,2,0:T(8,128)S(1)} fusion(bf16[2,112,120,240,1]{3,2,1,4,0:T(8,128)(2,1)} %bitcast.31, bf16[112,240,2,960]{3,1,0,2:T(8,128)(2,1)} %all-gather.2.cloned.1.call-done), kind=kOutput, calls=%fused_computation.4 | convolution fusion | flops 24772608000 | bytes 117964800 | tf_op jit(solution)/shard_map/ikac,kcjb->iajb/dot_general | solution.py:9
  2308.6 2.3 copy.10
  2310.9 50.5 %all_to_all.37 = f32[2,120,2,960]{1,2,0,3:T(2,128)S(1)} all-to-all(f32[2,120,2,960]{1,2,0,3:T(2,128)} %copy.10), channel_id=1, replica_groups=mesh['pair'=8,'virt'=4] {'pair'}, dimensions={3} | all-to-all | bytes 3686400 | tf_op jit(solution)/shard_map/all_to_all | solution.py:15
  2361.4 2.4 copy.19
  2363.9 2.8 all_to_all.33
  2366.7 3.2 bitcast_add_fusion
  2369.8 3.4 copy.15
  2373.2 2.8 reshape.3
  2376.0 0.0 reduce-scatter.4.cloned.1.call-update
  2376.0 28.3 %reduce-scatter.4.cloned.1.call-done = f32[240,480]{1,0:T(8,128)} async-done(((f32[960,480]{1,0:T(8,128)}), f32[240,480]{1,0:T(8,128)}) %reduce-scatter.4.cloned.1.call-update) | async-done | bytes 460816
  2404.3 1.6 reshape.4
  2406.0 1.2 copy.12
Async XLA Ops:
  6.5 2257.8 %all-gather.2.cloned.1.call-start = ((), (), s32[]{:S(2)}) async-start(), calls=%async_computation.3 | async-start | bytes 123863040 | tf_op jit(solution)/shard_map/all_gather | solution.py:12
  21.3 2383.0 %reduce-scatter.4.cloned.1.call-start = ((), (), s32[]{:S(2)}) async-start(), calls=%async_computation.4 | async-start | bytes 2457600
Sparse Core Ops, SparseCore 0:
  21.5 2242.8 all-gather.1
  2376.2 28.1 reduce-scatter.3
where the time goes:
time: 2420 us; the launch traced here: 2410 us
  waiting for transfers between devices  1610 us (67%)
  blocking collectives  672 us (28%)
  local copies, waits for them, and re-layouts  68.9 us (3%)
  matrix products  44.3 us (2%)
    all_gather x1, waiting for transfers between devices, shards(): lax.all_gather(integrals, 'pair', axis=0, tiled=True)  1580 us
    all_to_all x1, blocking collectives, shards(): lax.all_to_all(amplitudes, 'pair', split_axis=2, concat_axis=1, tiled=True)  621 us
    all_to_all x1, blocking collectives, shards(): lax.all_to_all(partial_sum, 'pair', split_axis=3, concat_axis=1, tiled=True)  50.5 us
  transfers between devices with their start and end apart: 2, of which 2 were waited for; matrix products, arithmetic and copies ran while one was open for 2% of the time, Pallas kernels for 0%

commit v1 on v0

v1 whole, which is shorter than its diff:
```python
import jax
import jax.numpy as jnp
from jax import lax
from jax.sharding import PartitionSpec as P

AXES = ("pair", "virt")
TOP = 12


def products(amplitudes, integrals):
    return [
        [
            jnp.einsum("kac,kcb->ab", amplitudes[i], integrals[:, :, j], preferred_element_type=jnp.float32)
            for j in range(2)
        ]
        for i in range(2)
    ]


def with_extras(block, diagonal, nv, width):
    rows, cols = block.shape
    largest = jnp.maximum(jnp.max(jnp.abs(block)), jnp.max(jnp.abs(diagonal)))
    parts = block.reshape(rows, nv, cols // nv).transpose(1, 0, 2)
    extra = jnp.stack([diagonal, jnp.full((rows,), largest)], axis=1)
    extra = jnp.pad(extra, ((0, 0), (0, width - cols // nv - 2)))
    return jnp.concatenate([parts, jnp.broadcast_to(extra, (nv, *extra.shape))], axis=2)


def coded(values, bound, at):
    exponent = jnp.clip(jnp.floor(jnp.log2(jnp.maximum(bound, 1e-30))), -100.0, 100.0)
    column = lax.broadcasted_iota(jnp.int32, values.shape, values.ndim - 1)
    return jnp.where(column == at, exponent, values * jnp.exp2(TOP - exponent)).astype(jnp.float16)


def decoded(block, at):
    exponent = block[..., at : at + 1].astype(jnp.float32)
    values = block.astype(jnp.float32) * jnp.exp2(exponent - TOP)
    column = lax.broadcasted_iota(jnp.int32, values.shape, values.ndim - 1)
    return jnp.where(column == at, jnp.exp2(exponent + 1.0), values)


def solution(mesh):
    np_, nv = mesh.shape["pair"], mesh.shape["virt"]
    nx, nz, ratio = nv // 2, np_ // 2, np_ // nv

    def permutation(move):
        pairs = []
        for p in range(np_):
            for v in range(nv):
                q, w = move(p, v)
                pairs.append((p * nv + v, q * nv + w))
        return pairs

    swap_core = permutation(lambda p, v: (p, v ^ 1))

    def send(block, pairs):
        return lax.ppermute(block, AXES, pairs)

    def reduced(chunk, at):
        p, v = lax.axis_index("pair"), lax.axis_index("virt")
        x, core, z, y = v // 2, v % 2, p // 2, p % 2
        width = chunk.shape[-1]
        chunk = chunk.reshape(nx, 2, nz, 2, -1, width)
        kept = lax.dynamic_index_in_dim(chunk, core, 1, keepdims=False)
        other = lax.dynamic_index_in_dim(chunk, 1 - core, 1, keepdims=False)
        chip = kept + send(other, swap_core)

        def pick(array, x_at, y_at):
            array = lax.dynamic_index_in_dim(array, x_at, 0, keepdims=False)
            return lax.dynamic_index_in_dim(array, y_at, 1, keepdims=False)

        plane = pick(chip, x, y)
        arrived = []
        for dx in range(nx):
            for dy in range(2):
                if dx or dy:
                    block = pick(chip, (x + dx) % nx, (y + dy) % 2)
                    block = coded(block, block[..., at : at + 1], at)
                    pairs = permutation(lambda p, v: (p ^ dy, (v + 2 * dx) % nv))
                    arrived.append(send(block, pairs))
        for block in arrived:
            plane = plane + decoded(block, at)
        total = lax.dynamic_index_in_dim(plane, z, 0, keepdims=False)
        arrived = []
        for dz in range(1, nz):
            block = lax.dynamic_index_in_dim(plane, (z + dz) % nz, 0, keepdims=False)
            block = coded(block, block[..., at : at + 1], at)
            pairs = permutation(lambda p, v: ((p + 2 * dz) % np_, v))
            arrived.append(send(block, pairs))
        for block in arrived:
            total = total + decoded(block, at)
        return total

    def shards(amplitudes, integrals):
        virtuals = amplitudes.shape[2]
        rows, cols = virtuals // np_, virtuals // nv
        width = -(-(cols + 2) // 128) * 128
        p, v = lax.axis_index("pair"), lax.axis_index("virt")
        (p00, p01), (p10, p11) = products(amplitudes, integrals)
        s01 = p01 + p10.T
        s00, s11 = p00 + p00.T, p11 + p11.T
        a, b = (lax.broadcasted_iota(jnp.int32, (virtuals, virtuals), d) for d in range(2))
        both = jnp.where(a <= b, s00, s11)
        crossed = reduced(with_extras(s01, jnp.zeros((virtuals,)), nv, width), cols + 1)
        same = reduced(with_extras(both, jnp.diagonal(s11), nv, width), cols + 1)

        mine = jnp.stack([crossed[:, :cols], same[:, :cols]])
        tiles = mine.reshape(2, rows, ratio, rows)
        mirrored = jnp.zeros((ratio, 2, rows, rows), jnp.float32)
        for t in range(ratio):
            h = (p % ratio + t) % ratio
            tile = lax.dynamic_index_in_dim(tiles, h, 2, keepdims=False).transpose(0, 2, 1)
            pairs = permutation(lambda p, v: (ratio * v + (p % ratio + t) % ratio, p // ratio))
            from_h = (p - t) % ratio
            mirrored = lax.dynamic_update_index_in_dim(mirrored, send(tile, pairs), from_h, 0)
        mirrored = mirrored.transpose(1, 2, 0, 3).reshape(2, rows, cols)
        a = p * rows + lax.broadcasted_iota(jnp.int32, (rows, cols), 0)
        b = v * cols + lax.broadcasted_iota(jnp.int32, (rows, cols), 1)
        out00 = jnp.where(a <= b, mine[1], mirrored[1])
        out11 = jnp.where(a > b, mine[1], mirrored[1])
        out11 = jnp.where(a == b, same[:, cols : cols + 1], out11)
        return jnp.stack([jnp.stack([out00, mine[0]], 1), jnp.stack([mirrored[0], out11], 1)])

    placed = (P(None, "pair", None, "virt"), P("pair", "virt", None, None))
    return jax.shard_map(
        shards, mesh=mesh, in_specs=placed, out_specs=P(None, "pair", None, "virt"), check_vma=False
    )
```

time: 2420 us -> 231 us (0.10)
  waiting for transfers between devices: 1610 us -> 32 us
  blocking collectives: 672 us -> 0 us
  other arithmetic: 3.16 us -> 29.6 us
  starting transfers between devices: 0.04 us -> 24.3 us
    all_gather x1 -> x0, waiting for transfers between devices: 1580 us -> none  [shards(): lax.all_gather(integrals, 'pair', axis=0, tiled=True)]
    all_to_all x2 -> x0, blocking collectives: 672 us -> none  [the longest x1 621 us: shards(): lax.all_to_all(amplitudes, 'pair', split_axis=2, concat_axis=1, tiled=True)]
    unnamed x5 -> x15, local copies, waits for them, and re-layouts: 43.3 us -> 4.08 us
    ppermute x0 -> x16, waiting for transfers between devices: none -> 32 us  [send(): return lax.ppermute(block, AXES, pairs)]
    unnamed x3 -> x0, waiting for transfers between devices: 28.3 us -> none
    slice x0 -> x3, local copies, waits for them, and re-layouts: none -> 26.6 us  [the longest x1 26.6 us: products(): integrals[:, :, j]]
    ppermute x0 -> x16, starting transfers between devices: none -> 24.3 us  [send(): return lax.ppermute(block, AXES, pairs)]
    dot_general x1 -> x4, matrix products: 44.3 us -> 56.2 us  [products(): jnp.einsum('kac,kcb->ab', amplitudes[i], integrals[:, :, j], preferred_el...]
  transfers between devices with their start and end apart: 2 -> 16, of which waited for: 2 -> 11; matrix products, arithmetic and copies ran while one was open for 2% -> 40% of each run, Pallas kernels for 0% -> 0%
where the time goes in v1:
time: 231 us; the launch traced here: 230 us
  local copies, waits for them, and re-layouts  85.2 us (37%)
  matrix products  56.2 us (24%)
  waiting for transfers between devices  32 us (14%)
  other arithmetic  29.6 us (13%)
  starting transfers between devices  24.3 us (11%)
  between operations  2.34 us (1%)
    dot_general x4, matrix products, products(): jnp.einsum('kac,kcb->ab', amplitudes[i], integrals[:, :, j], preferred_el...  56.2 us
    ppermute x16, waiting for transfers between devices, send(): return lax.ppermute(block, AXES, pairs)  32 us
    slice x1, local copies, waits for them, and re-layouts, products(): integrals[:, :, j]  26.6 us
    ppermute x16, starting transfers between devices, send(): return lax.ppermute(block, AXES, pairs)  24.3 us
    reshape x3, local copies, waits for them, and re-layouts, with_extras(): parts = block.reshape(rows, nv, cols // nv).transpose(1, 0, 2)  16.5 us
    gather x1, local copies, waits for them, and re-layouts, shards(): same = reduced(with_extras(both, jnp.diagonal(s11), nv, width), cols + 1)  15.4 us
    reduce_max x2, other arithmetic, with_extras(): largest = jnp.maximum(jnp.max(jnp.abs(block)), jnp.max(jnp.abs(diagonal)))  12.2 us
    dot_general x2, local copies, waits for them, and re-layouts, products(): jnp.einsum('kac,kcb->ab', amplitudes[i], integrals[:, :, j], preferred_el...  10.4 us
  transfers between devices with their start and end apart: 16, of which 11 were waited for; matrix products, arithmetic and copies ran while one was open for 40% of the time, Pallas kernels for 0%

profile of v1, /device:TPU:2, one launch (start us, length us, event | category | flops | bytes accessed | tf_op | source)
XLA Modules:
  0.0 229.7 jit_solution(10880070062948243156)
XLA Ops:
  0.0 26.6 %fusion.123 = (bf16[14,240,1,960]{3,2,1,0:T(2,128)(2,1)}, bf16[14,240,1,960]{3,2,1,0:T(2,128)(2,1)S(1)}) fusion(bf16[14,240,2,960]{3,2,1,0:T(2,128)(2,1)} %param.3), kind=kLoop, calls=%fused_computation.232 | loop fusion | bytes 25804800 | tf_op jit(solution)/shard_map/slice | solution.py:13
  26.6 12.2 %fusion = f32[960,960,1]{0,1,2:T(8,128)S(1)} fusion(bf16[2,14,960,240]{3,2,1,0:T(8,128)(2,1)} %param.2, bf16[14,240,1,960]{3,2,1,0:T(2,128)(2,1)S(1)} %get-tuple-element.21), kind=kOutput, calls=%fused_computation.3 | convolution fusion | flops 6193152000 | bytes 17018880 | tf_op jit(solution)/shard_map/kac,kcb->ab/dot_general | solution.py:13
  38.9 15.7 %abs_reduce_fusion = (f32[]{:T(128)}, f32[960,960]{0,1:T(8,128)}) fusion(f32[960,960,1]{0,1,2:T(8,128)S(1)} %fusion, bf16[14,240,1,960]{3,2,1,0:T(2,128)(2,1)} %get-tuple-element.20, bf16[2,14,960,240]{3,2,1,0:T(8,128)(2,1)} %param.2), kind=kOutput, calls=%fused_computation.22 | convolution fusion | flops 6195916800 | bytes 28016644 | tf_op jit(solution)/shard_map/kac,kcb->ab/dot_general | solution.py:13
  54.5 5.2 %copy.54 = f32[960,4,240]{2,0,1:T(8,128)} copy(f32[960,4,240]{0,2,1:T(8,128)} %bitcast.219) | data formatting | bytes 7372800 | tf_op jit(solution)/shard_map/reshape | solution.py:23
  66.3 16.1 %fusion.15 = f32[960,960]{1,0:T(8,128)} fusion(bf16[14,240,1,960]{3,2,1,0:T(2,128)(2,1)} %copy-done.2, bf16[2,14,960,240]{3,2,1,0:T(8,128)(2,1)} %param.2), kind=kOutput, calls=%fused_computation.25 | convolution fusion | flops 6193152000 | bytes 24330240 | tf_op jit(solution)/shard_map/kac,kcb->ab/dot_general | solution.py:13
  82.4 12.2 %fusion.18 = f32[960,960]{1,0:T(8,128)} fusion(bf16[14,240,1,960]{3,2,1,0:T(2,128)(2,1)S(1)} %bitcast.218, bf16[2,14,960,240]{3,2,1,0:T(8,128)(2,1)} %param.2), kind=kOutput, calls=%fused_computation.26 | convolution fusion | flops 6193152000 | bytes 17018880 | tf_op jit(solution)/shard_map/kac,kcb->ab/dot_general | solution.py:13
  94.7 5.2 %copy.41 = f32[960,960]{0,1:T(8,128)} copy(f32[960,960]{1,0:T(8,128)} %fusion.15) | data formatting | bytes 7372800 | tf_op jit(solution)/shard_map/kac,kcb->ab/dot_general | solution.py:13
  99.9 5.2 %copy.43 = f32[960,960]{0,1:T(8,128)} copy(f32[960,960]{1,0:T(8,128)} %fusion.18) | data formatting | bytes 7372800 | tf_op jit(solution)/shard_map/kac,kcb->ab/dot_general | solution.py:13
  105.1 11.6 %abs_reduce_fusion.1 = (f32[]{:T(128)}, f32[960,960]{1,0:T(8,128)}, f32[960,960]{1,0:T(8,128)}) fusion(f32[960,960]{1,0:T(8,128)} %fusion.15, f32[960,960]{0,1:T(8,128)} %copy.41, f32[960,960]{1,0:T(8,128)} %fusion.18, f32[960,960]{0,1:T(8,128)} %copy.43), kind=kLoop, calls=%fused_computation.23 | loop fusion | flops 5529599 | bytes 22118404 | tf_op jit(solution)/shard_map/reduce_max | solution.py:22
  116.7 15.4 %gather_fusion = f32[960]{0:T(1024)S(1)} fusion(f32[960,960]{1,0:T(8,128)} %get-tuple-element.13, s32[960]{0:T(1024)S(1)} %bitcast.210), kind=kCustom, calls=%fused_computation | custom fusion | bytes 15360 | tf_op jit(solution)/shard_map/jit(diagonal)/cond/branch_0_fun/gather | solution.py:105
  132.9 6.5 %reshape.39 = f32[960,4,240]{2,1,0:T(4,128)} reshape(f32[960,960]{1,0:T(8,128)} %get-tuple-element.12) | data formatting | bytes 7372800 | tf_op jit(solution)/shard_map/reshape | solution.py:23
  139.4 4.8 %copy.85 = f32[960,4,240]{2,0,1:T(8,128)} copy(f32[960,4,240]{2,1,0:T(4,128)} %reshape.39) | data formatting | bytes 7372800 | tf_op jit(solution)/shard_map/reshape | solution.py:23
  145.6 2.8 %pad_maximum_fusion = f32[4,960,256]{2,1,0:T(8,128)S(1)} fusion(f32[4,960,16]{2,1,0:T(8,128)S(1)} %broadcast_in_dim.204, f32[4,960,240]{2,1,0:T(8,128)} %bitcast.216), kind=kLoop, calls=%fused_computation.15 | loop fusion | flops 983040 | bytes 7864320 | tf_op jit(solution)/shard_map/concatenate | solution.py:26
  172.3 3.6 %collective-permute-done.2 = f16[4,120,256]{1,0,2:T(4,128)(2,1)S(1)} collective-permute-done((f16[4,120,256]{1,0,2:T(4,128)(2,1)}, f16[4,120,256]{1,0,2:T(4,128)(2,1)S(1)}, u32[]{:S(2)}, u32[]{:S(2)}) %collective-permute-start.2) | collective-permute-done | bytes 245792 | tf_op jit(solution)/shard_map/ppermute | solution.py:57
  176.0 5.7 %collective-permute-done.3 = f16[4,120,256]{1,0,2:T(4,128)(2,1)} collective-permute-done((f16[4,120,256]{1,0,2:T(4,128)(2,1)}, f16[4,120,256]{1,0,2:T(4,128)(2,1)}, u32[]{:S(2)}, u32[]{:S(2)}) %collective-permute-start.3) | collective-permute-done | bytes 245792 | tf_op jit(solution)/shard_map/ppermute | solution.py:57
  187.8 4.1 %collective-permute-done.8 = f16[4,120,256]{1,0,2:T(4,128)(2,1)S(1)} collective-permute-done((f16[4,120,256]{1,0,2:T(4,128)(2,1)S(1)}, f16[4,120,256]{1,0,2:T(4,128)(2,1)S(1)}, u32[]{:S(2)}, u32[]{:S(2)}) %collective-permute-start.8) | collective-permute-done | bytes 245792 | tf_op jit(solution)/shard_map/ppermute | solution.py:57
  191.9 2.7 %collective-permute-done.9 = f16[4,120,256]{1,0,2:T(4,128)(2,1)S(1)} collective-permute-done((f16[4,120,256]{1,0,2:T(4,128)(2,1)S(1)}, f16[4,120,256]{1,0,2:T(4,128)(2,1)S(1)}, u32[]{:S(2)}, u32[]{:S(2)}) %collective-permute-start.9) | collective-permute-done | bytes 245792 | tf_op jit(solution)/shard_map/ppermute | solution.py:57
  198.8 2.6 %collective-permute-start.5 = (f16[120,256]{0,1:T(8,128)(2,1)S(1)}, f16[120,256]{0,1:T(8,128)(2,1)S(1)}, u32[]{:S(2)}, u32[]{:S(2)}) collective-permute-start(f16[120,256]{0,1:T(8,128)(2,1)S(1)} %get-tuple-element.84), channel_id=1, source_target_pairs={{0,16},{1,17},{2,18},{3,19},{4,20},{5,21},{6,22},{7,23},{8,24},{9,... | collective-permute-start | bytes 184328 | tf_op jit(solution)/shard_map/ppermute | solution.py:57
  207.1 2.8 %collective-permute-start.13 = (f16[120,256]{0,1:T(8,128)(2,1)S(1)}, f16[120,256]{0,1:T(8,128)(2,1)S(1)}, u32[]{:S(2)}, u32[]{:S(2)}) collective-permute-start(f16[120,256]{0,1:T(8,128)(2,1)S(1)} %get-tuple-element.81), channel_id=1, source_target_pairs={{0,24},{1,25},{2,26},{3,27},{4,28},{5,29},{6,30},{7,31},{8,0},{9,1... | collective-permute-start | bytes 184328 | tf_op jit(solution)/shard_map/ppermute | solution.py:57
  210.0 2.6 %collective-permute-done.12 = f16[120,256]{0,1:T(8,128)(2,1)S(1)} collective-permute-done((f16[120,256]{0,1:T(8,128)(2,1)S(1)}, f16[120,256]{0,1:T(8,128)(2,1)S(1)}, u32[]{:S(2)}, u32[]{:S(2)}) %collective-permute-start.12) | collective-permute-done | bytes 61472 | tf_op jit(solution)/shard_map/ppermute | solution.py:57
  212.9 2.9 %collective-permute-start.14 = (f32[2,120,120]{1,2,0:T(8,128)S(1)}, f32[2,120,120]{1,2,0:T(8,128)S(1)}, u32[]{:S(2)}, u32[]{:S(2)}) collective-permute-start(f32[2,120,120]{1,2,0:T(8,128)S(1)} %bitcast.242), channel_id=1, source_target_pairs={{0,0},{1,8},{2,16},{3,24},{4,4},{5,12},{6,20},{7,28},{8,1},{9,9},{... | collective-permute-start | bytes 345608 | tf_op jit(solution)/shard_map/ppermute | solution.py:57
  215.9 3.8 %collective-permute-start.15 = (f32[2,120,120]{1,2,0:T(8,128)S(1)}, f32[2,120,120]{1,2,0:T(8,128)S(1)}, u32[]{:S(2)}, u32[]{:S(2)}) collective-permute-start(f32[2,120,120]{1,2,0:T(8,128)S(1)} %bitcast.241), channel_id=1, source_target_pairs={{0,4},{1,12},{2,20},{3,28},{4,0},{5,8},{6,16},{7,24},{8,5},{9,13},... | collective-permute-start | bytes 345608 | tf_op jit(solution)/shard_map/ppermute | solution.py:57
  219.7 4.2 %collective-permute-done.14 = f32[2,120,120]{1,2,0:T(8,128)S(1)} collective-permute-done((f32[2,120,120]{1,2,0:T(8,128)S(1)}, f32[2,120,120]{1,2,0:T(8,128)S(1)}, u32[]{:S(2)}, u32[]{:S(2)}) %collective-permute-start.14) | collective-permute-done | bytes 115232 | tf_op jit(solution)/shard_map/ppermute | solution.py:57
  224.0 4.5 %collective-permute-done.15 = f32[2,120,120]{1,2,0:T(8,128)S(1)} collective-permute-done((f32[2,120,120]{1,2,0:T(8,128)S(1)}, f32[2,120,120]{1,2,0:T(8,128)S(1)}, u32[]{:S(2)}, u32[]{:S(2)}) %collective-permute-start.15) | collective-permute-done | bytes 115232 | tf_op jit(solution)/shard_map/ppermute | solution.py:57
  (104 shorter events, 48.3 us)
Async XLA Ops:
  26.6 12.2 %copy-start.2 = (bf16[14,240,1,960]{3,2,1,0:T(2,128)(2,1)}, bf16[14,240,1,960]{3,2,1,0:T(2,128)(2,1)S(1)}, u32[]{:S(2)}) copy-start(bf16[14,240,1,960]{3,2,1,0:T(2,128)(2,1)S(1)} %get-tuple-element.21) | copy-start | bytes 19353604
  62.9 2.0 copy-start
  64.9 17.5 %slice-start = ((s8[13762560]{0:T(1024)(128)(4,1)}), s8[4194304]{0:T(1024)(128)(4,1)S(1)}, s32[]{:S(2)}) async-start(s8[13762560]{0:T(1024)(128)(4,1)} %bitcast.217), calls=%async_computation | async-start | bytes 8388608
  66.3 16.1 %slice-start.1 = ((s8[13762560]{0:T(1024)(128)(4,1)}), s8[4194304]{0:T(1024)(128)(4,1)S(1)}, s32[]{:S(2)}) async-start(s8[13762560]{0:T(1024)(128)(4,1)} %bitcast.217), calls=%async_computation.1 | async-start | bytes 8388608
  66.3 16.1 %slice-start.2 = ((s8[13762560]{0:T(1024)(128)(4,1)}), s8[4194304]{0:T(1024)(128)(4,1)S(1)}, s32[]{:S(2)}) async-start(s8[13762560]{0:T(1024)(128)(4,1)} %bitcast.217), calls=%async_computation.2 | async-start | bytes 8388608
  66.3 16.1 %slice-start.3 = ((s8[13762560]{0:T(1024)(128)(4,1)}), s8[1179648]{0:T(1024)(128)(4,1)S(1)}, s32[]{:S(2)}) async-start(s8[13762560]{0:T(1024)(128)(4,1)} %bitcast.217), calls=%async_computation.3 | async-start | bytes 2359296
  66.3 86.1 %collective-permute-start.7 = (f32[2,4,2,120,256]{4,3,2,1,0:T(8,128)}, f32[2,4,2,120,256]{4,3,2,1,0:T(8,128)S(1)}, u32[]{:S(2)}, u32[]{:S(2)}) collective-permute-start(f32[2,4,2,120,256]{4,3,2,1,0:T(8,128)} %dynamic-slice_bitcast_fusion), channel_id=1, source_target_pairs={{0,1},{1,0},{2,3},{3,2},{4,5},{5,4},{6,7},{7,6},{8,9},{9,8},{10,11... | collective-permute-start | bytes 5898248 | tf_op jit(solution)/shard_map/ppermute | solution.py:57
  148.4 1.9 copy-start.1
  151.7 4.6 %collective-permute-start = (f32[2,4,2,120,256]{4,3,2,1,0:T(8,128)}, f32[2,4,2,120,256]{4,3,2,1,0:T(8,128)}, u32[]{:S(2)}, u32[]{:S(2)}) collective-permute-start(f32[2,4,2,120,256]{4,3,2,1,0:T(8,128)} %dynamic-slice_bitcast_fusion.1), channel_id=1, source_target_pairs={{0,1},{1,0},{2,3},{3,2},{4,5},{5,4},{6,7},{7,6},{8,9},{9,8},{10,11... | collective-permute-start | bytes 5898248 | tf_op jit(solution)/shard_map/ppermute | solution.py:57
  163.5 8.8 %collective-permute-start.1 = (f16[4,120,256]{1,0,2:T(4,128)(2,1)}, f16[4,120,256]{1,0,2:T(4,128)(2,1)S(1)}, u32[]{:S(2)}, u32[]{:S(2)}) collective-permute-start(f16[4,120,256]{1,0,2:T(4,128)(2,1)} %get-tuple-element.90), channel_id=1, source_target_pairs={{0,4},{1,5},{2,6},{3,7},{4,0},{5,1},{6,2},{7,3},{8,12},{9,13},{10,... | collective-permute-start | bytes 737288 | tf_op jit(solution)/shard_map/ppermute | solution.py:57
  166.5 9.4 %collective-permute-start.2 = (f16[4,120,256]{1,0,2:T(4,128)(2,1)}, f16[4,120,256]{1,0,2:T(4,128)(2,1)S(1)}, u32[]{:S(2)}, u32[]{:S(2)}) collective-permute-start(f16[4,120,256]{1,0,2:T(4,128)(2,1)} %get-tuple-element.91), channel_id=1, source_target_pairs={{0,2},{1,3},{2,0},{3,1},{4,6},{5,7},{6,4},{7,5},{8,10},{9,11},{10,... | collective-permute-start | bytes 737288 | tf_op jit(solution)/shard_map/ppermute | solution.py:57
  167.1 14.5 %collective-permute-start.3 = (f16[4,120,256]{1,0,2:T(4,128)(2,1)}, f16[4,120,256]{1,0,2:T(4,128)(2,1)}, u32[]{:S(2)}, u32[]{:S(2)}) collective-permute-start(f16[4,120,256]{1,0,2:T(4,128)(2,1)} %get-tuple-element.92), channel_id=1, source_target_pairs={{0,6},{1,7},{2,4},{3,5},{4,2},{5,3},{6,0},{7,1},{8,14},{9,15},{10,... | collective-permute-start | bytes 737288 | tf_op jit(solution)/shard_map/ppermute | solution.py:57
  169.9 16.6 %collective-permute-start.10 = (f16[4,120,256]{1,0,2:T(4,128)(2,1)}, f16[4,120,256]{1,0,2:T(4,128)(2,1)}, u32[]{:S(2)}, u32[]{:S(2)}) collective-permute-start(f16[4,120,256]{1,0,2:T(4,128)(2,1)} %get-tuple-element.93), channel_id=1, source_target_pairs={{0,6},{1,7},{2,4},{3,5},{4,2},{5,3},{6,0},{7,1},{8,14},{9,15},{10,... | collective-permute-start | bytes 737288 | tf_op jit(solution)/shard_map/ppermute | solution.py:57
  184.4 7.5 %collective-permute-start.8 = (f16[4,120,256]{1,0,2:T(4,128)(2,1)S(1)}, f16[4,120,256]{1,0,2:T(4,128)(2,1)S(1)}, u32[]{:S(2)}, u32[]{:S(2)}) collective-permute-start(f16[4,120,256]{1,0,2:T(4,128)(2,1)S(1)} %get-tuple-element.89), channel_id=1, source_target_pairs={{0,4},{1,5},{2,6},{3,7},{4,0},{5,1},{6,2},{7,3},{8,12},{9,13},{10,... | collective-permute-start | bytes 737288 | tf_op jit(solution)/shard_map/ppermute | solution.py:57
  187.2 7.4 %collective-permute-start.9 = (f16[4,120,256]{1,0,2:T(4,128)(2,1)S(1)}, f16[4,120,256]{1,0,2:T(4,128)(2,1)S(1)}, u32[]{:S(2)}, u32[]{:S(2)}) collective-permute-start(f16[4,120,256]{1,0,2:T(4,128)(2,1)S(1)} %get-tuple-element.88), channel_id=1, source_target_pairs={{0,2},{1,3},{2,0},{3,1},{4,6},{5,7},{6,4},{7,5},{8,10},{9,11},{10,... | collective-permute-start | bytes 737288 | tf_op jit(solution)/shard_map/ppermute | solution.py:57
  197.1 6.3 %collective-permute-start.4 = (f16[120,256]{0,1:T(8,128)(2,1)S(1)}, f16[120,256]{0,1:T(8,128)(2,1)S(1)}, u32[]{:S(2)}, u32[]{:S(2)}) collective-permute-start(f16[120,256]{0,1:T(8,128)(2,1)S(1)} %get-tuple-element.83), channel_id=1, source_target_pairs={{0,8},{1,9},{2,10},{3,11},{4,12},{5,13},{6,14},{7,15},{8,16},{9,17... | collective-permute-start | bytes 184328 | tf_op jit(solution)/shard_map/ppermute | solution.py:57
  198.8 5.3 %collective-permute-start.5 = (f16[120,256]{0,1:T(8,128)(2,1)S(1)}, f16[120,256]{0,1:T(8,128)(2,1)S(1)}, u32[]{:S(2)}, u32[]{:S(2)}) collective-permute-start(f16[120,256]{0,1:T(8,128)(2,1)S(1)} %get-tuple-element.84), channel_id=1, source_target_pairs={{0,16},{1,17},{2,18},{3,19},{4,20},{5,21},{6,22},{7,23},{8,24},{9,... | collective-permute-start | bytes 184328 | tf_op jit(solution)/shard_map/ppermute | solution.py:57
  201.3 5.1 %collective-permute-start.6 = (f16[120,256]{0,1:T(8,128)(2,1)S(1)}, f16[120,256]{0,1:T(8,128)(2,1)S(1)}, u32[]{:S(2)}, u32[]{:S(2)}) collective-permute-start(f16[120,256]{0,1:T(8,128)(2,1)S(1)} %get-tuple-element.85), channel_id=1, source_target_pairs={{0,24},{1,25},{2,26},{3,27},{4,28},{5,29},{6,30},{7,31},{8,0},{9,1... | collective-permute-start | bytes 184328 | tf_op jit(solution)/shard_map/ppermute | solution.py:57
  202.7 7.2 %collective-permute-start.11 = (f16[120,256]{0,1:T(8,128)(2,1)S(1)}, f16[120,256]{0,1:T(8,128)(2,1)S(1)}, u32[]{:S(2)}, u32[]{:S(2)}) collective-permute-start(f16[120,256]{0,1:T(8,128)(2,1)S(1)} %get-tuple-element.86), channel_id=1, source_target_pairs={{0,8},{1,9},{2,10},{3,11},{4,12},{5,13},{6,14},{7,15},{8,16},{9,17... | collective-permute-start | bytes 184328 | tf_op jit(solution)/shard_map/ppermute | solution.py:57
  206.6 6.0 %collective-permute-start.12 = (f16[120,256]{0,1:T(8,128)(2,1)S(1)}, f16[120,256]{0,1:T(8,128)(2,1)S(1)}, u32[]{:S(2)}, u32[]{:S(2)}) collective-permute-start(f16[120,256]{0,1:T(8,128)(2,1)S(1)} %get-tuple-element.82), channel_id=1, source_target_pairs={{0,16},{1,17},{2,18},{3,19},{4,20},{5,21},{6,22},{7,23},{8,24},{9,... | collective-permute-start | bytes 184328 | tf_op jit(solution)/shard_map/ppermute | solution.py:57
  207.1 5.5 %collective-permute-start.13 = (f16[120,256]{0,1:T(8,128)(2,1)S(1)}, f16[120,256]{0,1:T(8,128)(2,1)S(1)}, u32[]{:S(2)}, u32[]{:S(2)}) collective-permute-start(f16[120,256]{0,1:T(8,128)(2,1)S(1)} %get-tuple-element.81), channel_id=1, source_target_pairs={{0,24},{1,25},{2,26},{3,27},{4,28},{5,29},{6,30},{7,31},{8,0},{9,1... | collective-permute-start | bytes 184328 | tf_op jit(solution)/shard_map/ppermute | solution.py:57
  212.9 11.1 %collective-permute-start.14 = (f32[2,120,120]{1,2,0:T(8,128)S(1)}, f32[2,120,120]{1,2,0:T(8,128)S(1)}, u32[]{:S(2)}, u32[]{:S(2)}) collective-permute-start(f32[2,120,120]{1,2,0:T(8,128)S(1)} %bitcast.242), channel_id=1, source_target_pairs={{0,0},{1,8},{2,16},{3,24},{4,4},{5,12},{6,20},{7,28},{8,1},{9,9},{... | collective-permute-start | bytes 345608 | tf_op jit(solution)/shard_map/ppermute | solution.py:57
  215.9 12.6 %collective-permute-start.15 = (f32[2,120,120]{1,2,0:T(8,128)S(1)}, f32[2,120,120]{1,2,0:T(8,128)S(1)}, u32[]{:S(2)}, u32[]{:S(2)}) collective-permute-start(f32[2,120,120]{1,2,0:T(8,128)S(1)} %bitcast.241), channel_id=1, source_target_pairs={{0,4},{1,12},{2,20},{3,28},{4,0},{5,8},{6,16},{7,24},{8,5},{9,13},... | collective-permute-start | bytes 345608 | tf_op jit(solution)/shard_map/ppermute | solution.py:57

commit v2 on v0

v2 whole, which is shorter than its diff:
```python
import jax
import jax.numpy as jnp
from jax import lax
from jax.experimental import pallas as pl
from jax.experimental.pallas import tpu as pltpu
from jax.sharding import PartitionSpec as P

AXES = ("pair", "virt")
F32, BF16 = jnp.float32, jnp.bfloat16
TOP = 1024.0
LANES = 128
ANY = pl.BlockSpec(memory_space=pl.ANY)
VMEM = pl.BlockSpec(memory_space=pltpu.VMEM)
SMEM = pl.BlockSpec(memory_space=pltpu.SMEM)


def dot(left, right):
    return jnp.dot(left, right, preferred_element_type=F32)


def iota(shape, axis):
    return lax.broadcasted_iota(jnp.int32, shape, axis)


def bound_at(block, at):
    return block[0:1, at : at + 1].astype(F32)


def with_bound(block, bound, at):
    here = (iota(block.shape, 0) == 0) & (iota(block.shape, 1) == at)
    return jnp.where(here, bound, block)


def sent_bound(bound):
    return jnp.maximum(bound * 1.01, 1e-35).astype(BF16).astype(F32)


def coded(values, bound):
    scaled = jnp.abs(values) * (TOP / bound)
    fourth = scaled * scaled
    fourth = fourth * fourth
    power = fourth * fourth * fourth
    return jnp.where(values < 0, -power, power)


def decoded(block, bound):
    power = block.astype(F32)
    magnitude = jnp.exp2(jnp.log2(jnp.maximum(jnp.abs(power), 1e-37)) * (1 / 12)) * (bound * (1 / TOP))
    return jnp.where(power == 0, 0.0, jnp.where(power < 0, -magnitude, magnitude))


def local(body, out_types, aligned, name, vmem=40):
    def kernel(index, *refs):
        results = body(index, *refs[: -len(out_types)])
        for ref, result in zip(refs[-len(out_types) :], results):
            if isinstance(result, list):
                for n, block in enumerate(result):
                    ref[n] = block.astype(ref.dtype)
            else:
                ref[...] = result.astype(ref.dtype)

    def call(index, *arrays):
        if not aligned:
            results = body(index, *arrays)
            results = [jnp.stack(result) if isinstance(result, list) else result for result in results]
            return [result.astype(kind.dtype) for result, kind in zip(results, out_types)]
        return pl.pallas_call(
            kernel,
            in_specs=[SMEM] + [VMEM] * len(arrays),
            out_specs=[VMEM] * len(out_types),
            out_shape=out_types,
            name=name,
            compiler_params=pltpu.CompilerParams(vmem_limit_bytes=vmem * 2**20),
        )(index, *arrays)

    return call


def product_kernel(same, depth, inner, virtuals, cols, nv):
    lane_tiles = -(-virtuals // LANES)
    half = depth // 2

    def lanes(tile):
        return min(LANES, virtuals - LANES * tile)

    def kernel(index, u_hbm, w_hbm, w_last, kept, sent, *scratch):
        bufs = list(scratch[: lane_tiles - 1]) + [w_last.reshape(depth * inner * 2, LANES)]
        us, first, second, out, sems, out_sems = (
            scratch[lane_tiles - 1 : lane_tiles + 1],
            *scratch[lane_tiles + 1 :],
        )
        w_rows = w_hbm.reshape(depth * inner * 2, virtuals)

        def u_copy(i, h):
            part = pl.ds(h * half, half)
            return pltpu.make_async_copy(u_hbm.at[i, part], us[i].at[part], sems.at[0, i, h])

        def w_copy(tile, h):
            part = pl.ds(h * half * inner * 2, half * inner * 2)
            return pltpu.make_async_copy(
                w_rows.at[part, pl.ds(LANES * tile, LANES)], bufs[tile].at[part], sems.at[1, tile, h]
            )

        order = ((0, 0), (1, 1)) if same else ((0, 1), (1, 0))
        lead = order[0][0]
        groups = [[("u", lead, h), ("w", 0, h), ("w", 1, h)] for h in range(2)]
        groups += [[("w", t, h) for t in (2 * n, 2 * n + 1) if t < lane_tiles - 1 for h in range(2)] for n in range(1, lane_tiles // 2)]
        groups += [[("u", 1 - lead, h)] for h in range(2)]
        copies = {key: (u_copy if key[0] == "u" else w_copy)(*key[1:]) for group in groups for key in group}
        state = {"started": 0, "waited": 0}

        def start_until(count):
            while state["started"] < min(count, len(groups)):
                for key in groups[state["started"]]:
                    copies[key].start()
                state["started"] += 1

        def need(group):
            while state["waited"] <= group:
                for key in groups[state["waited"]]:
                    copies[key].wait()
                state["waited"] += 1
                start_until(state["waited"] + 2)

        def weights(k, j, n):
            parts = [bufs[t][pl.ds(k * 2 * inner + j, inner, 2), :][:, : lanes(t)] for t in (2 * n, 2 * n + 1)]
            return jnp.concatenate(parts, axis=1)

        def product_tile(which, n):
            i, j = order[which]
            total = None
            for k in range(depth):
                if which == 0:
                    need(k // half if n == 0 else n + 1)
                elif n == 0:
                    need(len(groups) - 2 + k // half)
                term = dot(us[i][k], weights(k, j, n))
                total = term if total is None else total + term
            return total

        def place(v, rows, block):
            out[v, rows, :cols] = block
            return jnp.max(jnp.abs(block), axis=0, keepdims=True)

        start_until(2)
        largest = jnp.zeros((1, cols), F32)
        for n in range(lane_tiles // 2):
            tile = product_tile(0, n)
            first[:, 2 * LANES * n : 2 * LANES * n + tile.shape[1]] = tile

        def segment(v, tile, lower):
            big = jnp.zeros((1, cols), F32)
            begin, end = LANES * tile, LANES * tile + lanes(tile)
            on, past = v * cols, (v + 1) * cols
            flipped = {}

            def symmetric(source, r0, r1):
                if id(source) not in flipped:
                    flipped[id(source)] = source[on:past, begin:end].T
                return source[r0:r1, on:past] + flipped[id(source)][r0 - begin : r1 - begin]

            r0, r1 = begin, min(end, on)
            if not lower and r0 < r1:
                big = jnp.maximum(big, place(v, slice(r0, r1), symmetric(first, r0, r1)))
            r0, r1 = max(begin, on), min(end, past)
            if lower and r0 < r1:
                s00, s11 = symmetric(first, r0, r1), symmetric(second, r0, r1)
                a, b = r0 + iota(s00.shape, 0), on + iota(s00.shape, 1)
                big = jnp.maximum(big, place(v, slice(r0, r1), jnp.where(a <= b, s00, s11)))
                diagonal = jnp.sum(jnp.where(a == b, s11, 0.0), axis=1, keepdims=True)
                out[v, r0:r1, cols : cols + 1] = diagonal
                big = jnp.maximum(big, jnp.max(jnp.abs(diagonal)))
            r0, r1 = max(begin, past), end
            if lower and r0 < r1:
                big = jnp.maximum(big, place(v, slice(r0, r1), symmetric(second, r0, r1)))
            return big

        for n in range(lane_tiles // 2):
            tile = product_tile(1, n)
            second[:, 2 * LANES * n : 2 * LANES * n + tile.shape[1]] = tile
            for t in (2 * n, 2 * n + 1):
                rows = slice(LANES * t, LANES * t + lanes(t))
                for v in range(nv):
                    if same:
                        largest = jnp.maximum(largest, segment(v, t, False))
                    else:
                        block = first[rows, v * cols : (v + 1) * cols] + second[v * cols : (v + 1) * cols, rows].T
                        largest = jnp.maximum(largest, place(v, rows, block))
        if same:
            for t in range(lane_tiles):
                for v in range(nv):
                    largest = jnp.maximum(largest, segment(v, t, True))
        largest = jnp.max(largest)
        width = out.shape[-1] - cols
        for v in range(2):
            head = out[v, 0:8, cols:]
            here = (iota((8, width), 0) == 0) & (iota((8, width), 1) == 1)
            out[v, 0:8, cols:] = jnp.where(here, largest, head)
        for core in range(2):

            @pl.when(index[1] == core)
            def _():
                sends = []
                for x in range(nv // 2):
                    for slot, (target, v) in enumerate(((kept, 2 * x + core), (sent, 2 * x + 1 - core))):
                        sends.append(pltpu.make_async_copy(out.at[v], target.at[x], out_sems.at[x, slot]))
                for copy in sends:
                    copy.start()
                for copy in sends:
                    copy.wait()

    return kernel


def unique_sums(index, amplitudes, integrals, same, nv, width):
    _, depth, virtuals, inner = amplitudes.shape
    cols = virtuals // nv
    lane_tiles = -(-virtuals // LANES)
    half_type = jax.ShapeDtypeStruct((nv // 2, virtuals, width), F32)
    return pl.pallas_call(
        product_kernel(same, depth, inner, virtuals, cols, nv),
        grid=(1,),
        in_specs=[SMEM, ANY, ANY, pl.BlockSpec((depth, inner, 2, LANES), lambda _: (0, 0, 0, lane_tiles - 1))],
        out_specs=[ANY, ANY],
        out_shape=[half_type, half_type],
        scratch_shapes=[pltpu.VMEM((depth * inner * 2, LANES), BF16)] * (lane_tiles - 1)
        + [pltpu.VMEM((depth, virtuals, inner), BF16)] * 2
        + [pltpu.VMEM((virtuals, virtuals), F32)] * 2
        + [
            pltpu.VMEM((nv, virtuals, width), F32),
            pltpu.SemaphoreType.DMA((2, lane_tiles, 2)),
            pltpu.SemaphoreType.DMA((nv // 2, 2)),
        ],
        name="same" if same else "crossed",
        cost_estimate=pl.CostEstimate(
            flops=4 * depth * inner * virtuals * virtuals, bytes_accessed=4 * amplitudes.size, transcendentals=0
        ),
        compiler_params=pltpu.CompilerParams(vmem_limit_bytes=58 * 2**20),
    )(index, amplitudes, integrals, integrals)


def plain_sums(index, amplitudes, integrals, same, nv, width):
    virtuals = amplitudes.shape[2]
    cols = virtuals // nv

    def product(i, j):
        return jnp.einsum("kac,kcb->ab", amplitudes[i], integrals[:, :, j], preferred_element_type=F32)

    if same:
        s00, s11 = ((q + q.T) for q in (product(0, 0), product(1, 1)))
        a, b = (iota((virtuals, virtuals), axis) for axis in range(2))
        block, diagonal = jnp.where(a <= b, s00, s11), jnp.diagonal(s11)
    else:
        block, diagonal = product(0, 1) + product(1, 0).T, jnp.zeros((virtuals,), F32)
    largest = jnp.maximum(jnp.max(jnp.abs(block)), jnp.max(jnp.abs(diagonal)))
    parts = block.reshape(virtuals, nv, cols).transpose(1, 0, 2)
    extra = jnp.stack([diagonal, jnp.full((virtuals,), largest)], axis=1)
    extra = jnp.pad(extra, ((0, 0), (0, width - cols - 2)))
    parts = jnp.concatenate([parts, jnp.broadcast_to(extra, (nv, *extra.shape))], axis=2)
    parts = parts.reshape(nv // 2, 2, virtuals, width)
    return [lax.dynamic_index_in_dim(parts, c, 1, keepdims=False) for c in (index[1], 1 - index[1])]


def solution(mesh):
    np_, nv = mesh.shape["pair"], mesh.shape["virt"]
    nx, nz, ratio = nv // 2, np_ // 2, np_ // nv

    def send(block, move):
        pairs = []
        for p in range(np_):
            for v in range(nv):
                q, w = move(p, v)
                pairs.append((p * nv + v, q * nv + w))
        return lax.ppermute(block, AXES, pairs)

    def shards(amplitudes, integrals):
        _, _, virtuals, inner = amplitudes.shape
        rows, cols = virtuals // np_, virtuals // nv
        width = -(-(cols + 2) // LANES) * LANES
        at = cols + 1
        aligned = rows % 8 == 0 and inner % 16 == 0 and virtuals % 64 == 0
        p, v = lax.axis_index("pair"), lax.axis_index("virt")
        index = jnp.stack([v // 2, v % 2, p // 2, p % 2, p, v]).astype(jnp.int32)
        steps = [(dx, dy) for dx in range(nx) for dy in range(2) if dx or dy]

        def chip_sum(index, kept, came):
            x, y = index[0], index[3]
            bound = sent_bound(bound_at(kept[0, 0, 0], at) + bound_at(came[0, 0, 0], at))

            def block(x_at, y_at, z):
                return kept[x_at, z, y_at] + came[x_at, z, y_at]

            own = [block(x, y, z) for z in range(nz)]
            results = [[with_bound(own[0], bound, at)] + own[1:]]
            for dx, dy in steps:
                blocks = [coded(block((x + dx) % nx, (y + dy) % 2, z), bound) for z in range(nz)]
                results.append([with_bound(blocks[0], bound, at)] + blocks[1:])
            return results

        def plane_sum(index, own, *came):
            z_own = index[2]
            bounds = [bound_at(array[0], at) for array in came]
            bound = sent_bound(sum(bounds, bound_at(own[0], at)))

            def block(z):
                total = own[z]
                for array, of in zip(came, bounds):
                    total = total + decoded(array[z], of)
                return total

            results = [with_bound(block(z_own), bound, at)]
            for dz in range(1, nz):
                results.append(with_bound(coded(block((z_own + dz) % nz), bound), bound, at))
            return results

        def line_sum(index, own, *came):
            total = own[...]
            for array in came:
                array = array[...]
                total = total + decoded(array, bound_at(array, at))
            flipped = [total[:, h * rows : (h + 1) * rows].T for h in range(ratio)]
            results = [total]
            for t in range(ratio):
                tile = flipped[0]
                for h in range(1, ratio):
                    tile = jnp.where((index[4] + t) % ratio == h, flipped[h], tile)
                results.append(tile)
            return results

        def outcome(index, crossed, same, *came):
            def mirrored(tiles):
                parts = []
                for h in range(ratio):
                    part = tiles[0][...]
                    for t in range(1, ratio):
                        part = jnp.where((index[4] + ratio - h) % ratio == t, tiles[t][...], part)
                    parts.append(part)
                return jnp.concatenate(parts, axis=1) if ratio > 1 else parts[0]

            same = same[...]
            square = same[:, :cols]
            other = mirrored(came[ratio:])
            a = index[4] * rows + iota(square.shape, 0)
            b = index[5] * cols + iota(square.shape, 1)
            out00 = jnp.where(a <= b, square, other)
            out11 = jnp.where(a > b, square, jnp.where(a == b, same[:, cols : cols + 1], other))
            return [out00, crossed[...][:, :cols], mirrored(came[:ratio]), out11]

        def outcome_kernel(index, *refs):
            for n, block in enumerate(outcome(index, *refs[:-1])):
                refs[-1][n // 2, :, n % 2, :] = block

        def kind(shape, dtype=F32):
            return jax.ShapeDtypeStruct(shape, dtype)

        def reduced(same):
            sums = unique_sums if aligned else plain_sums
            kept, other = sums(index, amplitudes, integrals, same, nv, width)
            came = send(other, lambda p, v: (p, v ^ 1))
            shape = (nx, nz, 2, rows, width)
            types = [kind((nz, rows, width))] + [kind((nz, rows, width), BF16)] * len(steps)
            own, *outs = local(chip_sum, types, aligned, "chip_sum")(index, kept.reshape(shape), came.reshape(shape))
            came = [send(block, lambda p, v: (p ^ dy, (v + 2 * dx) % nv)) for (dx, dy), block in zip(steps, outs)]
            types = [kind((rows, width))] + [kind((rows, width), BF16)] * (nz - 1)
            own, *outs = local(plane_sum, types, aligned, "plane_sum")(index, own, *came)
            came = [send(block, lambda p, v: ((p + 2 * dz) % np_, v)) for dz, block in zip(range(1, nz), outs)]
            types = [kind((rows, width))] + [kind((rows, rows))] * ratio
            total, *tiles = local(line_sum, types, aligned, "line_sum")(index, own, *came)
            return total, [
                send(tile, lambda p, v: (ratio * v + (p % ratio + t) % ratio, p // ratio)) for t, tile in enumerate(tiles)
            ]

        crossed, crossed_tiles = reduced(False)
        same, same_tiles = reduced(True)
        arrays = [crossed, same, *crossed_tiles, *same_tiles]
        if not aligned:
            blocks = outcome(index, *arrays)
            return jnp.stack([jnp.stack(blocks[:2], 1), jnp.stack(blocks[2:], 1)])
        return pl.pallas_call(
            outcome_kernel,
            in_specs=[SMEM] + [VMEM] * len(arrays),
            out_specs=VMEM,
            out_shape=kind((2, rows, 2, cols)),
            name="outcome",
        )(index, *arrays)

    placed = (P(None, "pair", None, "virt"), P("pair", "virt", None, None))
    return jax.shard_map(
        shards, mesh=mesh, in_specs=placed, out_specs=P(None, "pair", None, "virt"), check_vma=False
    )
```

time: 2420 us -> 120 us (0.05)
  waiting for transfers between devices: 1610 us -> 13.1 us
  blocking collectives: 672 us -> 0 us
  Pallas kernels: 0 us -> 71.8 us
  local copies, waits for them, and re-layouts: 68.9 us -> 2.52 us
  matrix products: 44.3 us -> 0 us
  starting transfers between devices: 0.04 us -> 31.3 us
    all_gather x1 -> x0, waiting for transfers between devices: 1580 us -> none  [shards(): lax.all_gather(integrals, 'pair', axis=0, tiled=True)]
    all_to_all x2 -> x0, blocking collectives: 672 us -> none  [the longest x1 621 us: shards(): lax.all_to_all(amplitudes, 'pair', split_axis=2, concat_axis=1, tiled=True)]
    pallas_call x0 -> x9, Pallas kernels: none -> 71.8 us  [the longest x2 62.6 us: unique_sums(): pl.pallas_call(product_kernel(same, depth, inner, virtuals, cols, nv), gr...]
    dot_general x1 -> x0, matrix products: 44.3 us -> none  [shards(): jnp.einsum('ikac,kcjb->iajb', regrouped, lax.all_gather(integrals, 'pair'...]
    unnamed x5 -> x18, local copies, waits for them, and re-layouts: 43.3 us -> 1.91 us
    ppermute x0 -> x18, starting transfers between devices: none -> 31.3 us  [send(): return lax.ppermute(block, AXES, pairs)]
    unnamed x3 -> x0, waiting for transfers between devices: 28.3 us -> none
  transfers between devices with their start and end apart: 2 -> 18, of which waited for: 2 -> 5; matrix products, arithmetic and copies ran while one was open for 2% -> 0% of each run, Pallas kernels for 0% -> 32%
where the time goes in v2:
time: 120 us; the launch traced here: 119 us
  Pallas kernels  71.8 us (60%)
  starting transfers between devices  31.3 us (26%)
  waiting for transfers between devices  13.1 us (11%)
  local copies, waits for them, and re-layouts  2.52 us (2%)
    pallas_call x2, Pallas kernels, unique_sums(): pl.pallas_call(product_kernel(same, depth, inner, virtuals, cols, nv), gr...  62.6 us
    ppermute x18, starting transfers between devices, send(): return lax.ppermute(block, AXES, pairs)  31.3 us
    ppermute x18, waiting for transfers between devices, send(): return lax.ppermute(block, AXES, pairs)  13.1 us
    pallas_call x6, Pallas kernels, call(): pl.pallas_call(kernel, in_specs=[SMEM] + [VMEM] * len(arrays), out_specs=...  7.15 us
  transfers between devices with their start and end apart: 18, of which 5 were waited for; matrix products, arithmetic and copies ran while one was open for 0% of the time, Pallas kernels for 32%

profile of v2, /device:TPU:2, one launch (start us, length us, event | category | flops | bytes accessed | tf_op | source)
XLA Modules:
  0.0 118.8 jit_solution(15709908974443704415)
XLA Ops:
  0.6 31.4 %same.1 = (f32[2,960,256]{2,1,0:T(8,128)}, f32[2,960,256]{2,1,0:T(8,128)}) custom-call(s32[6]{0:T(128)} %stack.27.index, bf16[2,14,960,240]{3,2,1,0:T(8,128)(2,1)} %u_hbm.3, bf16[14,240,2,960]{3,2,1,0:T(2,128)(2,1)} %w_last.3, bf16[14,240,2,960]{3,2,1,0:T(2,128)(2,1)} %w_last.3), custom_call_target="tpu_custom_call" | custom-call | flops 12386304000 | bytes 25804800 | tf_op jit(solution)/shard_map/same/pallas_call | solution.py:220
  32.1 31.2 %crossed.1 = (f32[2,960,256]{2,1,0:T(8,128)}, f32[2,960,256]{2,1,0:T(8,128)}) custom-call(s32[6]{0:T(128)} %stack.27.index, bf16[2,14,960,240]{3,2,1,0:T(8,128)(2,1)} %u_hbm.3, bf16[14,240,2,960]{3,2,1,0:T(2,128)(2,1)} %w_last.3, bf16[14,240,2,960]{3,2,1,0:T(2,128)(2,1)} %w_last.3), custom_call_target="tpu_custom_call" | custom-call | flops 12386304000 | bytes 25804800 | tf_op jit(solution)/shard_map/crossed/pallas_call | solution.py:220
  65.1 1.6 %collective-permute-start.8 = (bf16[4,120,256]{2,1,0:T(8,128)(2,1)S(1)}, bf16[4,120,256]{2,1,0:T(8,128)(2,1)S(1)}, u32[]{:S(2)}, u32[]{:S(2)}) collective-permute-start(bf16[4,120,256]{2,1,0:T(8,128)(2,1)S(1)} %get-tuple-element.45), channel_id=1, source_target_pairs={{0,4},{1,5},{2,6},{3,7},{4,0},{5,1},{6,2},{7,3},{8,12},{9,13},{10,... | collective-permute-start | bytes 737288 | tf_op jit(solution)/shard_map/ppermute | solution.py:274
  67.2 1.4 %collective-permute-start.10 = (bf16[4,120,256]{2,1,0:T(8,128)(2,1)S(1)}, bf16[4,120,256]{2,1,0:T(8,128)(2,1)S(1)}, u32[]{:S(2)}, u32[]{:S(2)}) collective-permute-start(bf16[4,120,256]{2,1,0:T(8,128)(2,1)S(1)} %get-tuple-element.47), channel_id=1, source_target_pairs={{0,6},{1,7},{2,4},{3,5},{4,2},{5,3},{6,0},{7,1},{8,14},{9,15},{10,... | collective-permute-start | bytes 737288 | tf_op jit(solution)/shard_map/ppermute | solution.py:274
  68.6 1.3 %chip_sum.2 = (f32[4,120,256]{2,1,0:T(8,128)S(1)}, bf16[4,120,256]{2,1,0:T(8,128)(2,1)S(1)}, bf16[4,120,256]{2,1,0:T(8,128)(2,1)S(1)}, bf16[4,120,256]{2,1,0:T(8,128)(2,1)S(1)}) custom-call(s32[6]{0:T(128)S(1)} %copy-done.4, f32[2,4,2,120,256]{4,3,2,1,0:T(8,128)S(1)} %bitcast.10, f32[2,4,2,120,256]{4,3,2,1,0:T(8,128)S(1)} %bitcast.11), custom_call_target="tpu_custom_call" | custom-call | tf_op jit(solution)/shard_map/chip_sum/pallas_call | solution.py:67
  69.9 1.6 %collective-permute-start.1 = (bf16[4,120,256]{2,1,0:T(8,128)(2,1)S(1)}, bf16[4,120,256]{2,1,0:T(8,128)(2,1)S(1)}, u32[]{:S(2)}, u32[]{:S(2)}) collective-permute-start(bf16[4,120,256]{2,1,0:T(8,128)(2,1)S(1)} %get-tuple-element.34), channel_id=1, source_target_pairs={{0,4},{1,5},{2,6},{3,7},{4,0},{5,1},{6,2},{7,3},{8,12},{9,13},{10,... | collective-permute-start | bytes 737288 | tf_op jit(solution)/shard_map/ppermute | solution.py:274
  72.0 2.6 %collective-permute-done.8.refs_1_ = bf16[4,120,256]{2,1,0:T(8,128)(2,1)S(1)} collective-permute-done((bf16[4,120,256]{2,1,0:T(8,128)(2,1)S(1)}, bf16[4,120,256]{2,1,0:T(8,128)(2,1)S(1)}, u32[]{:S(2)}, u32[]{:S(2)}) %collective-permute-start.8) | collective-permute-done | bytes 245792 | tf_op jit(solution)/shard_map/ppermute | solution.py:274
  74.6 1.5 %collective-permute-start.3 = (bf16[4,120,256]{2,1,0:T(8,128)(2,1)S(1)}, bf16[4,120,256]{2,1,0:T(8,128)(2,1)S(1)}, u32[]{:S(2)}, u32[]{:S(2)}) collective-permute-start(bf16[4,120,256]{2,1,0:T(8,128)(2,1)S(1)} %get-tuple-element.36), channel_id=1, source_target_pairs={{0,6},{1,7},{2,4},{3,5},{4,2},{5,3},{6,0},{7,1},{8,14},{9,15},{10,... | collective-permute-start | bytes 737288 | tf_op jit(solution)/shard_map/ppermute | solution.py:274
  76.1 4.6 %collective-permute-done.10.refs_3_ = bf16[4,120,256]{2,1,0:T(8,128)(2,1)S(1)} collective-permute-done((bf16[4,120,256]{2,1,0:T(8,128)(2,1)S(1)}, bf16[4,120,256]{2,1,0:T(8,128)(2,1)S(1)}, u32[]{:S(2)}, u32[]{:S(2)}) %collective-permute-start.10) | collective-permute-done | bytes 245792 | tf_op jit(solution)/shard_map/ppermute | solution.py:274
  80.7 1.4 %plane_sum.3 = (f32[120,256]{1,0:T(8,128)S(1)}, bf16[120,256]{1,0:T(8,128)(2,1)S(1)}, bf16[120,256]{1,0:T(8,128)(2,1)S(1)}, bf16[120,256]{1,0:T(8,128)(2,1)S(1)}) custom-call(s32[6]{0:T(128)S(1)} %copy-done.4, f32[4,120,256]{2,1,0:T(8,128)S(1)} %get-tuple-element.44.refs_0_, bf16[4,120,256]{2,1,0:T(8,128)(2,1)S(1)} %collective-permute-done.8.refs_1_, ...), custom_call_target="tpu_custom_call" | custom-call | tf_op jit(solution)/shard_map/plane_sum/pallas_call | solution.py:67
  82.1 1.6 %collective-permute-start.11 = (bf16[120,256]{1,0:T(8,128)(2,1)S(1)}, bf16[120,256]{1,0:T(8,128)(2,1)S(1)}, u32[]{:S(2)}, u32[]{:S(2)}) collective-permute-start(bf16[120,256]{1,0:T(8,128)(2,1)S(1)} %get-tuple-element.49), channel_id=1, source_target_pairs={{0,8},{1,9},{2,10},{3,11},{4,12},{5,13},{6,14},{7,15},{8,16},{9,17... | collective-permute-start | bytes 184328 | tf_op jit(solution)/shard_map/ppermute | solution.py:274
  83.8 2.6 %collective-permute-start.12 = (bf16[120,256]{1,0:T(8,128)(2,1)S(1)}, bf16[120,256]{1,0:T(8,128)(2,1)S(1)}, u32[]{:S(2)}, u32[]{:S(2)}) collective-permute-start(bf16[120,256]{1,0:T(8,128)(2,1)S(1)} %get-tuple-element.50), channel_id=1, source_target_pairs={{0,16},{1,17},{2,18},{3,19},{4,20},{5,21},{6,22},{7,23},{8,24},{9,... | collective-permute-start | bytes 184328 | tf_op jit(solution)/shard_map/ppermute | solution.py:274
  86.4 1.3 %collective-permute-start.13 = (bf16[120,256]{1,0:T(8,128)(2,1)S(1)}, bf16[120,256]{1,0:T(8,128)(2,1)S(1)}, u32[]{:S(2)}, u32[]{:S(2)}) collective-permute-start(bf16[120,256]{1,0:T(8,128)(2,1)S(1)} %get-tuple-element.51), channel_id=1, source_target_pairs={{0,24},{1,25},{2,26},{3,27},{4,28},{5,29},{6,30},{7,31},{8,0},{9,1... | collective-permute-start | bytes 184328 | tf_op jit(solution)/shard_map/ppermute | solution.py:274
  87.7 2.4 %collective-permute-done.3.refs_3_ = bf16[4,120,256]{2,1,0:T(8,128)(2,1)S(1)} collective-permute-done((bf16[4,120,256]{2,1,0:T(8,128)(2,1)S(1)}, bf16[4,120,256]{2,1,0:T(8,128)(2,1)S(1)}, u32[]{:S(2)}, u32[]{:S(2)}) %collective-permute-start.3) | collective-permute-done | bytes 245792 | tf_op jit(solution)/shard_map/ppermute | solution.py:274
  90.2 1.4 %plane_sum.2 = (f32[120,256]{1,0:T(8,128)S(1)}, bf16[120,256]{1,0:T(8,128)(2,1)S(1)}, bf16[120,256]{1,0:T(8,128)(2,1)S(1)}, bf16[120,256]{1,0:T(8,128)(2,1)S(1)}) custom-call(s32[6]{0:T(128)S(1)} %copy-done.4, f32[4,120,256]{2,1,0:T(8,128)S(1)} %get-tuple-element.33.refs_0_, bf16[4,120,256]{2,1,0:T(8,128)(2,1)S(1)} %collective-permute-done.1.refs_1_, ...), custom_call_target="tpu_custom_call" | custom-call | tf_op jit(solution)/shard_map/plane_sum/pallas_call | solution.py:67
  91.6 1.6 %collective-permute-start.4 = (bf16[120,256]{1,0:T(8,128)(2,1)S(1)}, bf16[120,256]{1,0:T(8,128)(2,1)S(1)}, u32[]{:S(2)}, u32[]{:S(2)}) collective-permute-start(bf16[120,256]{1,0:T(8,128)(2,1)S(1)} %get-tuple-element.38), channel_id=1, source_target_pairs={{0,8},{1,9},{2,10},{3,11},{4,12},{5,13},{6,14},{7,15},{8,16},{9,17... | collective-permute-start | bytes 184328 | tf_op jit(solution)/shard_map/ppermute | solution.py:274
  93.2 2.6 %collective-permute-start.5 = (bf16[120,256]{1,0:T(8,128)(2,1)S(1)}, bf16[120,256]{1,0:T(8,128)(2,1)S(1)}, u32[]{:S(2)}, u32[]{:S(2)}) collective-permute-start(bf16[120,256]{1,0:T(8,128)(2,1)S(1)} %get-tuple-element.39), channel_id=1, source_target_pairs={{0,16},{1,17},{2,18},{3,19},{4,20},{5,21},{6,22},{7,23},{8,24},{9,... | collective-permute-start | bytes 184328 | tf_op jit(solution)/shard_map/ppermute | solution.py:274
  95.8 1.3 %collective-permute-start.6 = (bf16[120,256]{1,0:T(8,128)(2,1)S(1)}, bf16[120,256]{1,0:T(8,128)(2,1)S(1)}, u32[]{:S(2)}, u32[]{:S(2)}) collective-permute-start(bf16[120,256]{1,0:T(8,128)(2,1)S(1)} %get-tuple-element.40), channel_id=1, source_target_pairs={{0,24},{1,25},{2,26},{3,27},{4,28},{5,29},{6,30},{7,31},{8,0},{9,1... | collective-permute-start | bytes 184328 | tf_op jit(solution)/shard_map/ppermute | solution.py:274
  98.7 2.1 %collective-permute-start.16 = (f32[120,120]{1,0:T(8,128)S(1)}, f32[120,120]{1,0:T(8,128)S(1)}, u32[]{:S(2)}, u32[]{:S(2)}) collective-permute-start(f32[120,120]{1,0:T(8,128)S(1)} %get-tuple-element.55), channel_id=1, source_target_pairs={{0,0},{1,8},{2,16},{3,24},{4,4},{5,12},{6,20},{7,28},{8,1},{9,9},{... | collective-permute-start | bytes 172808 | tf_op jit(solution)/shard_map/ppermute | solution.py:274
  100.7 4.7 %collective-permute-start.17 = (f32[120,120]{1,0:T(8,128)S(1)}, f32[120,120]{1,0:T(8,128)S(1)}, u32[]{:S(2)}, u32[]{:S(2)}) collective-permute-start(f32[120,120]{1,0:T(8,128)S(1)} %get-tuple-element.56), channel_id=1, source_target_pairs={{0,4},{1,12},{2,20},{3,28},{4,0},{5,8},{6,16},{7,24},{8,5},{9,13},... | collective-permute-start | bytes 172808 | tf_op jit(solution)/shard_map/ppermute | solution.py:274
  107.0 2.2 %collective-permute-start.14 = (f32[120,120]{1,0:T(8,128)S(1)}, f32[120,120]{1,0:T(8,128)S(1)}, u32[]{:S(2)}, u32[]{:S(2)}) collective-permute-start(f32[120,120]{1,0:T(8,128)S(1)} %get-tuple-element.53), channel_id=1, source_target_pairs={{0,0},{1,8},{2,16},{3,24},{4,4},{5,12},{6,20},{7,28},{8,1},{9,9},{... | collective-permute-start | bytes 172808 | tf_op jit(solution)/shard_map/ppermute | solution.py:274
  109.2 3.5 %collective-permute-start.15 = (f32[120,120]{1,0:T(8,128)S(1)}, f32[120,120]{1,0:T(8,128)S(1)}, u32[]{:S(2)}, u32[]{:S(2)}) collective-permute-start(f32[120,120]{1,0:T(8,128)S(1)} %get-tuple-element.54), channel_id=1, source_target_pairs={{0,4},{1,12},{2,20},{3,28},{4,0},{5,8},{6,16},{7,24},{8,5},{9,13},... | collective-permute-start | bytes 172808 | tf_op jit(solution)/shard_map/ppermute | solution.py:274
  112.7 2.2 %collective-permute-done.14.refs_2_ = f32[120,120]{1,0:T(8,128)S(1)} collective-permute-done((f32[120,120]{1,0:T(8,128)S(1)}, f32[120,120]{1,0:T(8,128)S(1)}, u32[]{:S(2)}, u32[]{:S(2)}) %collective-permute-start.14) | collective-permute-done | bytes 57632 | tf_op jit(solution)/shard_map/ppermute | solution.py:274
  116.8 2.1 %outcome.1 = f32[2,120,2,240]{3,2,1,0:T(2,128)} custom-call(s32[6]{0:T(128)} %stack.27.index, f32[120,256]{1,0:T(8,128)} %copy-done.3, f32[120,256]{1,0:T(8,128)} %copy-done.2, f32[120,120]{1,0:T(8,128)} %copy-done.7, f32[120,120]{1,0:T(8,128)} %copy-done.8, f32[120,120]{1,0:T(8,128)} %copy-done.5, f32[120,120]{1,0:T(8,128)} %copy-done.6), custom_call_target="tpu_custom_call" | custom-call | tf_op jit(solution)/shard_map/outcome/pallas_call | solution.py:379
  (40 shorter events, 8.4 us)
Async XLA Ops:
  32.0 31.7 %copy-start.1 = (f32[2,960,256]{2,1,0:T(8,128)S(1)}, f32[2,960,256]{2,1,0:T(8,128)}, u32[]{:S(2)}) copy-start(f32[2,960,256]{2,1,0:T(8,128)} %get-tuple-element.42) | copy-start | bytes 5898244
  32.0 31.7 %copy-start.4 = (s32[6]{0:T(128)S(1)}, s32[6]{0:T(128)}, u32[]{:S(2)}) copy-start(s32[6]{0:T(128)} %stack.27.index) | copy-start | bytes 76
  32.0 31.7 %collective-permute-start.7 = (f32[2,960,256]{2,1,0:T(8,128)}, f32[2,960,256]{2,1,0:T(8,128)S(1)}, u32[]{:S(2)}, u32[]{:S(2)}) collective-permute-start(f32[2,960,256]{2,1,0:T(8,128)} %get-tuple-element.43), channel_id=1, source_target_pairs={{0,1},{1,0},{2,3},{3,2},{4,5},{5,4},{6,7},{7,6},{8,9},{9,8},{10,11... | collective-permute-start | bytes 5898248 | tf_op jit(solution)/shard_map/ppermute | solution.py:274
  63.3 5.3 %collective-permute-start = (f32[2,960,256]{2,1,0:T(8,128)}, f32[2,960,256]{2,1,0:T(8,128)S(1)}, u32[]{:S(2)}, u32[]{:S(2)}) collective-permute-start(f32[2,960,256]{2,1,0:T(8,128)} %get-tuple-element.32), channel_id=1, source_target_pairs={{0,1},{1,0},{2,3},{3,2},{4,5},{5,4},{6,7},{7,6},{8,9},{9,8},{10,11... | collective-permute-start | bytes 5898248 | tf_op jit(solution)/shard_map/ppermute | solution.py:274
  63.7 4.9 %copy-start = (f32[2,960,256]{2,1,0:T(8,128)S(1)}, f32[2,960,256]{2,1,0:T(8,128)}, u32[]{:S(2)}) copy-start(f32[2,960,256]{2,1,0:T(8,128)} %get-tuple-element.31) | copy-start | bytes 5898244
  65.1 9.6 %collective-permute-start.8 = (bf16[4,120,256]{2,1,0:T(8,128)(2,1)S(1)}, bf16[4,120,256]{2,1,0:T(8,128)(2,1)S(1)}, u32[]{:S(2)}, u32[]{:S(2)}) collective-permute-start(bf16[4,120,256]{2,1,0:T(8,128)(2,1)S(1)} %get-tuple-element.45), channel_id=1, source_target_pairs={{0,4},{1,5},{2,6},{3,7},{4,0},{5,1},{6,2},{7,3},{8,12},{9,13},{10,... | collective-permute-start | bytes 737288 | tf_op jit(solution)/shard_map/ppermute | solution.py:274
  66.6 9.5 %collective-permute-start.9 = (bf16[4,120,256]{2,1,0:T(8,128)(2,1)S(1)}, bf16[4,120,256]{2,1,0:T(8,128)(2,1)S(1)}, u32[]{:S(2)}, u32[]{:S(2)}) collective-permute-start(bf16[4,120,256]{2,1,0:T(8,128)(2,1)S(1)} %get-tuple-element.46), channel_id=1, source_target_pairs={{0,2},{1,3},{2,0},{3,1},{4,6},{5,7},{6,4},{7,5},{8,10},{9,11},{10,... | collective-permute-start | bytes 737288 | tf_op jit(solution)/shard_map/ppermute | solution.py:274
  67.2 13.6 %collective-permute-start.10 = (bf16[4,120,256]{2,1,0:T(8,128)(2,1)S(1)}, bf16[4,120,256]{2,1,0:T(8,128)(2,1)S(1)}, u32[]{:S(2)}, u32[]{:S(2)}) collective-permute-start(bf16[4,120,256]{2,1,0:T(8,128)(2,1)S(1)} %get-tuple-element.47), channel_id=1, source_target_pairs={{0,6},{1,7},{2,4},{3,5},{4,2},{5,3},{6,0},{7,1},{8,14},{9,15},{10,... | collective-permute-start | bytes 737288 | tf_op jit(solution)/shard_map/ppermute | solution.py:274
  69.9 16.5 %collective-permute-start.1 = (bf16[4,120,256]{2,1,0:T(8,128)(2,1)S(1)}, bf16[4,120,256]{2,1,0:T(8,128)(2,1)S(1)}, u32[]{:S(2)}, u32[]{:S(2)}) collective-permute-start(bf16[4,120,256]{2,1,0:T(8,128)(2,1)S(1)} %get-tuple-element.34), channel_id=1, source_target_pairs={{0,4},{1,5},{2,6},{3,7},{4,0},{5,1},{6,2},{7,3},{8,12},{9,13},{10,... | collective-permute-start | bytes 737288 | tf_op jit(solution)/shard_map/ppermute | solution.py:274
  71.5 16.2 %collective-permute-start.2 = (bf16[4,120,256]{2,1,0:T(8,128)(2,1)S(1)}, bf16[4,120,256]{2,1,0:T(8,128)(2,1)S(1)}, u32[]{:S(2)}, u32[]{:S(2)}) collective-permute-start(bf16[4,120,256]{2,1,0:T(8,128)(2,1)S(1)} %get-tuple-element.35), channel_id=1, source_target_pairs={{0,2},{1,3},{2,0},{3,1},{4,6},{5,7},{6,4},{7,5},{8,10},{9,11},{10,... | collective-permute-start | bytes 737288 | tf_op jit(solution)/shard_map/ppermute | solution.py:274
  74.6 15.5 %collective-permute-start.3 = (bf16[4,120,256]{2,1,0:T(8,128)(2,1)S(1)}, bf16[4,120,256]{2,1,0:T(8,128)(2,1)S(1)}, u32[]{:S(2)}, u32[]{:S(2)}) collective-permute-start(bf16[4,120,256]{2,1,0:T(8,128)(2,1)S(1)} %get-tuple-element.36), channel_id=1, source_target_pairs={{0,6},{1,7},{2,4},{3,5},{4,2},{5,3},{6,0},{7,1},{8,14},{9,15},{10,... | collective-permute-start | bytes 737288 | tf_op jit(solution)/shard_map/ppermute | solution.py:274
  82.1 13.6 %collective-permute-start.11 = (bf16[120,256]{1,0:T(8,128)(2,1)S(1)}, bf16[120,256]{1,0:T(8,128)(2,1)S(1)}, u32[]{:S(2)}, u32[]{:S(2)}) collective-permute-start(bf16[120,256]{1,0:T(8,128)(2,1)S(1)} %get-tuple-element.49), channel_id=1, source_target_pairs={{0,8},{1,9},{2,10},{3,11},{4,12},{5,13},{6,14},{7,15},{8,16},{9,17... | collective-permute-start | bytes 184328 | tf_op jit(solution)/shard_map/ppermute | solution.py:274
  83.8 13.4 %collective-permute-start.12 = (bf16[120,256]{1,0:T(8,128)(2,1)S(1)}, bf16[120,256]{1,0:T(8,128)(2,1)S(1)}, u32[]{:S(2)}, u32[]{:S(2)}) collective-permute-start(bf16[120,256]{1,0:T(8,128)(2,1)S(1)} %get-tuple-element.50), channel_id=1, source_target_pairs={{0,16},{1,17},{2,18},{3,19},{4,20},{5,21},{6,22},{7,23},{8,24},{9,... | collective-permute-start | bytes 184328 | tf_op jit(solution)/shard_map/ppermute | solution.py:274
  86.4 10.8 %collective-permute-start.13 = (bf16[120,256]{1,0:T(8,128)(2,1)S(1)}, bf16[120,256]{1,0:T(8,128)(2,1)S(1)}, u32[]{:S(2)}, u32[]{:S(2)}) collective-permute-start(bf16[120,256]{1,0:T(8,128)(2,1)S(1)} %get-tuple-element.51), channel_id=1, source_target_pairs={{0,24},{1,25},{2,26},{3,27},{4,28},{5,29},{6,30},{7,31},{8,0},{9,1... | collective-permute-start | bytes 184328 | tf_op jit(solution)/shard_map/ppermute | solution.py:274
  91.6 13.9 %collective-permute-start.4 = (bf16[120,256]{1,0:T(8,128)(2,1)S(1)}, bf16[120,256]{1,0:T(8,128)(2,1)S(1)}, u32[]{:S(2)}, u32[]{:S(2)}) collective-permute-start(bf16[120,256]{1,0:T(8,128)(2,1)S(1)} %get-tuple-element.38), channel_id=1, source_target_pairs={{0,8},{1,9},{2,10},{3,11},{4,12},{5,13},{6,14},{7,15},{8,16},{9,17... | collective-permute-start | bytes 184328 | tf_op jit(solution)/shard_map/ppermute | solution.py:274
  93.2 12.2 %collective-permute-start.5 = (bf16[120,256]{1,0:T(8,128)(2,1)S(1)}, bf16[120,256]{1,0:T(8,128)(2,1)S(1)}, u32[]{:S(2)}, u32[]{:S(2)}) collective-permute-start(bf16[120,256]{1,0:T(8,128)(2,1)S(1)} %get-tuple-element.39), channel_id=1, source_target_pairs={{0,16},{1,17},{2,18},{3,19},{4,20},{5,21},{6,22},{7,23},{8,24},{9,... | collective-permute-start | bytes 184328 | tf_op jit(solution)/shard_map/ppermute | solution.py:274
  95.8 9.6 %collective-permute-start.6 = (bf16[120,256]{1,0:T(8,128)(2,1)S(1)}, bf16[120,256]{1,0:T(8,128)(2,1)S(1)}, u32[]{:S(2)}, u32[]{:S(2)}) collective-permute-start(bf16[120,256]{1,0:T(8,128)(2,1)S(1)} %get-tuple-element.40), channel_id=1, source_target_pairs={{0,24},{1,25},{2,26},{3,27},{4,28},{5,29},{6,30},{7,31},{8,0},{9,1... | collective-permute-start | bytes 184328 | tf_op jit(solution)/shard_map/ppermute | solution.py:274
  98.7 14.0 %collective-permute-start.16 = (f32[120,120]{1,0:T(8,128)S(1)}, f32[120,120]{1,0:T(8,128)S(1)}, u32[]{:S(2)}, u32[]{:S(2)}) collective-permute-start(f32[120,120]{1,0:T(8,128)S(1)} %get-tuple-element.55), channel_id=1, source_target_pairs={{0,0},{1,8},{2,16},{3,24},{4,4},{5,12},{6,20},{7,28},{8,1},{9,9},{... | collective-permute-start | bytes 172808 | tf_op jit(solution)/shard_map/ppermute | solution.py:274
  100.7 12.0 %collective-permute-start.17 = (f32[120,120]{1,0:T(8,128)S(1)}, f32[120,120]{1,0:T(8,128)S(1)}, u32[]{:S(2)}, u32[]{:S(2)}) collective-permute-start(f32[120,120]{1,0:T(8,128)S(1)} %get-tuple-element.56), channel_id=1, source_target_pairs={{0,4},{1,12},{2,20},{3,28},{4,0},{5,8},{6,16},{7,24},{8,5},{9,13},... | collective-permute-start | bytes 172808 | tf_op jit(solution)/shard_map/ppermute | solution.py:274
  107.0 7.9 %collective-permute-start.14 = (f32[120,120]{1,0:T(8,128)S(1)}, f32[120,120]{1,0:T(8,128)S(1)}, u32[]{:S(2)}, u32[]{:S(2)}) collective-permute-start(f32[120,120]{1,0:T(8,128)S(1)} %get-tuple-element.53), channel_id=1, source_target_pairs={{0,0},{1,8},{2,16},{3,24},{4,4},{5,12},{6,20},{7,28},{8,1},{9,9},{... | collective-permute-start | bytes 172808 | tf_op jit(solution)/shard_map/ppermute | solution.py:274
  109.2 7.0 %collective-permute-start.15 = (f32[120,120]{1,0:T(8,128)S(1)}, f32[120,120]{1,0:T(8,128)S(1)}, u32[]{:S(2)}, u32[]{:S(2)}) collective-permute-start(f32[120,120]{1,0:T(8,128)S(1)} %get-tuple-element.54), channel_id=1, source_target_pairs={{0,4},{1,12},{2,20},{3,28},{4,0},{5,8},{6,16},{7,24},{8,5},{9,13},... | collective-permute-start | bytes 172808 | tf_op jit(solution)/shard_map/ppermute | solution.py:274
  112.7 3.5 %copy-start.5 = (f32[120,120]{1,0:T(8,128)}, f32[120,120]{1,0:T(8,128)S(1)}, u32[]{:S(2)}) copy-start(f32[120,120]{1,0:T(8,128)S(1)} %collective-permute-done.16.refs_4_) | copy-start | bytes 172804
  112.7 3.5 %copy-start.6 = (f32[120,120]{1,0:T(8,128)}, f32[120,120]{1,0:T(8,128)S(1)}, u32[]{:S(2)}) copy-start(f32[120,120]{1,0:T(8,128)S(1)} %collective-permute-done.17.refs_5_) | copy-start | bytes 172804
  114.9 1.3 %copy-start.7 = (f32[120,120]{1,0:T(8,128)}, f32[120,120]{1,0:T(8,128)S(1)}, u32[]{:S(2)}) copy-start(f32[120,120]{1,0:T(8,128)S(1)} %collective-permute-done.14.refs_2_) | copy-start | bytes 172804
  (3 other events, 1.9 us)

commit v3 on v0

v3 whole, which is shorter than its diff:
```python
import math

import jax
import jax.numpy as jnp
from jax import lax
from jax.experimental import pallas as pl
from jax.experimental.pallas import tpu as pltpu
from jax.sharding import PartitionSpec as P

AXES = ("pair", "virt")
F32, BF16 = jnp.float32, jnp.bfloat16
TOP = 1024.0
LANES = 128
ANY = pl.BlockSpec(memory_space=pl.ANY)
VMEM = pl.BlockSpec(memory_space=pltpu.VMEM)
SMEM = pl.BlockSpec(memory_space=pltpu.SMEM)


def dot(left, right):
    return jnp.dot(left, right, preferred_element_type=F32)


def iota(shape, axis):
    return lax.broadcasted_iota(jnp.int32, shape, axis)


def bound_at(block, at):
    return block[0:1, at : at + 1].astype(F32)


def with_bound(block, bound, at):
    here = (iota(block.shape, 0) == 0) & (iota(block.shape, 1) == at)
    return jnp.where(here, bound, block)


def sent_bound(bound):
    return jnp.maximum(bound * 1.01, 1e-35).astype(BF16).astype(F32)


def coded(values, bound):
    scaled = jnp.abs(values) * (TOP / bound)
    fourth = scaled * scaled
    fourth = fourth * fourth
    power = fourth * fourth * fourth
    return jnp.where(values < 0, -power, power)


def decoded(block, bound):
    power = block.astype(F32)
    magnitude = jnp.exp2(jnp.log2(jnp.maximum(jnp.abs(power), 1e-37)) * (1 / 12)) * (bound * (1 / TOP))
    return jnp.where(power == 0, 0.0, jnp.where(power < 0, -magnitude, magnitude))


def local(body, out_types, aligned, name, cost=0):
    def kernel(index, *refs):
        results = body(index, *refs[: -len(out_types)])
        for ref, result in zip(refs[-len(out_types) :], results):
            if isinstance(result, list):
                for n, block in enumerate(result):
                    ref[n] = block.astype(ref.dtype)
            else:
                ref[...] = result.astype(ref.dtype)

    def call(index, *arrays):
        if not aligned:
            results = body(index, *arrays)
            results = [jnp.stack(result) if isinstance(result, list) else result for result in results]
            return [result.astype(kind.dtype) for result, kind in zip(results, out_types)]
        return pl.pallas_call(
            kernel,
            in_specs=[SMEM] + [VMEM] * len(arrays),
            out_specs=[VMEM] * len(out_types),
            out_shape=out_types,
            name=name,
            cost_estimate=pl.CostEstimate(flops=cost, bytes_accessed=2**20, transcendentals=0),
            compiler_params=pltpu.CompilerParams(vmem_limit_bytes=4 * 2**20),
        )(index, *arrays)

    return call


def lane_tiles(virtuals):
    return -(-virtuals // LANES)


def lanes(tile, virtuals):
    return min(LANES, virtuals - LANES * tile)


def product(u, w, i, j, rows, n):
    _, depth, virtuals, inner = u.shape
    total = None
    for k in range(depth):
        parts = [
            w[pl.ds((t * depth + k) * 2 * inner + j, inner, 2), :][:, : lanes(t, virtuals)]
            for t in (2 * n, 2 * n + 1)
        ]
        term = dot(u[i, k, rows, :], jnp.concatenate(parts, axis=1))
        total = term if total is None else total + term
    return total


def pair_of_tiles(n, virtuals):
    return slice(2 * LANES * n, min(2 * LANES * (n + 1), virtuals))


def brought(u_hbm, w_hbm, u, w, sems):
    _, depth, virtuals, inner = u_hbm.shape
    tiles = lane_tiles(virtuals)
    w_rows = w_hbm.reshape(depth * inner * 2, virtuals)

    def u_copies(i):
        return [pltpu.make_async_copy(u_hbm.at[i, k], u.at[i, k], sems.at[i, k]) for k in range(depth)]

    def tile_rows(tile):
        return pl.ds(tile * depth * inner * 2, depth * inner * 2)

    def w_copy(tile):
        source = w_rows.at[:, pl.ds(LANES * tile, LANES)]
        return pltpu.make_async_copy(source, w.at[tile_rows(tile)], sems.at[2, tile])

    def last_tile(block):
        w[tile_rows(tiles - 1), :] = block.reshape(depth * inner * 2, LANES)[...]

    groups = [
        u_copies(1) + [w_copy(tile) for tile in range(2)],
        [w_copy(tile) for tile in range(2, tiles - 1)],
        u_copies(0),
    ]

    def start(group):
        for copy in groups[group]:
            copy.start()

    def wait(group):
        for copy in groups[group]:
            copy.wait()

    start(0)
    pltpu.emit_pipeline(
        last_tile,
        grid=(1,),
        in_specs=[pl.BlockSpec((depth, inner, 2, LANES), lambda _: (0, 0, 0, tiles - 1))],
    )(w_hbm)
    return start, wait


class Half:
    def __init__(self, out, low, cols):
        self.out, self.low, self.cols = out, low, cols
        self.high = low + out.shape[1]
        self.largest = jnp.zeros((1, cols), F32)

    def place(self, v, r0, r1, block):
        self.out[v, r0 - self.low : r1 - self.low, : self.cols] = block
        self.largest = jnp.maximum(self.largest, jnp.max(jnp.abs(block), axis=0, keepdims=True))

    def finish(self, index, kept, sent):
        out, cols = self.out, self.cols
        largest = jnp.max(self.largest)
        for v in range(2):
            head = out[v, 0:8, cols:]
            here = (iota(head.shape, 0) == 0) & (iota(head.shape, 1) == 1)
            out[v, 0:8, cols:] = jnp.where(here, largest, head)
        for core in range(2):

            @pl.when(index[1] == core)
            def _():
                for x in range(kept.shape[0]):
                    kept[x] = out[2 * x + core]
                    sent[x] = out[2 * x + 1 - core]


def crossed_kernel(cols):
    def kernel(index, u_hbm, w_hbm, kept, sent, u, w, other, own, out, sems):
        virtuals = u.shape[2]
        tiles = lane_tiles(virtuals)
        start, wait = brought(u_hbm, w_hbm, u, w, sems)
        half = Half(out, 0, cols)
        everything = slice(0, virtuals)
        wait(0)
        start(1)
        other[:, pair_of_tiles(0, virtuals)] = product(u, w, 1, 0, everything, 0)
        wait(1)
        start(2)
        for n in range(1, tiles // 2):
            other[:, pair_of_tiles(n, virtuals)] = product(u, w, 1, 0, everything, n)
        wait(2)
        v = 0
        for n in range(tiles // 2):
            columns = pair_of_tiles(n, virtuals)
            own[:, columns] = product(u, w, 0, 1, everything, n)
            while (v + 1) * cols <= columns.stop:
                on, past = v * cols, (v + 1) * cols
                for t in range(tiles):
                    r0, r1 = LANES * t, LANES * t + lanes(t, virtuals)
                    half.place(v, r0, r1, own[r0:r1, on:past] + other[on:past, r0:r1].T)
                v += 1
        half.finish(index, kept, sent)

    return kernel


def first_square_kernel(index, u, w, square):
    virtuals = u.shape[2]
    for n in range(lane_tiles(virtuals) // 2):
        square[:, pair_of_tiles(n, virtuals)] = product(u, w, 0, 0, slice(0, virtuals // 2), n)


def other_squares_kernel(index, u, w, rest, square):
    virtuals = u.shape[2]
    for n in range(lane_tiles(virtuals) // 2):
        rest[:, pair_of_tiles(n, virtuals)] = product(u, w, 0, 0, slice(virtuals // 2, virtuals), n)
        square[:, pair_of_tiles(n, virtuals)] = product(u, w, 1, 1, slice(0, virtuals), n)


def same_kernel(cols):
    def kernel(index, p00, p00_rest, p11, kept, sent, out):
        virtuals = p11.shape[0]
        middle, tiles, nv = virtuals // 2, lane_tiles(virtuals), virtuals // cols
        half = Half(out, 0, cols)

        def rows_of(i, r0, r1, c0, c1):
            if i == 1:
                return p11[r0:r1, c0:c1]
            if r1 <= middle:
                return p00[r0:r1, c0:c1]
            if r0 >= middle:
                return p00_rest[r0 - middle : r1 - middle, c0:c1]
            return jnp.concatenate([p00[r0:middle, c0:c1], p00_rest[0 : r1 - middle, c0:c1]], axis=0)

        def segment(v, tile):
            begin, end = LANES * tile, LANES * tile + lanes(tile, virtuals)
            on, past = v * cols, (v + 1) * cols
            flips = {}

            def symmetric(i, r0, r1):
                if i not in flips:
                    flips[i] = rows_of(i, on, past, begin, end).T
                return rows_of(i, r0, r1, on, past) + flips[i][r0 - begin : r1 - begin]

            r0, r1 = begin, min(end, on)
            if r0 < r1:
                half.place(v, r0, r1, symmetric(0, r0, r1))
            r0, r1 = max(begin, on), min(end, past)
            if r0 < r1:
                s00, s11 = symmetric(0, r0, r1), symmetric(1, r0, r1)
                a, b = r0 + iota(s00.shape, 0), on + iota(s00.shape, 1)
                half.place(v, r0, r1, jnp.where(a <= b, s00, s11))
                diagonal = jnp.where(a == b, s11, 0.0)
                out[v, r0:r1, cols : cols + 1] = jnp.sum(diagonal, axis=1, keepdims=True)
                half.largest = jnp.maximum(half.largest, jnp.max(jnp.abs(diagonal), axis=0, keepdims=True))
            r0, r1 = max(begin, past), end
            if r0 < r1:
                half.place(v, r0, r1, symmetric(1, r0, r1))

        for v in range(nv):
            for t in range(tiles):
                segment(v, t)
        half.finish(index, kept, sent)

    return kernel


def on_chip(body, name, out_shape, scratch, flops, index, u, w, *arrays):
    ins = 3 + len(arrays)
    outs = ins + len(out_shape)

    def kernel(*refs):
        body(*refs[:outs], *refs[outs + 2 :])

    *results, u, w = pl.pallas_call(
        kernel,
        in_specs=[SMEM] + [VMEM] * (ins - 1),
        out_specs=[VMEM] * (len(out_shape) + 2),
        out_shape=[*out_shape, jax.ShapeDtypeStruct(u.shape, u.dtype), jax.ShapeDtypeStruct(w.shape, w.dtype)],
        input_output_aliases={1: len(out_shape), 2: len(out_shape) + 1},
        scratch_shapes=[pltpu.VMEM(shape, F32) for shape in scratch],
        name=name,
        cost_estimate=pl.CostEstimate(flops=flops, bytes_accessed=2**20, transcendentals=0),
        compiler_params=pltpu.CompilerParams(vmem_limit_bytes=5 * 2**20),
    )(index, u, w, *arrays)
    return results, u, w


def crossed_sums(index, amplitudes, integrals, half_types, cols):
    _, depth, virtuals, inner = amplitudes.shape
    tiles = lane_tiles(virtuals)
    width, nv = half_types[0].shape[-1], virtuals // cols
    kept, sent, u, w = pl.pallas_call(
        crossed_kernel(cols),
        in_specs=[SMEM, ANY, ANY],
        out_specs=[VMEM] * 4,
        out_shape=[
            *half_types,
            jax.ShapeDtypeStruct(amplitudes.shape, BF16),
            jax.ShapeDtypeStruct((tiles * depth * inner * 2, LANES), BF16),
        ],
        scratch_shapes=[
            pltpu.VMEM((virtuals, virtuals), F32),
            pltpu.VMEM((virtuals, virtuals), F32),
            pltpu.VMEM((nv, virtuals, width), F32),
            pltpu.SemaphoreType.DMA((3, max(depth, tiles))),
        ],
        name="crossed",
        cost_estimate=pl.CostEstimate(
            flops=4 * depth * inner * virtuals * virtuals, bytes_accessed=4 * amplitudes.size, transcendentals=0
        ),
        compiler_params=pltpu.CompilerParams(vmem_limit_bytes=20 * 2**20),
    )(index, amplitudes, integrals)
    return (kept, sent), u, w


def after(value, *others):
    return lax.optimization_barrier((value, *others))[0]


def plain_sums(index, amplitudes, integrals, same, nv, width):
    virtuals = amplitudes.shape[2]
    cols = virtuals // nv

    def cycle(i, j):
        return jnp.einsum("kac,kcb->ab", amplitudes[i], integrals[:, :, j], preferred_element_type=F32)

    if same:
        s00, s11 = ((q + q.T) for q in (cycle(0, 0), cycle(1, 1)))
        a, b = (iota((virtuals, virtuals), axis) for axis in range(2))
        block, diagonal = jnp.where(a <= b, s00, s11), jnp.diagonal(s11)
    else:
        block, diagonal = cycle(0, 1) + cycle(1, 0).T, jnp.zeros((virtuals,), F32)
    largest = jnp.maximum(jnp.max(jnp.abs(block)), jnp.max(jnp.abs(diagonal)))
    parts = block.reshape(virtuals, nv, cols).transpose(1, 0, 2)
    extra = jnp.stack([diagonal, jnp.full((virtuals,), largest)], axis=1)
    extra = jnp.pad(extra, ((0, 0), (0, width - cols - 2)))
    parts = jnp.concatenate([parts, jnp.broadcast_to(extra, (nv, *extra.shape))], axis=2)
    parts = parts.reshape(nv // 2, 2, virtuals, width)
    return [lax.dynamic_index_in_dim(parts, c, 1, keepdims=False) for c in (index[1], 1 - index[1])]


def solution(mesh):
    np_, nv = mesh.shape["pair"], mesh.shape["virt"]
    nx, nz, ratio = nv // 2, np_ // 2, np_ // nv

    def send(block, move):
        pairs = []
        for p in range(np_):
            for v in range(nv):
                q, w = move(p, v)
                pairs.append((p * nv + v, q * nv + w))
        return lax.ppermute(block, AXES, pairs)

    def shards(amplitudes, integrals):
        _, _, virtuals, inner = amplitudes.shape
        rows, cols = virtuals // np_, virtuals // nv
        width = -(-(cols + 2) // LANES) * LANES
        at = cols + 1
        aligned = rows % 8 == 0 and inner % 16 == 0 and virtuals % 64 == 0
        p, v = lax.axis_index("pair"), lax.axis_index("virt")
        index = jnp.stack([v // 2, v % 2, p // 2, p % 2, p, v]).astype(jnp.int32)
        steps = [(dx, dy) for dx in range(nx) for dy in range(2) if dx or dy]

        def chip_sum(index, kept, came):
            x, y = index[0], index[3]
            bound = sent_bound(bound_at(kept[0, 0, 0], at) + bound_at(came[0, 0, 0], at))

            def block(x_at, y_at, z):
                return kept[x_at, z, y_at] + came[x_at, z, y_at]

            own = [block(x, y, z) for z in range(nz)]
            results = [[with_bound(own[0], bound, at)] + own[1:]]
            for dx, dy in steps:
                blocks = [coded(block((x + dx) % nx, (y + dy) % 2, z), bound) for z in range(nz)]
                results.append([with_bound(blocks[0], bound, at)] + blocks[1:])
            return results

        def plane_sum(index, own, *came):
            z_own = index[2]
            bounds = [bound_at(array[0], at) for array in came]
            bound = sent_bound(sum(bounds, bound_at(own[0], at)))

            def block(z):
                total = own[z]
                for array, of in zip(came, bounds):
                    total = total + decoded(array[z], of)
                return total

            results = [block(z_own)]
            for dz in range(1, nz):
                results.append(with_bound(coded(block((z_own + dz) % nz), bound), bound, at))
            return results

        def line_sum(count, paired):
            def body(index, own, *arrays):
                total = own[...]
                for array in arrays[:count]:
                    array = array[...]
                    total = total + decoded(array, bound_at(array, at))
                flipped = [total[:, h * rows : (h + 1) * rows].T for h in range(ratio)]
                results = [total]
                for t in range(ratio):
                    tile = flipped[0]
                    for h in range(1, ratio):
                        tile = jnp.where((index[4] + t) % ratio == h, flipped[h], tile)
                    results.append([arrays[count + t][...], tile] if paired else tile)
                return results

            return body

        def outcome(index, crossed, same, *came):
            def mirrored(which):
                parts = []
                for h in range(ratio):
                    part = came[0][which]
                    for t in range(1, ratio):
                        part = jnp.where((index[4] + ratio - h) % ratio == t, came[t][which], part)
                    parts.append(part)
                return jnp.concatenate(parts, axis=1) if ratio > 1 else parts[0]

            same = same[...]
            square = same[:, :cols]
            other = mirrored(1)
            a = index[4] * rows + iota(square.shape, 0)
            b = index[5] * cols + iota(square.shape, 1)
            out00 = jnp.where(a <= b, square, other)
            out11 = jnp.where(a > b, square, jnp.where(a == b, same[:, cols : cols + 1], other))
            return [out00, crossed[...][:, :cols], mirrored(0), out11]

        def outcome_kernel(index, *refs):
            for n, block in enumerate(outcome(index, *refs[:-1])):
                refs[-1][n // 2, :, n % 2, :] = block

        def kind(shape, dtype=F32):
            return jax.ShapeDtypeStruct(shape, dtype)

        work = amplitudes.size * virtuals

        def across_core(pair_of):
            return pair_of[0], send(pair_of[1], lambda p, v: (p, v ^ 1))

        def across_plane(index, kept, came):
            shape = (nx, nz, 2, rows, width)
            types = [kind((nz, rows, width))] + [kind((nz, rows, width), BF16)] * len(steps)
            own, *outs = local(chip_sum, types, aligned, "chip_sum", work)(index, kept.reshape(shape), came.reshape(shape))
            came = [send(block, lambda p, v: (p ^ dy, (v + 2 * dx) % nv)) for (dx, dy), block in zip(steps, outs)]
            return own, came

        def across_line(index, own, came):
            types = [kind((rows, width))] + [kind((rows, width), BF16)] * (nz - 1)
            own, *outs = local(plane_sum, types, aligned, "plane_sum", 2 * work)(index, own, *came)
            return own, [send(block, lambda p, v: ((p + 2 * dz) % np_, v)) for dz, block in zip(range(1, nz), outs)]

        def line_total(index, own, came, first_tiles=()):
            shape = (2, rows, rows) if first_tiles else (rows, rows)
            types = [kind((rows, width))] + [kind(shape)] * ratio
            body = line_sum(len(came), bool(first_tiles))
            return local(body, types, aligned, "line_sum")(index, own, *came, *first_tiles)

        def exchanged(tiles):
            return [
                send(tile, lambda p, v: (ratio * v + (p % ratio + t) % ratio, p // ratio)) for t, tile in enumerate(tiles)
            ]

        if aligned:
            half_types = [kind((nx, virtuals, width))] * 2
            crossed, u, w = crossed_sums(index, amplitudes, integrals, half_types, cols)
            crossed = across_core(crossed)
            square = kind((virtuals // 2, virtuals))
            (p00,), u, w = on_chip(
                first_square_kernel, "first_square", [square], [], work // 2, after(index, crossed[0]), u, w
            )
            crossed = across_plane(after(index, p00), *crossed)
            (p00_rest, p11), u, w = on_chip(
                other_squares_kernel,
                "other_squares",
                [square, kind((virtuals, virtuals))],
                [],
                3 * work // 2,
                after(index, crossed[0]),
                u,
                w,
            )
            crossed = across_line(after(index, p11), *crossed)
            same = pl.pallas_call(
                same_kernel(cols),
                in_specs=[SMEM] + [VMEM] * 3,
                out_specs=[VMEM] * 2,
                out_shape=half_types,
                scratch_shapes=[pltpu.VMEM((nv, virtuals, width), F32)],
                name="same",
                cost_estimate=pl.CostEstimate(flops=work // 2, bytes_accessed=2**20, transcendentals=0),
                compiler_params=pltpu.CompilerParams(vmem_limit_bytes=9 * 2**20),
            )(after(index, crossed[0]), p00, p00_rest, p11)
            same = across_core(same)
            same = across_plane(index, *same)
            crossed, *tiles = line_total(after(index, same[0]), *crossed)
            same = across_line(after(index, crossed), *same)
        else:
            crossed, same = (
                across_line(index, *across_plane(index, *across_core(plain_sums(index, amplitudes, integrals, kind_same, nv, width))))
                for kind_same in (False, True)
            )
            crossed, *tiles = line_total(index, *crossed)
        same, *tiles = line_total(index, *same, tiles)
        arrays = [crossed, same, *exchanged(tiles)]
        if not aligned:
            blocks = outcome(index, *arrays)
            return jnp.stack([jnp.stack(blocks[:2], 1), jnp.stack(blocks[2:], 1)])
        return pl.pallas_call(
            outcome_kernel,
            in_specs=[SMEM] + [VMEM] * len(arrays),
            out_specs=VMEM,
            out_shape=kind((2, rows, 2, cols)),
            name="outcome",
            compiler_params=pltpu.CompilerParams(vmem_limit_bytes=8 * 2**20),
        )(index, *arrays)

    placed = (P(None, "pair", None, "virt"), P("pair", "virt", None, None))
    return jax.shard_map(
        shards, mesh=mesh, in_specs=placed, out_specs=P(None, "pair", None, "virt"), check_vma=False
    )
```

time: 2420 us -> 103 us (0.04)
  waiting for transfers between devices: 1610 us -> 21.5 us
  blocking collectives: 672 us -> 0 us
  local copies, waits for them, and re-layouts: 68.9 us -> 0.08 us
  Pallas kernels: 0 us -> 56.8 us
  matrix products: 44.3 us -> 0 us
  starting transfers between devices: 0.04 us -> 24.5 us
    all_gather x1 -> x0, waiting for transfers between devices: 1580 us -> none  [shards(): lax.all_gather(integrals, 'pair', axis=0, tiled=True)]
    all_to_all x2 -> x0, blocking collectives: 672 us -> none  [the longest x1 621 us: shards(): lax.all_to_all(amplitudes, 'pair', split_axis=2, concat_axis=1, tiled=True)]
    pallas_call x0 -> x11, Pallas kernels: none -> 56.8 us  [the longest x1 25.9 us: crossed_sums(): pl.pallas_call(crossed_kernel(cols), in_specs=[SMEM, ANY, ANY], out_specs...]
    dot_general x1 -> x0, matrix products: 44.3 us -> none  [shards(): jnp.einsum('ikac,kcjb->iajb', regrouped, lax.all_gather(integrals, 'pair'...]
    unnamed x5 -> x0, local copies, waits for them, and re-layouts: 43.3 us -> none
    unnamed x3 -> x0, waiting for transfers between devices: 28.3 us -> none
    ppermute x0 -> x16, starting transfers between devices: none -> 24.5 us  [send(): return lax.ppermute(block, AXES, pairs)]
  transfers between devices with their start and end apart: 2 -> 16, of which waited for: 2 -> 9; matrix products, arithmetic and copies ran while one was open for 2% -> 0% of each run, Pallas kernels for 0% -> 16%
where the time goes in v3:
time: 103 us
  Pallas kernels  56.8 us (55%)
  starting transfers between devices  24.5 us (24%)
  waiting for transfers between devices  21.5 us (21%)
    pallas_call x1, Pallas kernels, crossed_sums(): pl.pallas_call(crossed_kernel(cols), in_specs=[SMEM, ANY, ANY], out_specs...  25.9 us
    ppermute x16, starting transfers between devices, send(): return lax.ppermute(block, AXES, pairs)  24.5 us
    ppermute x16, waiting for transfers between devices, send(): return lax.ppermute(block, AXES, pairs)  21.5 us
    pallas_call x2, Pallas kernels, on_chip(): pl.pallas_call(kernel, in_specs=[SMEM] + [VMEM] * (ins - 1), out_specs=[V...  15.6 us
    pallas_call x6, Pallas kernels, call(): pl.pallas_call(kernel, in_specs=[SMEM] + [VMEM] * len(arrays), out_specs=...  7.16 us
    pallas_call x1, Pallas kernels, shards(): pl.pallas_call(same_kernel(cols), in_specs=[SMEM] + [VMEM] * 3, out_specs...  6.55 us
  transfers between devices with their start and end apart: 16, of which 9 were waited for; matrix products, arithmetic and copies ran while one was open for 0% of the time, Pallas kernels for 16%

profile of v3, /device:TPU:2, one launch (start us, length us, event | category | flops | bytes accessed | tf_op | source)
XLA Modules:
  0.0 103.0 jit_solution(6412488211149725645)
XLA Ops:
  0.1 25.9 %crossed.1 = (f32[2,960,256]{2,1,0:T(8,128)S(1)}, f32[2,960,256]{2,1,0:T(8,128)S(1)}, bf16[2,14,960,240]{3,2,1,0:T(8,128)(2,1)S(1)}, bf16[53760,128]{1,0:T(8,128)(2,1)S(1)}) custom-call(s32[6]{0:T(128)S(1)} %stack.27.index.refs_0_, bf16[2,14,960,240]{3,2,1,0:T(8,128)(2,1)} %u_hbm.1, bf16[14,240,2,960]{3,2,1,0:T(2,128)(2,1)} %w_hbm.1), custom_call_target="tpu_custom_call" | custom-call | flops 12386304000 | bytes 25804800 | tf_op jit(solution)/shard_map/crossed/pallas_call | solution.py:290
  26.1 4.2 %first_square.1 = (f32[480,960]{1,0:T(8,128)S(1)}, bf16[2,14,960,240]{3,2,1,0:T(8,128)(2,1)S(1)}, bf16[53760,128]{1,0:T(8,128)(2,1)S(1)}) custom-call(s32[6]{0:T(128)S(1)} %stack.27.index.refs_0_, bf16[2,14,960,240]{3,2,1,0:T(8,128)(2,1)S(1)} %get-tuple-element.47.refs_1_, ...), custom_call_target="tpu_custom_call", output_to_operand_aliasing={{1}: (1, {}), {2}: (2, {})} | custom-call | flops 3096576000 | bytes 1048576 | tf_op jit(solution)/shard_map/first_square/pallas_call | solution.py:272
  30.3 1.3 %chip_sum.2 = (f32[4,120,256]{2,1,0:T(8,128)S(1)}, bf16[4,120,256]{2,1,0:T(8,128)(2,1)S(1)}, bf16[4,120,256]{2,1,0:T(8,128)(2,1)S(1)}, bf16[4,120,256]{2,1,0:T(8,128)(2,1)S(1)}) custom-call(s32[6]{0:T(128)S(1)} %stack.27.index.refs_0_, f32[2,4,2,120,256]{4,3,2,1,0:T(8,128)S(1)} %bitcast.12, f32[2,4,2,120,256]{4,3,2,1,0:T(8,128)S(1)} %bitcast.10), custom_call_target="tpu_custom_call" | custom-call | flops 6193152000 | bytes 1048576 | tf_op jit(solution)/shard_map/chip_sum/pallas_call | solution.py:69
  31.6 1.6 %collective-permute-start.1 = (bf16[4,120,256]{2,1,0:T(8,128)(2,1)S(1)}, bf16[4,120,256]{2,1,0:T(8,128)(2,1)S(1)}, u32[]{:S(2)}, u32[]{:S(2)}) collective-permute-start(bf16[4,120,256]{2,1,0:T(8,128)(2,1)S(1)} %get-tuple-element.58), channel_id=1, source_target_pairs={{0,4},{1,5},{2,6},{3,7},{4,0},{5,1},{6,2},{7,3},{8,12},{9,13},{10,... | collective-permute-start | bytes 737288 | tf_op jit(solution)/shard_map/ppermute | solution.py:350
  33.7 1.5 %collective-permute-start.3 = (bf16[4,120,256]{2,1,0:T(8,128)(2,1)S(1)}, bf16[4,120,256]{2,1,0:T(8,128)(2,1)S(1)}, u32[]{:S(2)}, u32[]{:S(2)}) collective-permute-start(bf16[4,120,256]{2,1,0:T(8,128)(2,1)S(1)} %get-tuple-element.60), channel_id=1, source_target_pairs={{0,6},{1,7},{2,4},{3,5},{4,2},{5,3},{6,0},{7,1},{8,14},{9,15},{10,... | collective-permute-start | bytes 737288 | tf_op jit(solution)/shard_map/ppermute | solution.py:350
  35.2 11.3 %other_squares.1 = (f32[480,960]{1,0:T(8,128)S(1)}, f32[960,960]{1,0:T(8,128)S(1)}, bf16[2,14,960,240]{3,2,1,0:T(8,128)(2,1)S(1)}, bf16[53760,128]{1,0:T(8,128)(2,1)S(1)}) custom-call(s32[6]{0:T(128)S(1)} %stack.27.index.refs_0_, bf16[2,14,960,240]{3,2,1,0:T(8,128)(2,1)S(1)} %get-tuple-element.54.refs_1_, ...), custom_call_target="tpu_custom_call", output_to_operand_aliasing={{2}: (1, {}), {3}: (2, {})} | custom-call | flops 9289728000 | bytes 1048576 | tf_op jit(solution)/shard_map/other_squares/pallas_call | solution.py:272
  46.6 1.4 %plane_sum.2 = (f32[120,256]{1,0:T(8,128)S(1)}, bf16[120,256]{1,0:T(8,128)(2,1)S(1)}, bf16[120,256]{1,0:T(8,128)(2,1)S(1)}, bf16[120,256]{1,0:T(8,128)(2,1)S(1)}) custom-call(s32[6]{0:T(128)S(1)} %stack.27.index.refs_0_, f32[4,120,256]{2,1,0:T(8,128)S(1)} %get-tuple-element.52.refs_0_, bf16[4,120,256]{2,1,0:T(8,128)(2,1)S(1)} %collective-permute-done.1.refs_1_, ...), custom_call_target="tpu_custom_call" | custom-call | flops 12386304000 | bytes 1048576 | tf_op jit(solution)/shard_map/plane_sum/pallas_call | solution.py:69
  48.0 6.6 %same.1 = (f32[2,960,256]{2,1,0:T(8,128)S(1)}, f32[2,960,256]{2,1,0:T(8,128)S(1)}) custom-call(s32[6]{0:T(128)S(1)} %stack.27.index.refs_0_, f32[480,960]{1,0:T(8,128)S(1)} %get-tuple-element.49.p00, f32[480,960]{1,0:T(8,128)S(1)} %get-tuple-element.63.p00_rest, f32[960,960]{1,0:T(8,128)S(1)} %get-tuple-element.56.p11), custom_call_target="tpu_custom_call" | custom-call | flops 3096576000 | bytes 1048576 | tf_op jit(solution)/shard_map/same/pallas_call | solution.py:483
  54.6 4.0 %collective-permute-done.4 = f32[2,960,256]{2,1,0:T(8,128)S(1)} collective-permute-done((f32[2,960,256]{2,1,0:T(8,128)S(1)}, f32[2,960,256]{2,1,0:T(8,128)S(1)}, u32[]{:S(2)}, u32[]{:S(2)}) %collective-permute-start.4) | collective-permute-done | bytes 1966112 | tf_op jit(solution)/shard_map/ppermute | solution.py:350
  59.9 1.6 %collective-permute-start.8 = (bf16[4,120,256]{2,1,0:T(8,128)(2,1)S(1)}, bf16[4,120,256]{2,1,0:T(8,128)(2,1)S(1)}, u32[]{:S(2)}, u32[]{:S(2)}) collective-permute-start(bf16[4,120,256]{2,1,0:T(8,128)(2,1)S(1)} %get-tuple-element.73), channel_id=1, source_target_pairs={{0,4},{1,5},{2,6},{3,7},{4,0},{5,1},{6,2},{7,3},{8,12},{9,13},{10,... | collective-permute-start | bytes 737288 | tf_op jit(solution)/shard_map/ppermute | solution.py:350
  62.0 1.4 %collective-permute-start.10 = (bf16[4,120,256]{2,1,0:T(8,128)(2,1)S(1)}, bf16[4,120,256]{2,1,0:T(8,128)(2,1)S(1)}, u32[]{:S(2)}, u32[]{:S(2)}) collective-permute-start(bf16[4,120,256]{2,1,0:T(8,128)(2,1)S(1)} %get-tuple-element.75), channel_id=1, source_target_pairs={{0,6},{1,7},{2,4},{3,5},{4,2},{5,3},{6,0},{7,1},{8,14},{9,15},{10,... | collective-permute-start | bytes 737288 | tf_op jit(solution)/shard_map/ppermute | solution.py:350
  63.4 1.6 %collective-permute-start.5 = (bf16[120,256]{1,0:T(8,128)(2,1)S(1)}, bf16[120,256]{1,0:T(8,128)(2,1)S(1)}, u32[]{:S(2)}, u32[]{:S(2)}) collective-permute-start(bf16[120,256]{1,0:T(8,128)(2,1)S(1)} %get-tuple-element.68), channel_id=1, source_target_pairs={{0,8},{1,9},{2,10},{3,11},{4,12},{5,13},{6,14},{7,15},{8,16},{9,17... | collective-permute-start | bytes 184328 | tf_op jit(solution)/shard_map/ppermute | solution.py:350
  65.0 2.6 %collective-permute-start.6 = (bf16[120,256]{1,0:T(8,128)(2,1)S(1)}, bf16[120,256]{1,0:T(8,128)(2,1)S(1)}, u32[]{:S(2)}, u32[]{:S(2)}) collective-permute-start(bf16[120,256]{1,0:T(8,128)(2,1)S(1)} %get-tuple-element.69), channel_id=1, source_target_pairs={{0,16},{1,17},{2,18},{3,19},{4,20},{5,21},{6,22},{7,23},{8,24},{9,... | collective-permute-start | bytes 184328 | tf_op jit(solution)/shard_map/ppermute | solution.py:350
  67.6 2.3 %collective-permute-done.5.refs_1_ = bf16[120,256]{1,0:T(8,128)(2,1)S(1)} collective-permute-done((bf16[120,256]{1,0:T(8,128)(2,1)S(1)}, bf16[120,256]{1,0:T(8,128)(2,1)S(1)}, u32[]{:S(2)}, u32[]{:S(2)}) %collective-permute-start.5) | collective-permute-done | bytes 61472 | tf_op jit(solution)/shard_map/ppermute | solution.py:350
  69.9 1.4 %collective-permute-start.7 = (bf16[120,256]{1,0:T(8,128)(2,1)S(1)}, bf16[120,256]{1,0:T(8,128)(2,1)S(1)}, u32[]{:S(2)}, u32[]{:S(2)}) collective-permute-start(bf16[120,256]{1,0:T(8,128)(2,1)S(1)} %get-tuple-element.70), channel_id=1, source_target_pairs={{0,24},{1,25},{2,26},{3,27},{4,28},{5,29},{6,30},{7,31},{8,0},{9,1... | collective-permute-start | bytes 184328 | tf_op jit(solution)/shard_map/ppermute | solution.py:350
  71.8 2.3 %collective-permute-done.7.refs_3_ = bf16[120,256]{1,0:T(8,128)(2,1)S(1)} collective-permute-done((bf16[120,256]{1,0:T(8,128)(2,1)S(1)}, bf16[120,256]{1,0:T(8,128)(2,1)S(1)}, u32[]{:S(2)}, u32[]{:S(2)}) %collective-permute-start.7) | collective-permute-done | bytes 61472 | tf_op jit(solution)/shard_map/ppermute | solution.py:350
  75.0 1.4 %plane_sum.3 = (f32[120,256]{1,0:T(8,128)S(1)}, bf16[120,256]{1,0:T(8,128)(2,1)S(1)}, bf16[120,256]{1,0:T(8,128)(2,1)S(1)}, bf16[120,256]{1,0:T(8,128)(2,1)S(1)}) custom-call(s32[6]{0:T(128)S(1)} %stack.27.index.refs_0_, f32[4,120,256]{2,1,0:T(8,128)S(1)} %get-tuple-element.66.refs_0_, bf16[4,120,256]{2,1,0:T(8,128)(2,1)S(1)} %collective-permute-done.8.refs_1_, ...), custom_call_target="tpu_custom_call" | custom-call | flops 12386304000 | bytes 1048576 | tf_op jit(solution)/shard_map/plane_sum/pallas_call | solution.py:69
  77.4 2.8 %collective-permute-start.12 = (bf16[120,256]{1,0:T(8,128)(2,1)S(1)}, bf16[120,256]{1,0:T(8,128)(2,1)S(1)}, u32[]{:S(2)}, u32[]{:S(2)}) collective-permute-start(bf16[120,256]{1,0:T(8,128)(2,1)S(1)} %get-tuple-element.78), channel_id=1, source_target_pairs={{0,16},{1,17},{2,18},{3,19},{4,20},{5,21},{6,22},{7,23},{8,24},{9,... | collective-permute-start | bytes 184328 | tf_op jit(solution)/shard_map/ppermute | solution.py:350
  81.3 1.3 %collective-permute-done.11.refs_1_ = bf16[120,256]{1,0:T(8,128)(2,1)S(1)} collective-permute-done((bf16[120,256]{1,0:T(8,128)(2,1)S(1)}, bf16[120,256]{1,0:T(8,128)(2,1)S(1)}, u32[]{:S(2)}, u32[]{:S(2)}) %collective-permute-start.11) | collective-permute-done | bytes 61472 | tf_op jit(solution)/shard_map/ppermute | solution.py:350
  85.5 2.6 %collective-permute-start.14 = (f32[2,120,120]{2,1,0:T(8,128)S(1)}, f32[2,120,120]{2,1,0:T(8,128)S(1)}, u32[]{:S(2)}, u32[]{:S(2)}) collective-permute-start(f32[2,120,120]{2,1,0:T(8,128)S(1)} %get-tuple-element.83), channel_id=1, source_target_pairs={{0,0},{1,8},{2,16},{3,24},{4,4},{5,12},{6,20},{7,28},{8,1},{9,9},{... | collective-permute-start | bytes 345608 | tf_op jit(solution)/shard_map/ppermute | solution.py:350
  88.1 4.1 %collective-permute-start.15 = (f32[2,120,120]{2,1,0:T(8,128)S(1)}, f32[2,120,120]{2,1,0:T(8,128)S(1)}, u32[]{:S(2)}, u32[]{:S(2)}) collective-permute-start(f32[2,120,120]{2,1,0:T(8,128)S(1)} %get-tuple-element.84), channel_id=1, source_target_pairs={{0,4},{1,12},{2,20},{3,28},{4,0},{5,8},{6,16},{7,24},{8,5},{9,13},... | collective-permute-start | bytes 345608 | tf_op jit(solution)/shard_map/ppermute | solution.py:350
  92.2 4.9 %collective-permute-done.14.refs_2_ = f32[2,120,120]{2,1,0:T(8,128)S(1)} collective-permute-done((f32[2,120,120]{2,1,0:T(8,128)S(1)}, f32[2,120,120]{2,1,0:T(8,128)S(1)}, u32[]{:S(2)}, u32[]{:S(2)}) %collective-permute-start.14) | collective-permute-done | bytes 115232 | tf_op jit(solution)/shard_map/ppermute | solution.py:350
  97.1 4.3 %collective-permute-done.15.refs_3_ = f32[2,120,120]{2,1,0:T(8,128)S(1)} collective-permute-done((f32[2,120,120]{2,1,0:T(8,128)S(1)}, f32[2,120,120]{2,1,0:T(8,128)S(1)}, u32[]{:S(2)}, u32[]{:S(2)}) %collective-permute-start.15) | collective-permute-done | bytes 115232 | tf_op jit(solution)/shard_map/ppermute | solution.py:350
  101.4 1.6 %outcome.1 = f32[2,120,2,240]{3,2,1,0:T(2,128)} custom-call(s32[6]{0:T(128)S(1)} %stack.27.index.refs_0_, f32[120,256]{1,0:T(8,128)S(1)} %get-tuple-element.71.refs_0_, f32[120,256]{1,0:T(8,128)S(1)} %get-tuple-element.82.refs_1_, f32[2,120,120]{2,1,0:T(8,128)S(1)} %collective-permute-done.14.refs_2_, f32[2,120,120]{2,1,0:T(8,128)S(1)} %collective-permute-done.15.refs_3_), custom_call_target="tpu_custom_call" | custom-call | tf_op jit(solution)/shard_map/outcome/pallas_call | solution.py:508
  (20 shorter events, 8.9 us)
Async XLA Ops:
  26.0 4.3 %collective-permute-start = (f32[2,960,256]{2,1,0:T(8,128)S(1)}, f32[2,960,256]{2,1,0:T(8,128)S(1)}, u32[]{:S(2)}, u32[]{:S(2)}) collective-permute-start(f32[2,960,256]{2,1,0:T(8,128)S(1)} %get-tuple-element.51), channel_id=1, source_target_pairs={{0,1},{1,0},{2,3},{3,2},{4,5},{5,4},{6,7},{7,6},{8,9},{9,8},{10,11... | collective-permute-start | bytes 5898248 | tf_op jit(solution)/shard_map/ppermute | solution.py:350
  31.6 14.9 %collective-permute-start.1 = (bf16[4,120,256]{2,1,0:T(8,128)(2,1)S(1)}, bf16[4,120,256]{2,1,0:T(8,128)(2,1)S(1)}, u32[]{:S(2)}, u32[]{:S(2)}) collective-permute-start(bf16[4,120,256]{2,1,0:T(8,128)(2,1)S(1)} %get-tuple-element.58), channel_id=1, source_target_pairs={{0,4},{1,5},{2,6},{3,7},{4,0},{5,1},{6,2},{7,3},{8,12},{9,13},{10,... | collective-permute-start | bytes 737288 | tf_op jit(solution)/shard_map/ppermute | solution.py:350
  33.2 13.3 %collective-permute-start.2 = (bf16[4,120,256]{2,1,0:T(8,128)(2,1)S(1)}, bf16[4,120,256]{2,1,0:T(8,128)(2,1)S(1)}, u32[]{:S(2)}, u32[]{:S(2)}) collective-permute-start(bf16[4,120,256]{2,1,0:T(8,128)(2,1)S(1)} %get-tuple-element.59), channel_id=1, source_target_pairs={{0,2},{1,3},{2,0},{3,1},{4,6},{5,7},{6,4},{7,5},{8,10},{9,11},{10,... | collective-permute-start | bytes 737288 | tf_op jit(solution)/shard_map/ppermute | solution.py:350
  33.7 12.8 %collective-permute-start.3 = (bf16[4,120,256]{2,1,0:T(8,128)(2,1)S(1)}, bf16[4,120,256]{2,1,0:T(8,128)(2,1)S(1)}, u32[]{:S(2)}, u32[]{:S(2)}) collective-permute-start(bf16[4,120,256]{2,1,0:T(8,128)(2,1)S(1)} %get-tuple-element.60), channel_id=1, source_target_pairs={{0,6},{1,7},{2,4},{3,5},{4,2},{5,3},{6,0},{7,1},{8,14},{9,15},{10,... | collective-permute-start | bytes 737288 | tf_op jit(solution)/shard_map/ppermute | solution.py:350
  54.5 4.0 %collective-permute-start.4 = (f32[2,960,256]{2,1,0:T(8,128)S(1)}, f32[2,960,256]{2,1,0:T(8,128)S(1)}, u32[]{:S(2)}, u32[]{:S(2)}) collective-permute-start(f32[2,960,256]{2,1,0:T(8,128)S(1)} %get-tuple-element.65), channel_id=1, source_target_pairs={{0,1},{1,0},{2,3},{3,2},{4,5},{5,4},{6,7},{7,6},{8,9},{9,8},{10,11... | collective-permute-start | bytes 5898248 | tf_op jit(solution)/shard_map/ppermute | solution.py:350
  59.9 15.1 %collective-permute-start.8 = (bf16[4,120,256]{2,1,0:T(8,128)(2,1)S(1)}, bf16[4,120,256]{2,1,0:T(8,128)(2,1)S(1)}, u32[]{:S(2)}, u32[]{:S(2)}) collective-permute-start(bf16[4,120,256]{2,1,0:T(8,128)(2,1)S(1)} %get-tuple-element.73), channel_id=1, source_target_pairs={{0,4},{1,5},{2,6},{3,7},{4,0},{5,1},{6,2},{7,3},{8,12},{9,13},{10,... | collective-permute-start | bytes 737288 | tf_op jit(solution)/shard_map/ppermute | solution.py:350
  61.4 13.5 %collective-permute-start.9 = (bf16[4,120,256]{2,1,0:T(8,128)(2,1)S(1)}, bf16[4,120,256]{2,1,0:T(8,128)(2,1)S(1)}, u32[]{:S(2)}, u32[]{:S(2)}) collective-permute-start(bf16[4,120,256]{2,1,0:T(8,128)(2,1)S(1)} %get-tuple-element.74), channel_id=1, source_target_pairs={{0,2},{1,3},{2,0},{3,1},{4,6},{5,7},{6,4},{7,5},{8,10},{9,11},{10,... | collective-permute-start | bytes 737288 | tf_op jit(solution)/shard_map/ppermute | solution.py:350
  62.0 13.0 %collective-permute-start.10 = (bf16[4,120,256]{2,1,0:T(8,128)(2,1)S(1)}, bf16[4,120,256]{2,1,0:T(8,128)(2,1)S(1)}, u32[]{:S(2)}, u32[]{:S(2)}) collective-permute-start(bf16[4,120,256]{2,1,0:T(8,128)(2,1)S(1)} %get-tuple-element.75), channel_id=1, source_target_pairs={{0,6},{1,7},{2,4},{3,5},{4,2},{5,3},{6,0},{7,1},{8,14},{9,15},{10,... | collective-permute-start | bytes 737288 | tf_op jit(solution)/shard_map/ppermute | solution.py:350
  63.4 6.5 %collective-permute-start.5 = (bf16[120,256]{1,0:T(8,128)(2,1)S(1)}, bf16[120,256]{1,0:T(8,128)(2,1)S(1)}, u32[]{:S(2)}, u32[]{:S(2)}) collective-permute-start(bf16[120,256]{1,0:T(8,128)(2,1)S(1)} %get-tuple-element.68), channel_id=1, source_target_pairs={{0,8},{1,9},{2,10},{3,11},{4,12},{5,13},{6,14},{7,15},{8,16},{9,17... | collective-permute-start | bytes 184328 | tf_op jit(solution)/shard_map/ppermute | solution.py:350
  65.0 6.8 %collective-permute-start.6 = (bf16[120,256]{1,0:T(8,128)(2,1)S(1)}, bf16[120,256]{1,0:T(8,128)(2,1)S(1)}, u32[]{:S(2)}, u32[]{:S(2)}) collective-permute-start(bf16[120,256]{1,0:T(8,128)(2,1)S(1)} %get-tuple-element.69), channel_id=1, source_target_pairs={{0,16},{1,17},{2,18},{3,19},{4,20},{5,21},{6,22},{7,23},{8,24},{9,... | collective-permute-start | bytes 184328 | tf_op jit(solution)/shard_map/ppermute | solution.py:350
  69.9 4.2 %collective-permute-start.7 = (bf16[120,256]{1,0:T(8,128)(2,1)S(1)}, bf16[120,256]{1,0:T(8,128)(2,1)S(1)}, u32[]{:S(2)}, u32[]{:S(2)}) collective-permute-start(bf16[120,256]{1,0:T(8,128)(2,1)S(1)} %get-tuple-element.70), channel_id=1, source_target_pairs={{0,24},{1,25},{2,26},{3,27},{4,28},{5,29},{6,30},{7,31},{8,0},{9,1... | collective-permute-start | bytes 184328 | tf_op jit(solution)/shard_map/ppermute | solution.py:350
  76.4 6.3 %collective-permute-start.11 = (bf16[120,256]{1,0:T(8,128)(2,1)S(1)}, bf16[120,256]{1,0:T(8,128)(2,1)S(1)}, u32[]{:S(2)}, u32[]{:S(2)}) collective-permute-start(bf16[120,256]{1,0:T(8,128)(2,1)S(1)} %get-tuple-element.77), channel_id=1, source_target_pairs={{0,8},{1,9},{2,10},{3,11},{4,12},{5,13},{6,14},{7,15},{8,16},{9,17... | collective-permute-start | bytes 184328 | tf_op jit(solution)/shard_map/ppermute | solution.py:350
  77.4 6.5 %collective-permute-start.12 = (bf16[120,256]{1,0:T(8,128)(2,1)S(1)}, bf16[120,256]{1,0:T(8,128)(2,1)S(1)}, u32[]{:S(2)}, u32[]{:S(2)}) collective-permute-start(bf16[120,256]{1,0:T(8,128)(2,1)S(1)} %get-tuple-element.78), channel_id=1, source_target_pairs={{0,16},{1,17},{2,18},{3,19},{4,20},{5,21},{6,22},{7,23},{8,24},{9,... | collective-permute-start | bytes 184328 | tf_op jit(solution)/shard_map/ppermute | solution.py:350
  80.2 4.4 %collective-permute-start.13 = (bf16[120,256]{1,0:T(8,128)(2,1)S(1)}, bf16[120,256]{1,0:T(8,128)(2,1)S(1)}, u32[]{:S(2)}, u32[]{:S(2)}) collective-permute-start(bf16[120,256]{1,0:T(8,128)(2,1)S(1)} %get-tuple-element.79), channel_id=1, source_target_pairs={{0,24},{1,25},{2,26},{3,27},{4,28},{5,29},{6,30},{7,31},{8,0},{9,1... | collective-permute-start | bytes 184328 | tf_op jit(solution)/shard_map/ppermute | solution.py:350
  85.5 11.6 %collective-permute-start.14 = (f32[2,120,120]{2,1,0:T(8,128)S(1)}, f32[2,120,120]{2,1,0:T(8,128)S(1)}, u32[]{:S(2)}, u32[]{:S(2)}) collective-permute-start(f32[2,120,120]{2,1,0:T(8,128)S(1)} %get-tuple-element.83), channel_id=1, source_target_pairs={{0,0},{1,8},{2,16},{3,24},{4,4},{5,12},{6,20},{7,28},{8,1},{9,9},{... | collective-permute-start | bytes 345608 | tf_op jit(solution)/shard_map/ppermute | solution.py:350
  88.1 13.3 %collective-permute-start.15 = (f32[2,120,120]{2,1,0:T(8,128)S(1)}, f32[2,120,120]{2,1,0:T(8,128)S(1)}, u32[]{:S(2)}, u32[]{:S(2)}) collective-permute-start(f32[2,120,120]{2,1,0:T(8,128)S(1)} %get-tuple-element.84), channel_id=1, source_target_pairs={{0,4},{1,12},{2,20},{3,28},{4,0},{5,8},{6,16},{7,24},{8,5},{9,13},... | collective-permute-start | bytes 345608 | tf_op jit(solution)/shard_map/ppermute | solution.py:350

commit v4 on v3

--- a/solution.py
+++ b/solution.py
@@ -73,7 +73,7 @@
             out_shape=out_types,
             name=name,
             cost_estimate=pl.CostEstimate(flops=cost, bytes_accessed=2**20, transcendentals=0),
-            compiler_params=pltpu.CompilerParams(vmem_limit_bytes=4 * 2**20),
+            compiler_params=pltpu.CompilerParams(vmem_limit_bytes=2 * 2**20),
         )(index, *arrays)
 
     return call
@@ -87,10 +87,10 @@
     return min(LANES, virtuals - LANES * tile)
 
 
-def product(u, w, i, j, rows, n):
+def product(u, w, i, j, rows, n, ks=None):
     _, depth, virtuals, inner = u.shape
     total = None
-    for k in range(depth):
+    for k in ks or range(depth):
         parts = [
             w[pl.ds((t * depth + k) * 2 * inner + j, inner, 2), :][:, : lanes(t, virtuals)]
             for t in (2 * n, 2 * n + 1)
@@ -102,47 +102,6 @@
 
 def pair_of_tiles(n, virtuals):
     return slice(2 * LANES * n, min(2 * LANES * (n + 1), virtuals))
-
-
-def brought(u_hbm, w_hbm, u, w, sems):
-    _, depth, virtuals, inner = u_hbm.shape
-    tiles = lane_tiles(virtuals)
-    w_rows = w_hbm.reshape(depth * inner * 2, virtuals)
-
-    def u_copies(i):
-        return [pltpu.make_async_copy(u_hbm.at[i, k], u.at[i, k], sems.at[i, k]) for k in range(depth)]
-
-    def tile_rows(tile):
-        return pl.ds(tile * depth * inner * 2, depth * inner * 2)
-
-    def w_copy(tile):
-        source = w_rows.at[:, pl.ds(LANES * tile, LANES)]
-        return pltpu.make_async_copy(source, w.at[tile_rows(tile)], sems.at[2, tile])
-
-    def last_tile(block):
-        w[tile_rows(tiles - 1), :] = block.reshape(depth * inner * 2, LANES)[...]
-
-    groups = [
-        u_copies(1) + [w_copy(tile) for tile in range(2)],
-        [w_copy(tile) for tile in range(2, tiles - 1)],
-        u_copies(0),
-    ]
-
-    def start(group):
-        for copy in groups[group]:
-            copy.start()
-
-    def wait(group):
-        for copy in groups[group]:
-            copy.wait()
-
-    start(0)
-    pltpu.emit_pipeline(
-        last_tile,
-        grid=(1,),
-        in_specs=[pl.BlockSpec((depth, inner, 2, LANES), lambda _: (0, 0, 0, tiles - 1))],
-    )(w_hbm)
-    return start, wait
 
 
 class Half:
@@ -172,29 +131,59 @@
 
 
 def crossed_kernel(cols):
-    def kernel(index, u_hbm, w_hbm, kept, sent, u, w, other, own, out, sems):
-        virtuals = u.shape[2]
-        tiles = lane_tiles(virtuals)
-        start, wait = brought(u_hbm, w_hbm, u, w, sems)
+    def kernel(index, u_hbm, w_hbm, kept, sent, u, w, other, own, out, ring, u_sems, w_sems):
+        _, depth, virtuals, inner = u.shape
+        tiles, slots = lane_tiles(virtuals), ring.shape[0]
+        everything, pairs = slice(0, virtuals), tiles // 2
         half = Half(out, 0, cols)
-        everything = slice(0, virtuals)
-        wait(0)
-        start(1)
-        other[:, pair_of_tiles(0, virtuals)] = product(u, w, 1, 0, everything, 0)
-        wait(1)
-        start(2)
-        for n in range(1, tiles // 2):
-            other[:, pair_of_tiles(n, virtuals)] = product(u, w, 1, 0, everything, n)
-        wait(2)
-        v = 0
-        for n in range(tiles // 2):
+
+        def u_copy(i, k):
+            return pltpu.make_async_copy(u_hbm.at[i, k], u.at[i, k], u_sems.at[i, k])
+
+        def w_copy(k):
+            source = w_hbm.at[k].reshape(2 * inner, virtuals)
+            return pltpu.make_async_copy(source, ring.at[k % slots], w_sems.at[k])
+
+        def take(k):
+            w_copy(k).wait()
+            for t in range(tiles):
+                rows = slice((t * depth + k) * 2 * inner, (t * depth + k + 1) * 2 * inner)
+                width = lanes(t, virtuals)
+                w[rows, :width] = ring[k % slots, :, LANES * t : LANES * t + width]
+            if k + slots < depth:
+                w_copy(k + slots).start()
+
+        cuts = [0, 2 * depth // 7, 9 * depth // 14, depth]
+        parts = [range(*cuts[n : n + 2]) for n in range(3)]
+        for k in range(slots):
+            w_copy(k).start()
+        for k in parts[0]:
+            u_copy(1, k).start()
+        for number, ks in enumerate(parts):
+            for k in ks:
+                take(k)
+            for k in ks:
+                u_copy(1, k).wait()
+            for k in parts[number + 1] if number < 2 else range(depth):
+                u_copy(1 if number < 2 else 0, k).start()
+            for n in range(pairs):
+                term = product(u, w, 1, 0, everything, n, ks)
+                columns = pair_of_tiles(n, virtuals)
+                other[:, columns] = term if number == 0 else other[:, columns] + term
+        for k in range(depth):
+            u_copy(0, k).wait()
+        v, wide = 0, 2 * LANES
+        for n in range(pairs):
             columns = pair_of_tiles(n, virtuals)
-            own[:, columns] = product(u, w, 0, 1, everything, n)
+            if n:
+                own[:, :wide] = own[:, wide:]
+            own[:, wide : wide + columns.stop - columns.start] = product(u, w, 0, 1, everything, n)
             while (v + 1) * cols <= columns.stop:
                 on, past = v * cols, (v + 1) * cols
+                shift = wide - columns.start
                 for t in range(tiles):
                     r0, r1 = LANES * t, LANES * t + lanes(t, virtuals)
-                    half.place(v, r0, r1, own[r0:r1, on:past] + other[on:past, r0:r1].T)
+                    half.place(v, r0, r1, own[r0:r1, on + shift : past + shift] + other[on:past, r0:r1].T)
                 v += 1
         half.finish(index, kept, sent)
 
@@ -207,78 +196,89 @@
         square[:, pair_of_tiles(n, virtuals)] = product(u, w, 0, 0, slice(0, virtuals // 2), n)
 
 
-def other_squares_kernel(index, u, w, rest, square):
-    virtuals = u.shape[2]
-    for n in range(lane_tiles(virtuals) // 2):
-        rest[:, pair_of_tiles(n, virtuals)] = product(u, w, 0, 0, slice(virtuals // 2, virtuals), n)
-        square[:, pair_of_tiles(n, virtuals)] = product(u, w, 1, 1, slice(0, virtuals), n)
+class Triangles:
+    def __init__(self, half, p00, p00_rest, p11, virtuals):
+        self.half, self.p00, self.p00_rest, self.p11, self.virtuals = half, p00, p00_rest, p11, virtuals
+
+    def rows_of(self, i, r0, r1, c0, c1):
+        middle = self.virtuals // 2
+        if i == 1:
+            return self.p11[r0:r1, c0:c1]
+        if r1 <= middle:
+            return self.p00[r0:r1, c0:c1]
+        if r0 >= middle:
+            return self.p00_rest[r0 - middle : r1 - middle, c0:c1]
+        return jnp.concatenate([self.p00[r0:middle, c0:c1], self.p00_rest[0 : r1 - middle, c0:c1]], axis=0)
+
+    def place(self, v, tile, above):
+        half, cols = self.half, self.half.cols
+        begin, end = LANES * tile, LANES * tile + lanes(tile, self.virtuals)
+        on, past = v * cols, (v + 1) * cols
+        flips = {}
+
+        def symmetric(i, r0, r1):
+            if i not in flips:
+                flips[i] = self.rows_of(i, on, past, begin, end).T
+            return self.rows_of(i, r0, r1, on, past) + flips[i][r0 - begin : r1 - begin]
+
+        r0, r1 = begin, min(end, on)
+        if above and r0 < r1:
+            half.place(v, r0, r1, symmetric(0, r0, r1))
+        r0, r1 = max(begin, on), min(end, past)
+        if not above and r0 < r1:
+            s00, s11 = symmetric(0, r0, r1), symmetric(1, r0, r1)
+            a, b = r0 + iota(s00.shape, 0), on + iota(s00.shape, 1)
+            half.place(v, r0, r1, jnp.where(a <= b, s00, s11))
+            diagonal = jnp.where(a == b, s11, 0.0)
+            half.out[v, r0:r1, cols : cols + 1] = jnp.sum(diagonal, axis=1, keepdims=True)
+            half.largest = jnp.maximum(half.largest, jnp.max(jnp.abs(diagonal), axis=0, keepdims=True))
+        r0, r1 = max(begin, past), end
+        if not above and r0 < r1:
+            half.place(v, r0, r1, symmetric(1, r0, r1))
+
+
+def other_squares_kernel(cols):
+    def kernel(index, u, w, p00, p00_rest, p11, out, largest):
+        virtuals = u.shape[2]
+        tiles, nv = lane_tiles(virtuals), virtuals // cols
+        half = Half(out, 0, cols)
+        triangles = Triangles(half, p00, p00_rest, p11, virtuals)
+        for n in range(tiles // 2):
+            p00_rest[:, pair_of_tiles(n, virtuals)] = product(u, w, 0, 0, slice(virtuals // 2, virtuals), n)
+        for n in range(tiles // 2):
+            p11[:, pair_of_tiles(n, virtuals)] = product(u, w, 1, 1, slice(0, virtuals), n)
+            for v in range(n, nv, tiles // 2):
+                for t in range(tiles):
+                    triangles.place(v, t, True)
+        largest[...] = half.largest
+
+    return kernel
 
 
 def same_kernel(cols):
-    def kernel(index, p00, p00_rest, p11, kept, sent, out):
+    def kernel(index, out, p00, p00_rest, p11, largest, kept, sent, _):
         virtuals = p11.shape[0]
-        middle, tiles, nv = virtuals // 2, lane_tiles(virtuals), virtuals // cols
         half = Half(out, 0, cols)
-
-        def rows_of(i, r0, r1, c0, c1):
-            if i == 1:
-                return p11[r0:r1, c0:c1]
-            if r1 <= middle:
-                return p00[r0:r1, c0:c1]
-            if r0 >= middle:
-                return p00_rest[r0 - middle : r1 - middle, c0:c1]
-            return jnp.concatenate([p00[r0:middle, c0:c1], p00_rest[0 : r1 - middle, c0:c1]], axis=0)
-
-        def segment(v, tile):
-            begin, end = LANES * tile, LANES * tile + lanes(tile, virtuals)
-            on, past = v * cols, (v + 1) * cols
-            flips = {}
-
-            def symmetric(i, r0, r1):
-                if i not in flips:
-                    flips[i] = rows_of(i, on, past, begin, end).T
-                return rows_of(i, r0, r1, on, past) + flips[i][r0 - begin : r1 - begin]
-
-            r0, r1 = begin, min(end, on)
-            if r0 < r1:
-                half.place(v, r0, r1, symmetric(0, r0, r1))
-            r0, r1 = max(begin, on), min(end, past)
-            if r0 < r1:
-                s00, s11 = symmetric(0, r0, r1), symmetric(1, r0, r1)
-                a, b = r0 + iota(s00.shape, 0), on + iota(s00.shape, 1)
-                half.place(v, r0, r1, jnp.where(a <= b, s00, s11))
-                diagonal = jnp.where(a == b, s11, 0.0)
-                out[v, r0:r1, cols : cols + 1] = jnp.sum(diagonal, axis=1, keepdims=True)
-                half.largest = jnp.maximum(half.largest, jnp.max(jnp.abs(diagonal), axis=0, keepdims=True))
-            r0, r1 = max(begin, past), end
-            if r0 < r1:
-                half.place(v, r0, r1, symmetric(1, r0, r1))
-
-        for v in range(nv):
-            for t in range(tiles):
-                segment(v, t)
+        half.largest = largest[...]
+        triangles = Triangles(half, p00, p00_rest, p11, virtuals)
+        for v in range(virtuals // cols):
+            for t in range(lane_tiles(virtuals)):
+                triangles.place(v, t, False)
         half.finish(index, kept, sent)
 
     return kernel
 
 
 def on_chip(body, name, out_shape, scratch, flops, index, u, w, *arrays):
-    ins = 3 + len(arrays)
-    outs = ins + len(out_shape)
-
-    def kernel(*refs):
-        body(*refs[:outs], *refs[outs + 2 :])
-
-    *results, u, w = pl.pallas_call(
-        kernel,
-        in_specs=[SMEM] + [VMEM] * (ins - 1),
-        out_specs=[VMEM] * (len(out_shape) + 2),
-        out_shape=[*out_shape, jax.ShapeDtypeStruct(u.shape, u.dtype), jax.ShapeDtypeStruct(w.shape, w.dtype)],
-        input_output_aliases={1: len(out_shape), 2: len(out_shape) + 1},
+    results = pl.pallas_call(
+        body,
+        in_specs=[SMEM] + [VMEM] * (2 + len(arrays)),
+        out_specs=[VMEM] * len(out_shape),
+        out_shape=out_shape,
         scratch_shapes=[pltpu.VMEM(shape, F32) for shape in scratch],
         name=name,
         cost_estimate=pl.CostEstimate(flops=flops, bytes_accessed=2**20, transcendentals=0),
-        compiler_params=pltpu.CompilerParams(vmem_limit_bytes=5 * 2**20),
+        compiler_params=pltpu.CompilerParams(vmem_limit_bytes=3 * 2**20),
     )(index, u, w, *arrays)
     return results, u, w
 
@@ -298,15 +298,17 @@
         ],
         scratch_shapes=[
             pltpu.VMEM((virtuals, virtuals), F32),
-            pltpu.VMEM((virtuals, virtuals), F32),
+            pltpu.VMEM((virtuals, 4 * LANES), F32),
             pltpu.VMEM((nv, virtuals, width), F32),
-            pltpu.SemaphoreType.DMA((3, max(depth, tiles))),
+            pltpu.VMEM((min(5, depth), 2 * inner, virtuals), BF16),
+            pltpu.SemaphoreType.DMA((2, depth)),
+            pltpu.SemaphoreType.DMA((depth,)),
         ],
         name="crossed",
         cost_estimate=pl.CostEstimate(
             flops=4 * depth * inner * virtuals * virtuals, bytes_accessed=4 * amplitudes.size, transcendentals=0
         ),
-        compiler_params=pltpu.CompilerParams(vmem_limit_bytes=20 * 2**20),
+        compiler_params=pltpu.CompilerParams(vmem_limit_bytes=18 * 2**20),
     )(index, amplitudes, integrals)
     return (kept, sent), u, w
 
@@ -357,7 +359,7 @@
         aligned = rows % 8 == 0 and inner % 16 == 0 and virtuals % 64 == 0
         p, v = lax.axis_index("pair"), lax.axis_index("virt")
         index = jnp.stack([v // 2, v % 2, p // 2, p % 2, p, v]).astype(jnp.int32)
-        steps = [(dx, dy) for dx in range(nx) for dy in range(2) if dx or dy]
+        steps = [(dx, dy) for dx in range(nx - 1, -1, -1) for dy in (1, 0) if dx or dy]
 
         def chip_sum(index, kept, came):
             x, y = index[0], index[3]
@@ -384,23 +386,30 @@
                     total = total + decoded(array[z], of)
                 return total
 
-            results = [block(z_own)]
+            results = [with_bound(block(z_own), bound, at)]
             for dz in range(1, nz):
                 results.append(with_bound(coded(block((z_own + dz) % nz), bound), bound, at))
             return results
 
+        tile_width = -(-(rows + 1) // LANES) * LANES
+
         def line_sum(count, paired):
             def body(index, own, *arrays):
                 total = own[...]
+                bound = bound_at(total, at)
                 for array in arrays[:count]:
                     array = array[...]
                     total = total + decoded(array, bound_at(array, at))
+                    bound = bound + bound_at(array, at)
+                bound = sent_bound(bound)
                 flipped = [total[:, h * rows : (h + 1) * rows].T for h in range(ratio)]
                 results = [total]
                 for t in range(ratio):
                     tile = flipped[0]
                     for h in range(1, ratio):
                         tile = jnp.where((index[4] + t) % ratio == h, flipped[h], tile)
+                    tile = coded(tile, bound)
+                    tile = jnp.concatenate([tile, jnp.broadcast_to(bound, (rows, tile_width - rows))], axis=1)
                     results.append([arrays[count + t][...], tile] if paired else tile)
                 return results
 
@@ -410,10 +419,10 @@
             def mirrored(which):
                 parts = []
                 for h in range(ratio):
-                    part = came[0][which]
+                    part = came[0][which].astype(F32)
                     for t in range(1, ratio):
-                        part = jnp.where((index[4] + ratio - h) % ratio == t, came[t][which], part)
-                    parts.append(part)
+                        part = jnp.where((index[4] + ratio - h) % ratio == t, came[t][which].astype(F32), part)
+                    parts.append(decoded(part[:, :rows], bound_at(part, rows)))
                 return jnp.concatenate(parts, axis=1) if ratio > 1 else parts[0]
 
             same = same[...]
@@ -450,8 +459,8 @@
             return own, [send(block, lambda p, v: ((p + 2 * dz) % np_, v)) for dz, block in zip(range(1, nz), outs)]
 
         def line_total(index, own, came, first_tiles=()):
-            shape = (2, rows, rows) if first_tiles else (rows, rows)
-            types = [kind((rows, width))] + [kind(shape)] * ratio
+            shape = (2, rows, tile_width) if first_tiles else (rows, tile_width)
+            types = [kind((rows, width))] + [kind(shape, BF16)] * ratio
             body = line_sum(len(came), bool(first_tiles))
             return local(body, types, aligned, "line_sum")(index, own, *came, *first_tiles)
 
@@ -469,29 +478,31 @@
                 first_square_kernel, "first_square", [square], [], work // 2, after(index, crossed[0]), u, w
             )
             crossed = across_plane(after(index, p00), *crossed)
-            (p00_rest, p11), u, w = on_chip(
-                other_squares_kernel,
+            placed = kind((nv, virtuals, width))
+            (p00_rest, p11, out, largest), u, w = on_chip(
+                other_squares_kernel(cols),
                 "other_squares",
-                [square, kind((virtuals, virtuals))],
+                [square, kind((virtuals, virtuals)), placed, kind((1, cols))],
                 [],
                 3 * work // 2,
                 after(index, crossed[0]),
                 u,
                 w,
+                p00,
             )
-            crossed = across_line(after(index, p11), *crossed)
-            same = pl.pallas_call(
+            *same, _ = pl.pallas_call(
                 same_kernel(cols),
-                in_specs=[SMEM] + [VMEM] * 3,
-                out_specs=[VMEM] * 2,
-                out_shape=half_types,
-                scratch_shapes=[pltpu.VMEM((nv, virtuals, width), F32)],
+                in_specs=[SMEM] + [VMEM] * 5,
+                out_specs=[VMEM] * 3,
+                out_shape=[*half_types, placed],
+                input_output_aliases={1: 2},
                 name="same",
                 cost_estimate=pl.CostEstimate(flops=work // 2, bytes_accessed=2**20, transcendentals=0),
-                compiler_params=pltpu.CompilerParams(vmem_limit_bytes=9 * 2**20),
-            )(after(index, crossed[0]), p00, p00_rest, p11)
+                compiler_params=pltpu.CompilerParams(vmem_limit_bytes=3 * 2**20),
+            )(after(index, p11, *crossed[1]), out, p00, p00_rest, p11, largest)
+            crossed = across_line(after(index, same[0]), *crossed)
             same = across_core(same)
-            same = across_plane(index, *same)
+            same = across_plane(after(index, crossed[0]), *same)
             crossed, *tiles = line_total(after(index, same[0]), *crossed)
             same = across_line(after(index, crossed), *same)
         else:

time: 103 us -> 93.6 us (0.909)
  waiting for transfers between devices: 21.5 us -> 16 us
  Pallas kernels: 56.8 us -> 51.5 us
    ppermute x16, waiting for transfers between devices: 21.5 us -> 16 us  [send(): return lax.ppermute(block, AXES, pairs)]
    pallas_call x1, Pallas kernels: 25.9 us -> 22.1 us  [crossed_sums(): pl.pallas_call(crossed_kernel(cols), in_specs=[SMEM, ANY, ANY], out_specs...]
    pallas_call x3, Pallas kernels: 22.1 us -> 20.5 us  [the longest x2 15.7 us: on_chip(): pl.pallas_call(body, in_specs=[SMEM] + [VMEM] * (2 + len(arrays)), out_sp...]
  transfers between devices with their start and end apart: 16 -> 16, of which waited for: 9 -> 9; matrix products, arithmetic and copies ran while one was open for 0% -> 0% of each run, Pallas kernels for 16% -> 19%
where the time goes in v4:
time: 93.6 us; the launch traced here: 92.8 us
  Pallas kernels  51.5 us (55%)
  starting transfers between devices  24.4 us (26%)
  waiting for transfers between devices  16 us (17%)
    ppermute x16, starting transfers between devices, send(): return lax.ppermute(block, AXES, pairs)  24.4 us
    pallas_call x1, Pallas kernels, crossed_sums(): pl.pallas_call(crossed_kernel(cols), in_specs=[SMEM, ANY, ANY], out_specs...  22.1 us
    ppermute x16, waiting for transfers between devices, send(): return lax.ppermute(block, AXES, pairs)  16 us
    pallas_call x2, Pallas kernels, on_chip(): pl.pallas_call(body, in_specs=[SMEM] + [VMEM] * (2 + len(arrays)), out_sp...  15.7 us
    pallas_call x6, Pallas kernels, call(): pl.pallas_call(kernel, in_specs=[SMEM] + [VMEM] * len(arrays), out_specs=...  7.21 us
    pallas_call x1, Pallas kernels, shards(): pl.pallas_call(same_kernel(cols), in_specs=[SMEM] + [VMEM] * 5, out_specs...  4.81 us
  transfers between devices with their start and end apart: 16, of which 9 were waited for; matrix products, arithmetic and copies ran while one was open for 0% of the time, Pallas kernels for 19%

profile of v4, /device:TPU:2, one launch (start us, length us, event | category | flops | bytes accessed | tf_op | source)
XLA Modules:
  0.0 92.8 jit_solution(6736694908495756709)
XLA Ops:
  0.1 22.1 %crossed.1 = (f32[2,960,256]{2,1,0:T(8,128)S(1)}, f32[2,960,256]{2,1,0:T(8,128)S(1)}, bf16[2,14,960,240]{3,2,1,0:T(8,128)(2,1)S(1)}, bf16[53760,128]{1,0:T(8,128)(2,1)S(1)}) custom-call(s32[6]{0:T(128)S(1)} %stack.27.index, bf16[2,14,960,240]{3,2,1,0:T(8,128)(2,1)} %u_hbm.1, bf16[14,240,2,960]{3,2,1,0:T(2,128)(2,1)} %w_hbm.1), custom_call_target="tpu_custom_call" | custom-call | flops 12386304000 | bytes 25804800 | tf_op jit(solution)/shard_map/crossed/pallas_call | solution.py:290
  22.3 4.2 %first_square.1.p00 = f32[480,960]{1,0:T(8,128)S(1)} custom-call(s32[6]{0:T(128)S(1)} %stack.27.index, bf16[2,14,960,240]{3,2,1,0:T(8,128)(2,1)S(1)} %get-tuple-element.47.u, bf16[53760,128]{1,0:T(8,128)(2,1)S(1)} %get-tuple-element.48.w), custom_call_target="tpu_custom_call" | custom-call | flops 3096576000 | bytes 1048576 | tf_op jit(solution)/shard_map/first_square/pallas_call | solution.py:273
  28.5 1.6 %collective-permute-start.1 = (bf16[4,120,256]{2,1,0:T(8,128)(2,1)S(1)}, bf16[4,120,256]{2,1,0:T(8,128)(2,1)S(1)}, u32[]{:S(2)}, u32[]{:S(2)}) collective-permute-start(bf16[4,120,256]{2,1,0:T(8,128)(2,1)S(1)} %get-tuple-element.54), channel_id=1, source_target_pairs={{0,6},{1,7},{2,4},{3,5},{4,2},{5,3},{6,0},{7,1},{8,14},{9,15},{10,... | collective-permute-start | bytes 737288 | tf_op jit(solution)/shard_map/ppermute | solution.py:352
  30.0 1.5 %collective-permute-start.2 = (bf16[4,120,256]{2,1,0:T(8,128)(2,1)S(1)}, bf16[4,120,256]{2,1,0:T(8,128)(2,1)S(1)}, u32[]{:S(2)}, u32[]{:S(2)}) collective-permute-start(bf16[4,120,256]{2,1,0:T(8,128)(2,1)S(1)} %get-tuple-element.55), channel_id=1, source_target_pairs={{0,2},{1,3},{2,0},{3,1},{4,6},{5,7},{6,4},{7,5},{8,10},{9,11},{10,... | collective-permute-start | bytes 737288 | tf_op jit(solution)/shard_map/ppermute | solution.py:352
  32.1 11.4 %other_squares.1 = (f32[480,960]{1,0:T(8,128)S(1)}, f32[960,960]{1,0:T(8,128)S(1)}, f32[4,960,256]{2,1,0:T(8,128)S(1)}, f32[1,240]{1,0:T(1,128)S(1)}) custom-call(s32[6]{0:T(128)S(1)} %stack.27.index, bf16[2,14,960,240]{3,2,1,0:T(8,128)(2,1)S(1)} %get-tuple-element.47.u, bf16[53760,128]{1,0:T(8,128)(2,1)S(1)} %copy-done.1, f32[480,960]{1,0:T(8,128)S(1)} %first_square.1.p00), custom_call_target="tpu_custom_call" | custom-call | flops 9289728000 | bytes 1048576 | tf_op jit(solution)/shard_map/other_squares/pallas_call | solution.py:273
  43.6 4.8 %same.1 = (f32[2,960,256]{2,1,0:T(8,128)S(1)}, f32[2,960,256]{2,1,0:T(8,128)S(1)}, f32[4,960,256]{2,1,0:T(8,128)S(1)}) custom-call(s32[6]{0:T(128)S(1)} %stack.27.index, f32[4,960,256]{2,1,0:T(8,128)S(1)} %get-tuple-element.58.out, f32[480,960]{1,0:T(8,128)S(1)} %first_square.1.p00, ...), custom_call_target="tpu_custom_call", output_to_operand_aliasing={{2}: (1, {})} | custom-call | flops 3096576000 | bytes 1048576 | tf_op jit(solution)/shard_map/same/pallas_call | solution.py:493
  48.5 1.4 %plane_sum.2 = (f32[120,256]{1,0:T(8,128)S(1)}, bf16[120,256]{1,0:T(8,128)(2,1)S(1)}, bf16[120,256]{1,0:T(8,128)(2,1)S(1)}, bf16[120,256]{1,0:T(8,128)(2,1)S(1)}) custom-call(s32[6]{0:T(128)S(1)} %stack.27.index, f32[4,120,256]{2,1,0:T(8,128)S(1)} %get-tuple-element.51.refs_0_, bf16[4,120,256]{2,1,0:T(8,128)(2,1)S(1)} %collective-permute-done.1.refs_1_, ...), custom_call_target="tpu_custom_call" | custom-call | flops 12386304000 | bytes 1048576 | tf_op jit(solution)/shard_map/plane_sum/pallas_call | solution.py:69
  50.0 2.5 %collective-permute-done.4 = f32[2,960,256]{2,1,0:T(8,128)S(1)} collective-permute-done((f32[2,960,256]{2,1,0:T(8,128)S(1)}, f32[2,960,256]{2,1,0:T(8,128)S(1)}, u32[]{:S(2)}, u32[]{:S(2)}) %collective-permute-start.4) | collective-permute-done | bytes 1966112 | tf_op jit(solution)/shard_map/ppermute | solution.py:352
  53.7 1.6 %collective-permute-start.8 = (bf16[4,120,256]{2,1,0:T(8,128)(2,1)S(1)}, bf16[4,120,256]{2,1,0:T(8,128)(2,1)S(1)}, u32[]{:S(2)}, u32[]{:S(2)}) collective-permute-start(bf16[4,120,256]{2,1,0:T(8,128)(2,1)S(1)} %get-tuple-element.73), channel_id=1, source_target_pairs={{0,6},{1,7},{2,4},{3,5},{4,2},{5,3},{6,0},{7,1},{8,14},{9,15},{10,... | collective-permute-start | bytes 737288 | tf_op jit(solution)/shard_map/ppermute | solution.py:352
  55.3 1.5 %collective-permute-start.9 = (bf16[4,120,256]{2,1,0:T(8,128)(2,1)S(1)}, bf16[4,120,256]{2,1,0:T(8,128)(2,1)S(1)}, u32[]{:S(2)}, u32[]{:S(2)}) collective-permute-start(bf16[4,120,256]{2,1,0:T(8,128)(2,1)S(1)} %get-tuple-element.74), channel_id=1, source_target_pairs={{0,2},{1,3},{2,0},{3,1},{4,6},{5,7},{6,4},{7,5},{8,10},{9,11},{10,... | collective-permute-start | bytes 737288 | tf_op jit(solution)/shard_map/ppermute | solution.py:352
  57.3 1.6 %collective-permute-start.5 = (bf16[120,256]{1,0:T(8,128)(2,1)S(1)}, bf16[120,256]{1,0:T(8,128)(2,1)S(1)}, u32[]{:S(2)}, u32[]{:S(2)}) collective-permute-start(bf16[120,256]{1,0:T(8,128)(2,1)S(1)} %get-tuple-element.68), channel_id=1, source_target_pairs={{0,8},{1,9},{2,10},{3,11},{4,12},{5,13},{6,14},{7,15},{8,16},{9,17... | collective-permute-start | bytes 184328 | tf_op jit(solution)/shard_map/ppermute | solution.py:352
  58.8 2.6 %collective-permute-start.6 = (bf16[120,256]{1,0:T(8,128)(2,1)S(1)}, bf16[120,256]{1,0:T(8,128)(2,1)S(1)}, u32[]{:S(2)}, u32[]{:S(2)}) collective-permute-start(bf16[120,256]{1,0:T(8,128)(2,1)S(1)} %get-tuple-element.69), channel_id=1, source_target_pairs={{0,16},{1,17},{2,18},{3,19},{4,20},{5,21},{6,22},{7,23},{8,24},{9,... | collective-permute-start | bytes 184328 | tf_op jit(solution)/shard_map/ppermute | solution.py:352
  61.4 2.3 %collective-permute-done.5.refs_1_ = bf16[120,256]{1,0:T(8,128)(2,1)S(1)} collective-permute-done((bf16[120,256]{1,0:T(8,128)(2,1)S(1)}, bf16[120,256]{1,0:T(8,128)(2,1)S(1)}, u32[]{:S(2)}, u32[]{:S(2)}) %collective-permute-start.5) | collective-permute-done | bytes 61472 | tf_op jit(solution)/shard_map/ppermute | solution.py:352
  63.7 1.4 %collective-permute-start.7 = (bf16[120,256]{1,0:T(8,128)(2,1)S(1)}, bf16[120,256]{1,0:T(8,128)(2,1)S(1)}, u32[]{:S(2)}, u32[]{:S(2)}) collective-permute-start(bf16[120,256]{1,0:T(8,128)(2,1)S(1)} %get-tuple-element.70), channel_id=1, source_target_pairs={{0,24},{1,25},{2,26},{3,27},{4,28},{5,29},{6,30},{7,31},{8,0},{9,1... | collective-permute-start | bytes 184328 | tf_op jit(solution)/shard_map/ppermute | solution.py:352
  65.6 2.3 %collective-permute-done.7.refs_3_ = bf16[120,256]{1,0:T(8,128)(2,1)S(1)} collective-permute-done((bf16[120,256]{1,0:T(8,128)(2,1)S(1)}, bf16[120,256]{1,0:T(8,128)(2,1)S(1)}, u32[]{:S(2)}, u32[]{:S(2)}) %collective-permute-start.7) | collective-permute-done | bytes 61472 | tf_op jit(solution)/shard_map/ppermute | solution.py:352
  68.9 1.4 %plane_sum.3 = (f32[120,256]{1,0:T(8,128)S(1)}, bf16[120,256]{1,0:T(8,128)(2,1)S(1)}, bf16[120,256]{1,0:T(8,128)(2,1)S(1)}, bf16[120,256]{1,0:T(8,128)(2,1)S(1)}) custom-call(s32[6]{0:T(128)S(1)} %stack.27.index, f32[4,120,256]{2,1,0:T(8,128)S(1)} %get-tuple-element.66.refs_0_, bf16[4,120,256]{2,1,0:T(8,128)(2,1)S(1)} %collective-permute-done.8.refs_1_, ...), custom_call_target="tpu_custom_call" | custom-call | flops 12386304000 | bytes 1048576 | tf_op jit(solution)/shard_map/plane_sum/pallas_call | solution.py:69
  71.1 3.0 %collective-permute-start.12 = (bf16[120,256]{1,0:T(8,128)(2,1)S(1)}, bf16[120,256]{1,0:T(8,128)(2,1)S(1)}, u32[]{:S(2)}, u32[]{:S(2)}) collective-permute-start(bf16[120,256]{1,0:T(8,128)(2,1)S(1)} %get-tuple-element.78), channel_id=1, source_target_pairs={{0,16},{1,17},{2,18},{3,19},{4,20},{5,21},{6,22},{7,23},{8,24},{9,... | collective-permute-start | bytes 184328 | tf_op jit(solution)/shard_map/ppermute | solution.py:352
  75.0 1.9 %collective-permute-done.11.refs_1_ = bf16[120,256]{1,0:T(8,128)(2,1)S(1)} collective-permute-done((bf16[120,256]{1,0:T(8,128)(2,1)S(1)}, bf16[120,256]{1,0:T(8,128)(2,1)S(1)}, u32[]{:S(2)}, u32[]{:S(2)}) %collective-permute-start.11) | collective-permute-done | bytes 61472 | tf_op jit(solution)/shard_map/ppermute | solution.py:352
  77.0 1.6 %collective-permute-done.12.refs_2_ = bf16[120,256]{1,0:T(8,128)(2,1)S(1)} collective-permute-done((bf16[120,256]{1,0:T(8,128)(2,1)S(1)}, bf16[120,256]{1,0:T(8,128)(2,1)S(1)}, u32[]{:S(2)}, u32[]{:S(2)}) %collective-permute-start.12) | collective-permute-done | bytes 61472 | tf_op jit(solution)/shard_map/ppermute | solution.py:352
  79.6 2.4 %collective-permute-start.14 = (bf16[2,120,128]{2,1,0:T(8,128)(2,1)S(1)}, bf16[2,120,128]{2,1,0:T(8,128)(2,1)S(1)}, u32[]{:S(2)}, u32[]{:S(2)}) collective-permute-start(bf16[2,120,128]{2,1,0:T(8,128)(2,1)S(1)} %get-tuple-element.83), channel_id=1, source_target_pairs={{0,0},{1,8},{2,16},{3,24},{4,4},{5,12},{6,20},{7,28},{8,1},{9,9},{... | collective-permute-start | bytes 184328 | tf_op jit(solution)/shard_map/ppermute | solution.py:352
  82.0 4.3 %collective-permute-start.15 = (bf16[2,120,128]{2,1,0:T(8,128)(2,1)S(1)}, bf16[2,120,128]{2,1,0:T(8,128)(2,1)S(1)}, u32[]{:S(2)}, u32[]{:S(2)}) collective-permute-start(bf16[2,120,128]{2,1,0:T(8,128)(2,1)S(1)} %get-tuple-element.84), channel_id=1, source_target_pairs={{0,4},{1,12},{2,20},{3,28},{4,0},{5,8},{6,16},{7,24},{8,5},{9,13},... | collective-permute-start | bytes 184328 | tf_op jit(solution)/shard_map/ppermute | solution.py:352
  86.3 2.6 %collective-permute-done.14.refs_2_ = bf16[2,120,128]{2,1,0:T(8,128)(2,1)S(1)} collective-permute-done((bf16[2,120,128]{2,1,0:T(8,128)(2,1)S(1)}, bf16[2,120,128]{2,1,0:T(8,128)(2,1)S(1)}, u32[]{:S(2)}, u32[]{:S(2)}) %collective-permute-start.14) | collective-permute-done | bytes 61472 | tf_op jit(solution)/shard_map/ppermute | solution.py:352
  88.9 2.2 %collective-permute-done.15.refs_3_ = bf16[2,120,128]{2,1,0:T(8,128)(2,1)S(1)} collective-permute-done((bf16[2,120,128]{2,1,0:T(8,128)(2,1)S(1)}, bf16[2,120,128]{2,1,0:T(8,128)(2,1)S(1)}, u32[]{:S(2)}, u32[]{:S(2)}) %collective-permute-start.15) | collective-permute-done | bytes 61472 | tf_op jit(solution)/shard_map/ppermute | solution.py:352
  91.1 1.7 %outcome.1 = f32[2,120,2,240]{3,2,1,0:T(2,128)} custom-call(s32[6]{0:T(128)S(1)} %stack.27.index, f32[120,256]{1,0:T(8,128)S(1)} %get-tuple-element.71.refs_0_, f32[120,256]{1,0:T(8,128)S(1)} %get-tuple-element.82.refs_1_, bf16[2,120,128]{2,1,0:T(8,128)(2,1)S(1)} %collective-permute-done.14.refs_2_, bf16[2,120,128]{2,1,0:T(8,128)(2,1)S(1)} %collective-permute-done.15.refs_3_), custom_call_target="tpu_custom_call" | custom-call | tf_op jit(solution)/shard_map/outcome/pallas_call | solution.py:519
  (24 shorter events, 8.8 us)
Async XLA Ops:
  22.2 4.9 %copy-start = (bf16[53760,128]{1,0:T(8,128)(2,1)}, bf16[53760,128]{1,0:T(8,128)(2,1)S(1)}, u32[]{:S(2)}) copy-start(bf16[53760,128]{1,0:T(8,128)(2,1)S(1)} %get-tuple-element.48.w) | copy-start | bytes 41287684
  22.2 4.9 %collective-permute-start = (f32[2,960,256]{2,1,0:T(8,128)S(1)}, f32[2,960,256]{2,1,0:T(8,128)S(1)}, u32[]{:S(2)}, u32[]{:S(2)}) collective-permute-start(f32[2,960,256]{2,1,0:T(8,128)S(1)} %get-tuple-element.50), channel_id=1, source_target_pairs={{0,1},{1,0},{2,3},{3,2},{4,5},{5,4},{6,7},{7,6},{8,9},{9,8},{10,11... | collective-permute-start | bytes 5898248 | tf_op jit(solution)/shard_map/ppermute | solution.py:352
  27.2 4.9 %copy-start.1 = (bf16[53760,128]{1,0:T(8,128)(2,1)S(1)}, bf16[53760,128]{1,0:T(8,128)(2,1)}, u32[]{:S(2)}) copy-start(bf16[53760,128]{1,0:T(8,128)(2,1)} %copy-done) | copy-start | bytes 41287684
  28.5 15.1 %collective-permute-start.1 = (bf16[4,120,256]{2,1,0:T(8,128)(2,1)S(1)}, bf16[4,120,256]{2,1,0:T(8,128)(2,1)S(1)}, u32[]{:S(2)}, u32[]{:S(2)}) collective-permute-start(bf16[4,120,256]{2,1,0:T(8,128)(2,1)S(1)} %get-tuple-element.54), channel_id=1, source_target_pairs={{0,6},{1,7},{2,4},{3,5},{4,2},{5,3},{6,0},{7,1},{8,14},{9,15},{10,... | collective-permute-start | bytes 737288 | tf_op jit(solution)/shard_map/ppermute | solution.py:352
  30.0 13.5 %collective-permute-start.2 = (bf16[4,120,256]{2,1,0:T(8,128)(2,1)S(1)}, bf16[4,120,256]{2,1,0:T(8,128)(2,1)S(1)}, u32[]{:S(2)}, u32[]{:S(2)}) collective-permute-start(bf16[4,120,256]{2,1,0:T(8,128)(2,1)S(1)} %get-tuple-element.55), channel_id=1, source_target_pairs={{0,2},{1,3},{2,0},{3,1},{4,6},{5,7},{6,4},{7,5},{8,10},{9,11},{10,... | collective-permute-start | bytes 737288 | tf_op jit(solution)/shard_map/ppermute | solution.py:352
  31.5 12.0 %collective-permute-start.3 = (bf16[4,120,256]{2,1,0:T(8,128)(2,1)S(1)}, bf16[4,120,256]{2,1,0:T(8,128)(2,1)S(1)}, u32[]{:S(2)}, u32[]{:S(2)}) collective-permute-start(bf16[4,120,256]{2,1,0:T(8,128)(2,1)S(1)} %get-tuple-element.56), channel_id=1, source_target_pairs={{0,4},{1,5},{2,6},{3,7},{4,0},{5,1},{6,2},{7,3},{8,12},{9,13},{10,... | collective-permute-start | bytes 737288 | tf_op jit(solution)/shard_map/ppermute | solution.py:352
  48.4 4.0 %collective-permute-start.4 = (f32[2,960,256]{2,1,0:T(8,128)S(1)}, f32[2,960,256]{2,1,0:T(8,128)S(1)}, u32[]{:S(2)}, u32[]{:S(2)}) collective-permute-start(f32[2,960,256]{2,1,0:T(8,128)S(1)} %get-tuple-element.65), channel_id=1, source_target_pairs={{0,1},{1,0},{2,3},{3,2},{4,5},{5,4},{6,7},{7,6},{8,9},{9,8},{10,11... | collective-permute-start | bytes 5898248 | tf_op jit(solution)/shard_map/ppermute | solution.py:352
  53.7 15.2 %collective-permute-start.8 = (bf16[4,120,256]{2,1,0:T(8,128)(2,1)S(1)}, bf16[4,120,256]{2,1,0:T(8,128)(2,1)S(1)}, u32[]{:S(2)}, u32[]{:S(2)}) collective-permute-start(bf16[4,120,256]{2,1,0:T(8,128)(2,1)S(1)} %get-tuple-element.73), channel_id=1, source_target_pairs={{0,6},{1,7},{2,4},{3,5},{4,2},{5,3},{6,0},{7,1},{8,14},{9,15},{10,... | collective-permute-start | bytes 737288 | tf_op jit(solution)/shard_map/ppermute | solution.py:352
  55.3 13.6 %collective-permute-start.9 = (bf16[4,120,256]{2,1,0:T(8,128)(2,1)S(1)}, bf16[4,120,256]{2,1,0:T(8,128)(2,1)S(1)}, u32[]{:S(2)}, u32[]{:S(2)}) collective-permute-start(bf16[4,120,256]{2,1,0:T(8,128)(2,1)S(1)} %get-tuple-element.74), channel_id=1, source_target_pairs={{0,2},{1,3},{2,0},{3,1},{4,6},{5,7},{6,4},{7,5},{8,10},{9,11},{10,... | collective-permute-start | bytes 737288 | tf_op jit(solution)/shard_map/ppermute | solution.py:352
  56.8 12.1 %collective-permute-start.10 = (bf16[4,120,256]{2,1,0:T(8,128)(2,1)S(1)}, bf16[4,120,256]{2,1,0:T(8,128)(2,1)S(1)}, u32[]{:S(2)}, u32[]{:S(2)}) collective-permute-start(bf16[4,120,256]{2,1,0:T(8,128)(2,1)S(1)} %get-tuple-element.75), channel_id=1, source_target_pairs={{0,4},{1,5},{2,6},{3,7},{4,0},{5,1},{6,2},{7,3},{8,12},{9,13},{10,... | collective-permute-start | bytes 737288 | tf_op jit(solution)/shard_map/ppermute | solution.py:352
  57.3 6.5 %collective-permute-start.5 = (bf16[120,256]{1,0:T(8,128)(2,1)S(1)}, bf16[120,256]{1,0:T(8,128)(2,1)S(1)}, u32[]{:S(2)}, u32[]{:S(2)}) collective-permute-start(bf16[120,256]{1,0:T(8,128)(2,1)S(1)} %get-tuple-element.68), channel_id=1, source_target_pairs={{0,8},{1,9},{2,10},{3,11},{4,12},{5,13},{6,14},{7,15},{8,16},{9,17... | collective-permute-start | bytes 184328 | tf_op jit(solution)/shard_map/ppermute | solution.py:352
  58.8 6.8 %collective-permute-start.6 = (bf16[120,256]{1,0:T(8,128)(2,1)S(1)}, bf16[120,256]{1,0:T(8,128)(2,1)S(1)}, u32[]{:S(2)}, u32[]{:S(2)}) collective-permute-start(bf16[120,256]{1,0:T(8,128)(2,1)S(1)} %get-tuple-element.69), channel_id=1, source_target_pairs={{0,16},{1,17},{2,18},{3,19},{4,20},{5,21},{6,22},{7,23},{8,24},{9,... | collective-permute-start | bytes 184328 | tf_op jit(solution)/shard_map/ppermute | solution.py:352
  63.7 4.2 %collective-permute-start.7 = (bf16[120,256]{1,0:T(8,128)(2,1)S(1)}, bf16[120,256]{1,0:T(8,128)(2,1)S(1)}, u32[]{:S(2)}, u32[]{:S(2)}) collective-permute-start(bf16[120,256]{1,0:T(8,128)(2,1)S(1)} %get-tuple-element.70), channel_id=1, source_target_pairs={{0,24},{1,25},{2,26},{3,27},{4,28},{5,29},{6,30},{7,31},{8,0},{9,1... | collective-permute-start | bytes 184328 | tf_op jit(solution)/shard_map/ppermute | solution.py:352
  70.3 6.7 %collective-permute-start.11 = (bf16[120,256]{1,0:T(8,128)(2,1)S(1)}, bf16[120,256]{1,0:T(8,128)(2,1)S(1)}, u32[]{:S(2)}, u32[]{:S(2)}) collective-permute-start(bf16[120,256]{1,0:T(8,128)(2,1)S(1)} %get-tuple-element.77), channel_id=1, source_target_pairs={{0,8},{1,9},{2,10},{3,11},{4,12},{5,13},{6,14},{7,15},{8,16},{9,17... | collective-permute-start | bytes 184328 | tf_op jit(solution)/shard_map/ppermute | solution.py:352
  71.1 7.4 %collective-permute-start.12 = (bf16[120,256]{1,0:T(8,128)(2,1)S(1)}, bf16[120,256]{1,0:T(8,128)(2,1)S(1)}, u32[]{:S(2)}, u32[]{:S(2)}) collective-permute-start(bf16[120,256]{1,0:T(8,128)(2,1)S(1)} %get-tuple-element.78), channel_id=1, source_target_pairs={{0,16},{1,17},{2,18},{3,19},{4,20},{5,21},{6,22},{7,23},{8,24},{9,... | collective-permute-start | bytes 184328 | tf_op jit(solution)/shard_map/ppermute | solution.py:352
  74.1 4.6 %collective-permute-start.13 = (bf16[120,256]{1,0:T(8,128)(2,1)S(1)}, bf16[120,256]{1,0:T(8,128)(2,1)S(1)}, u32[]{:S(2)}, u32[]{:S(2)}) collective-permute-start(bf16[120,256]{1,0:T(8,128)(2,1)S(1)} %get-tuple-element.79), channel_id=1, source_target_pairs={{0,24},{1,25},{2,26},{3,27},{4,28},{5,29},{6,30},{7,31},{8,0},{9,1... | collective-permute-start | bytes 184328 | tf_op jit(solution)/shard_map/ppermute | solution.py:352
  79.6 9.3 %collective-permute-start.14 = (bf16[2,120,128]{2,1,0:T(8,128)(2,1)S(1)}, bf16[2,120,128]{2,1,0:T(8,128)(2,1)S(1)}, u32[]{:S(2)}, u32[]{:S(2)}) collective-permute-start(bf16[2,120,128]{2,1,0:T(8,128)(2,1)S(1)} %get-tuple-element.83), channel_id=1, source_target_pairs={{0,0},{1,8},{2,16},{3,24},{4,4},{5,12},{6,20},{7,28},{8,1},{9,9},{... | collective-permute-start | bytes 184328 | tf_op jit(solution)/shard_map/ppermute | solution.py:352
  82.0 9.1 %collective-permute-start.15 = (bf16[2,120,128]{2,1,0:T(8,128)(2,1)S(1)}, bf16[2,120,128]{2,1,0:T(8,128)(2,1)S(1)}, u32[]{:S(2)}, u32[]{:S(2)}) collective-permute-start(bf16[2,120,128]{2,1,0:T(8,128)(2,1)S(1)} %get-tuple-element.84), channel_id=1, source_target_pairs={{0,4},{1,12},{2,20},{3,28},{4,0},{5,8},{6,16},{7,24},{8,5},{9,13},... | collective-permute-start | bytes 184328 | tf_op jit(solution)/shard_map/ppermute | solution.py:352

commit v5 on v4

--- a/solution.py
+++ b/solution.py
@@ -210,6 +210,9 @@
             return self.p00_rest[r0 - middle : r1 - middle, c0:c1]
         return jnp.concatenate([self.p00[r0:middle, c0:c1], self.p00_rest[0 : r1 - middle, c0:c1]], axis=0)
 
+    def ready(self, v, tile):
+        return max(-(-(v + 1) * self.half.cols // (2 * LANES)) - 1, tile // 2)
+
     def place(self, v, tile, above):
         half, cols = self.half, self.half.cols
         begin, end = LANES * tile, LANES * tile + lanes(tile, self.virtuals)
@@ -250,6 +253,10 @@
             for v in range(n, nv, tiles // 2):
                 for t in range(tiles):
                     triangles.place(v, t, True)
+            for v in range(nv):
+                for t in range(tiles):
+                    if n == triangles.ready(v, t) < tiles // 2 - 1:
+                        triangles.place(v, t, False)
         largest[...] = half.largest
 
     return kernel
@@ -261,9 +268,11 @@
         half = Half(out, 0, cols)
         half.largest = largest[...]
         triangles = Triangles(half, p00, p00_rest, p11, virtuals)
+        tiles = lane_tiles(virtuals)
         for v in range(virtuals // cols):
-            for t in range(lane_tiles(virtuals)):
-                triangles.place(v, t, False)
+            for t in range(tiles):
+                if triangles.ready(v, t) == tiles // 2 - 1:
+                    triangles.place(v, t, False)
         half.finish(index, kept, sent)
 
     return kernel
@@ -388,7 +397,7 @@
 
             results = [with_bound(block(z_own), bound, at)]
             for dz in range(1, nz):
-                results.append(with_bound(coded(block((z_own + dz) % nz), bound), bound, at))
+                results.append(with_bound(coded(block(z_own ^ dz), bound), bound, at))
             return results
 
         tile_width = -(-(rows + 1) // LANES) * LANES
@@ -456,7 +465,7 @@
         def across_line(index, own, came):
             types = [kind((rows, width))] + [kind((rows, width), BF16)] * (nz - 1)
             own, *outs = local(plane_sum, types, aligned, "plane_sum", 2 * work)(index, own, *came)
-            return own, [send(block, lambda p, v: ((p + 2 * dz) % np_, v)) for dz, block in zip(range(1, nz), outs)]
+            return own, [send(block, lambda p, v: (p ^ 2 * dz, v)) for dz, block in zip(range(1, nz), outs)]
 
         def line_total(index, own, came, first_tiles=()):
             shape = (2, rows, tile_width) if first_tiles else (rows, tile_width)

time: 93.6 us -> 91.8 us (0.981)
  Pallas kernels: 51.5 us -> 49.8 us
  waiting for transfers between devices: 16 us -> 14.3 us
  starting transfers between devices: 24.4 us -> 25.8 us
    pallas_call x1, Pallas kernels: 4.81 us -> 2.46 us  [shards(): pl.pallas_call(same_kernel(cols), in_specs=[SMEM] + [VMEM] * 5, out_specs...]
    ppermute x16, waiting for transfers between devices: 16 us -> 14.3 us  [send(): return lax.ppermute(block, AXES, pairs)]
    ppermute x16, starting transfers between devices: 24.4 us -> 25.8 us  [send(): return lax.ppermute(block, AXES, pairs)]
  transfers between devices with their start and end apart: 16 -> 16, of which waited for: 9 -> 9; matrix products, arithmetic and copies ran while one was open for 0% -> 0% of each run, Pallas kernels for 19% -> 21%
where the time goes in v5:
time: 91.8 us; the launch traced here: 90.8 us
  Pallas kernels  49.8 us (54%)
  starting transfers between devices  25.8 us (28%)
  waiting for transfers between devices  14.3 us (16%)
    ppermute x16, starting transfers between devices, send(): return lax.ppermute(block, AXES, pairs)  25.8 us
    pallas_call x1, Pallas kernels, crossed_sums(): pl.pallas_call(crossed_kernel(cols), in_specs=[SMEM, ANY, ANY], out_specs...  22.1 us
    pallas_call x2, Pallas kernels, on_chip(): pl.pallas_call(body, in_specs=[SMEM] + [VMEM] * (2 + len(arrays)), out_sp...  16.3 us
    ppermute x16, waiting for transfers between devices, send(): return lax.ppermute(block, AXES, pairs)  14.3 us
    pallas_call x6, Pallas kernels, call(): pl.pallas_call(kernel, in_specs=[SMEM] + [VMEM] * len(arrays), out_specs=...  7.21 us
    pallas_call x1, Pallas kernels, shards(): pl.pallas_call(same_kernel(cols), in_specs=[SMEM] + [VMEM] * 5, out_specs...  2.46 us
  transfers between devices with their start and end apart: 16, of which 9 were waited for; matrix products, arithmetic and copies ran while one was open for 0% of the time, Pallas kernels for 21%

profile of v5, /device:TPU:2, one launch (start us, length us, event | category | flops | bytes accessed | tf_op | source)
XLA Modules:
  0.0 90.8 jit_solution(16038983091616402854)
XLA Ops:
  0.1 22.1 %crossed.1 = (f32[2,960,256]{2,1,0:T(8,128)S(1)}, f32[2,960,256]{2,1,0:T(8,128)S(1)}, bf16[2,14,960,240]{3,2,1,0:T(8,128)(2,1)S(1)}, bf16[53760,128]{1,0:T(8,128)(2,1)S(1)}) custom-call(s32[6]{0:T(128)S(1)} %stack.27.index, bf16[2,14,960,240]{3,2,1,0:T(8,128)(2,1)} %u_hbm.1, bf16[14,240,2,960]{3,2,1,0:T(2,128)(2,1)} %w_hbm.1), custom_call_target="tpu_custom_call" | custom-call | flops 12386304000 | bytes 25804800 | tf_op jit(solution)/shard_map/crossed/pallas_call | solution.py:299
  22.3 4.2 %first_square.1.p00 = f32[480,960]{1,0:T(8,128)S(1)} custom-call(s32[6]{0:T(128)S(1)} %stack.27.index, bf16[2,14,960,240]{3,2,1,0:T(8,128)(2,1)S(1)} %get-tuple-element.47.u, bf16[53760,128]{1,0:T(8,128)(2,1)S(1)} %get-tuple-element.48.w), custom_call_target="tpu_custom_call" | custom-call | flops 3096576000 | bytes 1048576 | tf_op jit(solution)/shard_map/first_square/pallas_call | solution.py:282
  27.2 1.3 %chip_sum.2 = (f32[4,120,256]{2,1,0:T(8,128)S(1)}, bf16[4,120,256]{2,1,0:T(8,128)(2,1)S(1)}, bf16[4,120,256]{2,1,0:T(8,128)(2,1)S(1)}, bf16[4,120,256]{2,1,0:T(8,128)(2,1)S(1)}) custom-call(s32[6]{0:T(128)S(1)} %stack.27.index, f32[2,4,2,120,256]{4,3,2,1,0:T(8,128)S(1)} %bitcast.13, f32[2,4,2,120,256]{4,3,2,1,0:T(8,128)S(1)} %bitcast.12), custom_call_target="tpu_custom_call" | custom-call | flops 6193152000 | bytes 1048576 | tf_op jit(solution)/shard_map/chip_sum/pallas_call | solution.py:69
  28.5 1.6 %collective-permute-start.1 = (bf16[4,120,256]{2,1,0:T(8,128)(2,1)S(1)}, bf16[4,120,256]{2,1,0:T(8,128)(2,1)S(1)}, u32[]{:S(2)}, u32[]{:S(2)}) collective-permute-start(bf16[4,120,256]{2,1,0:T(8,128)(2,1)S(1)} %get-tuple-element.54), channel_id=1, source_target_pairs={{0,6},{1,7},{2,4},{3,5},{4,2},{5,3},{6,0},{7,1},{8,14},{9,15},{10,... | collective-permute-start | bytes 737288 | tf_op jit(solution)/shard_map/ppermute | solution.py:361
  30.0 1.5 %collective-permute-start.2 = (bf16[4,120,256]{2,1,0:T(8,128)(2,1)S(1)}, bf16[4,120,256]{2,1,0:T(8,128)(2,1)S(1)}, u32[]{:S(2)}, u32[]{:S(2)}) collective-permute-start(bf16[4,120,256]{2,1,0:T(8,128)(2,1)S(1)} %get-tuple-element.55), channel_id=1, source_target_pairs={{0,2},{1,3},{2,0},{3,1},{4,6},{5,7},{6,4},{7,5},{8,10},{9,11},{10,... | collective-permute-start | bytes 737288 | tf_op jit(solution)/shard_map/ppermute | solution.py:361
  32.1 12.1 %other_squares.1 = (f32[480,960]{1,0:T(8,128)S(1)}, f32[960,960]{1,0:T(8,128)S(1)}, f32[4,960,256]{2,1,0:T(8,128)S(1)}, f32[1,240]{1,0:T(1,128)S(1)}) custom-call(s32[6]{0:T(128)S(1)} %stack.27.index, bf16[2,14,960,240]{3,2,1,0:T(8,128)(2,1)S(1)} %get-tuple-element.47.u, bf16[53760,128]{1,0:T(8,128)(2,1)S(1)} %copy-done.1, f32[480,960]{1,0:T(8,128)S(1)} %first_square.1.p00), custom_call_target="tpu_custom_call" | custom-call | flops 9289728000 | bytes 1048576 | tf_op jit(solution)/shard_map/other_squares/pallas_call | solution.py:282
  44.2 2.5 %same.1 = (f32[2,960,256]{2,1,0:T(8,128)S(1)}, f32[2,960,256]{2,1,0:T(8,128)S(1)}, f32[4,960,256]{2,1,0:T(8,128)S(1)}) custom-call(s32[6]{0:T(128)S(1)} %stack.27.index, f32[4,960,256]{2,1,0:T(8,128)S(1)} %get-tuple-element.58.out, f32[480,960]{1,0:T(8,128)S(1)} %first_square.1.p00, ...), custom_call_target="tpu_custom_call", output_to_operand_aliasing={{2}: (1, {})} | custom-call | flops 3096576000 | bytes 1048576 | tf_op jit(solution)/shard_map/same/pallas_call | solution.py:502
  46.8 1.4 %plane_sum.2 = (f32[120,256]{1,0:T(8,128)S(1)}, bf16[120,256]{1,0:T(8,128)(2,1)S(1)}, bf16[120,256]{1,0:T(8,128)(2,1)S(1)}, bf16[120,256]{1,0:T(8,128)(2,1)S(1)}) custom-call(s32[6]{0:T(128)S(1)} %stack.27.index, f32[4,120,256]{2,1,0:T(8,128)S(1)} %get-tuple-element.51.refs_0_, bf16[4,120,256]{2,1,0:T(8,128)(2,1)S(1)} %collective-permute-done.1.refs_1_, ...), custom_call_target="tpu_custom_call" | custom-call | flops 12386304000 | bytes 1048576 | tf_op jit(solution)/shard_map/plane_sum/pallas_call | solution.py:69
  48.3 2.5 %collective-permute-done.4 = f32[2,960,256]{2,1,0:T(8,128)S(1)} collective-permute-done((f32[2,960,256]{2,1,0:T(8,128)S(1)}, f32[2,960,256]{2,1,0:T(8,128)S(1)}, u32[]{:S(2)}, u32[]{:S(2)}) %collective-permute-start.4) | collective-permute-done | bytes 1966112 | tf_op jit(solution)/shard_map/ppermute | solution.py:361
  52.0 1.6 %collective-permute-start.8 = (bf16[4,120,256]{2,1,0:T(8,128)(2,1)S(1)}, bf16[4,120,256]{2,1,0:T(8,128)(2,1)S(1)}, u32[]{:S(2)}, u32[]{:S(2)}) collective-permute-start(bf16[4,120,256]{2,1,0:T(8,128)(2,1)S(1)} %get-tuple-element.73), channel_id=1, source_target_pairs={{0,6},{1,7},{2,4},{3,5},{4,2},{5,3},{6,0},{7,1},{8,14},{9,15},{10,... | collective-permute-start | bytes 737288 | tf_op jit(solution)/shard_map/ppermute | solution.py:361
  53.6 1.5 %collective-permute-start.9 = (bf16[4,120,256]{2,1,0:T(8,128)(2,1)S(1)}, bf16[4,120,256]{2,1,0:T(8,128)(2,1)S(1)}, u32[]{:S(2)}, u32[]{:S(2)}) collective-permute-start(bf16[4,120,256]{2,1,0:T(8,128)(2,1)S(1)} %get-tuple-element.74), channel_id=1, source_target_pairs={{0,2},{1,3},{2,0},{3,1},{4,6},{5,7},{6,4},{7,5},{8,10},{9,11},{10,... | collective-permute-start | bytes 737288 | tf_op jit(solution)/shard_map/ppermute | solution.py:361
  55.6 1.6 %collective-permute-start.5 = (bf16[120,256]{1,0:T(8,128)(2,1)S(1)}, bf16[120,256]{1,0:T(8,128)(2,1)S(1)}, u32[]{:S(2)}, u32[]{:S(2)}) collective-permute-start(bf16[120,256]{1,0:T(8,128)(2,1)S(1)} %get-tuple-element.68), channel_id=1, source_target_pairs={{0,8},{1,9},{2,10},{3,11},{4,12},{5,13},{6,14},{7,15},{8,0},{9,1},... | collective-permute-start | bytes 184328 | tf_op jit(solution)/shard_map/ppermute | solution.py:361
  57.1 2.6 %collective-permute-start.6 = (bf16[120,256]{1,0:T(8,128)(2,1)S(1)}, bf16[120,256]{1,0:T(8,128)(2,1)S(1)}, u32[]{:S(2)}, u32[]{:S(2)}) collective-permute-start(bf16[120,256]{1,0:T(8,128)(2,1)S(1)} %get-tuple-element.69), channel_id=1, source_target_pairs={{0,16},{1,17},{2,18},{3,19},{4,20},{5,21},{6,22},{7,23},{8,24},{9,... | collective-permute-start | bytes 184328 | tf_op jit(solution)/shard_map/ppermute | solution.py:361
  60.4 3.1 %collective-permute-start.7 = (bf16[120,256]{1,0:T(8,128)(2,1)S(1)}, bf16[120,256]{1,0:T(8,128)(2,1)S(1)}, u32[]{:S(2)}, u32[]{:S(2)}) collective-permute-start(bf16[120,256]{1,0:T(8,128)(2,1)S(1)} %get-tuple-element.70), channel_id=1, source_target_pairs={{0,24},{1,25},{2,26},{3,27},{4,28},{5,29},{6,30},{7,31},{8,16},{9,... | collective-permute-start | bytes 184328 | tf_op jit(solution)/shard_map/ppermute | solution.py:361
  64.0 2.4 %collective-permute-done.7.refs_3_ = bf16[120,256]{1,0:T(8,128)(2,1)S(1)} collective-permute-done((bf16[120,256]{1,0:T(8,128)(2,1)S(1)}, bf16[120,256]{1,0:T(8,128)(2,1)S(1)}, u32[]{:S(2)}, u32[]{:S(2)}) %collective-permute-start.7) | collective-permute-done | bytes 61472 | tf_op jit(solution)/shard_map/ppermute | solution.py:361
  67.4 1.4 %plane_sum.3 = (f32[120,256]{1,0:T(8,128)S(1)}, bf16[120,256]{1,0:T(8,128)(2,1)S(1)}, bf16[120,256]{1,0:T(8,128)(2,1)S(1)}, bf16[120,256]{1,0:T(8,128)(2,1)S(1)}) custom-call(s32[6]{0:T(128)S(1)} %stack.27.index, f32[4,120,256]{2,1,0:T(8,128)S(1)} %get-tuple-element.66.refs_0_, bf16[4,120,256]{2,1,0:T(8,128)(2,1)S(1)} %collective-permute-done.8.refs_1_, ...), custom_call_target="tpu_custom_call" | custom-call | flops 12386304000 | bytes 1048576 | tf_op jit(solution)/shard_map/plane_sum/pallas_call | solution.py:69
  69.4 3.1 %collective-permute-start.12 = (bf16[120,256]{1,0:T(8,128)(2,1)S(1)}, bf16[120,256]{1,0:T(8,128)(2,1)S(1)}, u32[]{:S(2)}, u32[]{:S(2)}) collective-permute-start(bf16[120,256]{1,0:T(8,128)(2,1)S(1)} %get-tuple-element.78), channel_id=1, source_target_pairs={{0,16},{1,17},{2,18},{3,19},{4,20},{5,21},{6,22},{7,23},{8,24},{9,... | collective-permute-start | bytes 184328 | tf_op jit(solution)/shard_map/ppermute | solution.py:361
  73.6 2.9 %collective-permute-done.12.refs_2_ = bf16[120,256]{1,0:T(8,128)(2,1)S(1)} collective-permute-done((bf16[120,256]{1,0:T(8,128)(2,1)S(1)}, bf16[120,256]{1,0:T(8,128)(2,1)S(1)}, u32[]{:S(2)}, u32[]{:S(2)}) %collective-permute-start.12) | collective-permute-done | bytes 61472 | tf_op jit(solution)/shard_map/ppermute | solution.py:361
  76.5 2.0 %collective-permute-done.13.refs_3_ = bf16[120,256]{1,0:T(8,128)(2,1)S(1)} collective-permute-done((bf16[120,256]{1,0:T(8,128)(2,1)S(1)}, bf16[120,256]{1,0:T(8,128)(2,1)S(1)}, u32[]{:S(2)}, u32[]{:S(2)}) %collective-permute-start.13) | collective-permute-done | bytes 61472 | tf_op jit(solution)/shard_map/ppermute | solution.py:361
  79.4 2.8 %collective-permute-start.14 = (bf16[2,120,128]{2,1,0:T(8,128)(2,1)S(1)}, bf16[2,120,128]{2,1,0:T(8,128)(2,1)S(1)}, u32[]{:S(2)}, u32[]{:S(2)}) collective-permute-start(bf16[2,120,128]{2,1,0:T(8,128)(2,1)S(1)} %get-tuple-element.83), channel_id=1, source_target_pairs={{0,0},{1,8},{2,16},{3,24},{4,4},{5,12},{6,20},{7,28},{8,1},{9,9},{... | collective-permute-start | bytes 184328 | tf_op jit(solution)/shard_map/ppermute | solution.py:361
  82.2 4.0 %collective-permute-start.15 = (bf16[2,120,128]{2,1,0:T(8,128)(2,1)S(1)}, bf16[2,120,128]{2,1,0:T(8,128)(2,1)S(1)}, u32[]{:S(2)}, u32[]{:S(2)}) collective-permute-start(bf16[2,120,128]{2,1,0:T(8,128)(2,1)S(1)} %get-tuple-element.84), channel_id=1, source_target_pairs={{0,4},{1,12},{2,20},{3,28},{4,0},{5,8},{6,16},{7,24},{8,5},{9,13},... | collective-permute-start | bytes 184328 | tf_op jit(solution)/shard_map/ppermute | solution.py:361
  86.2 1.4 %collective-permute-done.14.refs_2_ = bf16[2,120,128]{2,1,0:T(8,128)(2,1)S(1)} collective-permute-done((bf16[2,120,128]{2,1,0:T(8,128)(2,1)S(1)}, bf16[2,120,128]{2,1,0:T(8,128)(2,1)S(1)}, u32[]{:S(2)}, u32[]{:S(2)}) %collective-permute-start.14) | collective-permute-done | bytes 61472 | tf_op jit(solution)/shard_map/ppermute | solution.py:361
  87.5 1.6 %collective-permute-done.15.refs_3_ = bf16[2,120,128]{2,1,0:T(8,128)(2,1)S(1)} collective-permute-done((bf16[2,120,128]{2,1,0:T(8,128)(2,1)S(1)}, bf16[2,120,128]{2,1,0:T(8,128)(2,1)S(1)}, u32[]{:S(2)}, u32[]{:S(2)}) %collective-permute-start.15) | collective-permute-done | bytes 61472 | tf_op jit(solution)/shard_map/ppermute | solution.py:361
  89.2 1.7 %outcome.1 = f32[2,120,2,240]{3,2,1,0:T(2,128)} custom-call(s32[6]{0:T(128)S(1)} %stack.27.index, f32[120,256]{1,0:T(8,128)S(1)} %get-tuple-element.71.refs_0_, f32[120,256]{1,0:T(8,128)S(1)} %get-tuple-element.82.refs_1_, bf16[2,120,128]{2,1,0:T(8,128)(2,1)S(1)} %collective-permute-done.14.refs_2_, bf16[2,120,128]{2,1,0:T(8,128)(2,1)S(1)} %collective-permute-done.15.refs_3_), custom_call_target="tpu_custom_call" | custom-call | tf_op jit(solution)/shard_map/outcome/pallas_call | solution.py:528
  (24 shorter events, 8.1 us)
Async XLA Ops:
  22.2 4.9 %copy-start = (bf16[53760,128]{1,0:T(8,128)(2,1)}, bf16[53760,128]{1,0:T(8,128)(2,1)S(1)}, u32[]{:S(2)}) copy-start(bf16[53760,128]{1,0:T(8,128)(2,1)S(1)} %get-tuple-element.48.w) | copy-start | bytes 41287684
  22.2 4.9 %collective-permute-start = (f32[2,960,256]{2,1,0:T(8,128)S(1)}, f32[2,960,256]{2,1,0:T(8,128)S(1)}, u32[]{:S(2)}, u32[]{:S(2)}) collective-permute-start(f32[2,960,256]{2,1,0:T(8,128)S(1)} %get-tuple-element.50), channel_id=1, source_target_pairs={{0,1},{1,0},{2,3},{3,2},{4,5},{5,4},{6,7},{7,6},{8,9},{9,8},{10,11... | collective-permute-start | bytes 5898248 | tf_op jit(solution)/shard_map/ppermute | solution.py:361
  27.2 4.9 %copy-start.1 = (bf16[53760,128]{1,0:T(8,128)(2,1)S(1)}, bf16[53760,128]{1,0:T(8,128)(2,1)}, u32[]{:S(2)}) copy-start(bf16[53760,128]{1,0:T(8,128)(2,1)} %copy-done) | copy-start | bytes 41287684
  28.5 15.7 %collective-permute-start.1 = (bf16[4,120,256]{2,1,0:T(8,128)(2,1)S(1)}, bf16[4,120,256]{2,1,0:T(8,128)(2,1)S(1)}, u32[]{:S(2)}, u32[]{:S(2)}) collective-permute-start(bf16[4,120,256]{2,1,0:T(8,128)(2,1)S(1)} %get-tuple-element.54), channel_id=1, source_target_pairs={{0,6},{1,7},{2,4},{3,5},{4,2},{5,3},{6,0},{7,1},{8,14},{9,15},{10,... | collective-permute-start | bytes 737288 | tf_op jit(solution)/shard_map/ppermute | solution.py:361
  30.0 14.2 %collective-permute-start.2 = (bf16[4,120,256]{2,1,0:T(8,128)(2,1)S(1)}, bf16[4,120,256]{2,1,0:T(8,128)(2,1)S(1)}, u32[]{:S(2)}, u32[]{:S(2)}) collective-permute-start(bf16[4,120,256]{2,1,0:T(8,128)(2,1)S(1)} %get-tuple-element.55), channel_id=1, source_target_pairs={{0,2},{1,3},{2,0},{3,1},{4,6},{5,7},{6,4},{7,5},{8,10},{9,11},{10,... | collective-permute-start | bytes 737288 | tf_op jit(solution)/shard_map/ppermute | solution.py:361
  31.5 12.7 %collective-permute-start.3 = (bf16[4,120,256]{2,1,0:T(8,128)(2,1)S(1)}, bf16[4,120,256]{2,1,0:T(8,128)(2,1)S(1)}, u32[]{:S(2)}, u32[]{:S(2)}) collective-permute-start(bf16[4,120,256]{2,1,0:T(8,128)(2,1)S(1)} %get-tuple-element.56), channel_id=1, source_target_pairs={{0,4},{1,5},{2,6},{3,7},{4,0},{5,1},{6,2},{7,3},{8,12},{9,13},{10,... | collective-permute-start | bytes 737288 | tf_op jit(solution)/shard_map/ppermute | solution.py:361
  46.7 4.0 %collective-permute-start.4 = (f32[2,960,256]{2,1,0:T(8,128)S(1)}, f32[2,960,256]{2,1,0:T(8,128)S(1)}, u32[]{:S(2)}, u32[]{:S(2)}) collective-permute-start(f32[2,960,256]{2,1,0:T(8,128)S(1)} %get-tuple-element.65), channel_id=1, source_target_pairs={{0,1},{1,0},{2,3},{3,2},{4,5},{5,4},{6,7},{7,6},{8,9},{9,8},{10,11... | collective-permute-start | bytes 5898248 | tf_op jit(solution)/shard_map/ppermute | solution.py:361
  52.0 15.3 %collective-permute-start.8 = (bf16[4,120,256]{2,1,0:T(8,128)(2,1)S(1)}, bf16[4,120,256]{2,1,0:T(8,128)(2,1)S(1)}, u32[]{:S(2)}, u32[]{:S(2)}) collective-permute-start(bf16[4,120,256]{2,1,0:T(8,128)(2,1)S(1)} %get-tuple-element.73), channel_id=1, source_target_pairs={{0,6},{1,7},{2,4},{3,5},{4,2},{5,3},{6,0},{7,1},{8,14},{9,15},{10,... | collective-permute-start | bytes 737288 | tf_op jit(solution)/shard_map/ppermute | solution.py:361
  53.6 13.8 %collective-permute-start.9 = (bf16[4,120,256]{2,1,0:T(8,128)(2,1)S(1)}, bf16[4,120,256]{2,1,0:T(8,128)(2,1)S(1)}, u32[]{:S(2)}, u32[]{:S(2)}) collective-permute-start(bf16[4,120,256]{2,1,0:T(8,128)(2,1)S(1)} %get-tuple-element.74), channel_id=1, source_target_pairs={{0,2},{1,3},{2,0},{3,1},{4,6},{5,7},{6,4},{7,5},{8,10},{9,11},{10,... | collective-permute-start | bytes 737288 | tf_op jit(solution)/shard_map/ppermute | solution.py:361
  55.1 12.3 %collective-permute-start.10 = (bf16[4,120,256]{2,1,0:T(8,128)(2,1)S(1)}, bf16[4,120,256]{2,1,0:T(8,128)(2,1)S(1)}, u32[]{:S(2)}, u32[]{:S(2)}) collective-permute-start(bf16[4,120,256]{2,1,0:T(8,128)(2,1)S(1)} %get-tuple-element.75), channel_id=1, source_target_pairs={{0,4},{1,5},{2,6},{3,7},{4,0},{5,1},{6,2},{7,3},{8,12},{9,13},{10,... | collective-permute-start | bytes 737288 | tf_op jit(solution)/shard_map/ppermute | solution.py:361
  55.6 4.8 %collective-permute-start.5 = (bf16[120,256]{1,0:T(8,128)(2,1)S(1)}, bf16[120,256]{1,0:T(8,128)(2,1)S(1)}, u32[]{:S(2)}, u32[]{:S(2)}) collective-permute-start(bf16[120,256]{1,0:T(8,128)(2,1)S(1)} %get-tuple-element.68), channel_id=1, source_target_pairs={{0,8},{1,9},{2,10},{3,11},{4,12},{5,13},{6,14},{7,15},{8,0},{9,1},... | collective-permute-start | bytes 184328 | tf_op jit(solution)/shard_map/ppermute | solution.py:361
  57.1 6.9 %collective-permute-start.6 = (bf16[120,256]{1,0:T(8,128)(2,1)S(1)}, bf16[120,256]{1,0:T(8,128)(2,1)S(1)}, u32[]{:S(2)}, u32[]{:S(2)}) collective-permute-start(bf16[120,256]{1,0:T(8,128)(2,1)S(1)} %get-tuple-element.69), channel_id=1, source_target_pairs={{0,16},{1,17},{2,18},{3,19},{4,20},{5,21},{6,22},{7,23},{8,24},{9,... | collective-permute-start | bytes 184328 | tf_op jit(solution)/shard_map/ppermute | solution.py:361
  60.4 6.0 %collective-permute-start.7 = (bf16[120,256]{1,0:T(8,128)(2,1)S(1)}, bf16[120,256]{1,0:T(8,128)(2,1)S(1)}, u32[]{:S(2)}, u32[]{:S(2)}) collective-permute-start(bf16[120,256]{1,0:T(8,128)(2,1)S(1)} %get-tuple-element.70), channel_id=1, source_target_pairs={{0,24},{1,25},{2,26},{3,27},{4,28},{5,29},{6,30},{7,31},{8,16},{9,... | collective-permute-start | bytes 184328 | tf_op jit(solution)/shard_map/ppermute | solution.py:361
  68.8 4.9 %collective-permute-start.11 = (bf16[120,256]{1,0:T(8,128)(2,1)S(1)}, bf16[120,256]{1,0:T(8,128)(2,1)S(1)}, u32[]{:S(2)}, u32[]{:S(2)}) collective-permute-start(bf16[120,256]{1,0:T(8,128)(2,1)S(1)} %get-tuple-element.77), channel_id=1, source_target_pairs={{0,8},{1,9},{2,10},{3,11},{4,12},{5,13},{6,14},{7,15},{8,0},{9,1},... | collective-permute-start | bytes 184328 | tf_op jit(solution)/shard_map/ppermute | solution.py:361
  69.4 7.1 %collective-permute-start.12 = (bf16[120,256]{1,0:T(8,128)(2,1)S(1)}, bf16[120,256]{1,0:T(8,128)(2,1)S(1)}, u32[]{:S(2)}, u32[]{:S(2)}) collective-permute-start(bf16[120,256]{1,0:T(8,128)(2,1)S(1)} %get-tuple-element.78), channel_id=1, source_target_pairs={{0,16},{1,17},{2,18},{3,19},{4,20},{5,21},{6,22},{7,23},{8,24},{9,... | collective-permute-start | bytes 184328 | tf_op jit(solution)/shard_map/ppermute | solution.py:361
  72.5 6.0 %collective-permute-start.13 = (bf16[120,256]{1,0:T(8,128)(2,1)S(1)}, bf16[120,256]{1,0:T(8,128)(2,1)S(1)}, u32[]{:S(2)}, u32[]{:S(2)}) collective-permute-start(bf16[120,256]{1,0:T(8,128)(2,1)S(1)} %get-tuple-element.79), channel_id=1, source_target_pairs={{0,24},{1,25},{2,26},{3,27},{4,28},{5,29},{6,30},{7,31},{8,16},{9,... | collective-permute-start | bytes 184328 | tf_op jit(solution)/shard_map/ppermute | solution.py:361
  79.4 8.1 %collective-permute-start.14 = (bf16[2,120,128]{2,1,0:T(8,128)(2,1)S(1)}, bf16[2,120,128]{2,1,0:T(8,128)(2,1)S(1)}, u32[]{:S(2)}, u32[]{:S(2)}) collective-permute-start(bf16[2,120,128]{2,1,0:T(8,128)(2,1)S(1)} %get-tuple-element.83), channel_id=1, source_target_pairs={{0,0},{1,8},{2,16},{3,24},{4,4},{5,12},{6,20},{7,28},{8,1},{9,9},{... | collective-permute-start | bytes 184328 | tf_op jit(solution)/shard_map/ppermute | solution.py:361
  82.2 7.0 %collective-permute-start.15 = (bf16[2,120,128]{2,1,0:T(8,128)(2,1)S(1)}, bf16[2,120,128]{2,1,0:T(8,128)(2,1)S(1)}, u32[]{:S(2)}, u32[]{:S(2)}) collective-permute-start(bf16[2,120,128]{2,1,0:T(8,128)(2,1)S(1)} %get-tuple-element.84), channel_id=1, source_target_pairs={{0,4},{1,12},{2,20},{3,28},{4,0},{5,8},{6,16},{7,24},{8,5},{9,13},... | collective-permute-start | bytes 184328 | tf_op jit(solution)/shard_map/ppermute | solution.py:361

commit v6 on v5

--- a/solution.py
+++ b/solution.py
@@ -33,8 +33,9 @@
     return jnp.where(here, bound, block)
 
 
-def sent_bound(bound):
-    return jnp.maximum(bound * 1.01, 1e-35).astype(BF16).astype(F32)
+def sent_bound(bound, index):
+    more = ((5 * index[4] + 11 * index[5]) % 16).astype(F32)
+    return jnp.maximum(bound * (1.01 + 0.0037 * more), 1e-35).astype(BF16).astype(F32)
 
 
 def coded(values, bound):
@@ -372,7 +373,7 @@
 
         def chip_sum(index, kept, came):
             x, y = index[0], index[3]
-            bound = sent_bound(bound_at(kept[0, 0, 0], at) + bound_at(came[0, 0, 0], at))
+            bound = sent_bound(bound_at(kept[0, 0, 0], at) + bound_at(came[0, 0, 0], at), index)
 
             def block(x_at, y_at, z):
                 return kept[x_at, z, y_at] + came[x_at, z, y_at]
@@ -387,7 +388,7 @@
         def plane_sum(index, own, *came):
             z_own = index[2]
             bounds = [bound_at(array[0], at) for array in came]
-            bound = sent_bound(sum(bounds, bound_at(own[0], at)))
+            bound = sent_bound(sum(bounds, bound_at(own[0], at)), index)
 
             def block(z):
                 total = own[z]
@@ -410,7 +411,7 @@
                     array = array[...]
                     total = total + decoded(array, bound_at(array, at))
                     bound = bound + bound_at(array, at)
-                bound = sent_bound(bound)
+                bound = sent_bound(bound, index)
                 flipped = [total[:, h * rows : (h + 1) * rows].T for h in range(ratio)]
                 results = [total]
                 for t in range(ratio):

time: 91.8 us -> 91.9 us (level)
  no operation moved by 1% of the time
where the time goes in v6:
time: 91.9 us; the launch traced here: 90.8 us
  Pallas kernels  49.8 us (54%)
  starting transfers between devices  25.8 us (28%)
  waiting for transfers between devices  14.3 us (16%)
    ppermute x16, starting transfers between devices, send(): return lax.ppermute(block, AXES, pairs)  25.8 us
    pallas_call x1, Pallas kernels, crossed_sums(): pl.pallas_call(crossed_kernel(cols), in_specs=[SMEM, ANY, ANY], out_specs...  22.1 us
    pallas_call x2, Pallas kernels, on_chip(): pl.pallas_call(body, in_specs=[SMEM] + [VMEM] * (2 + len(arrays)), out_sp...  16.3 us
    ppermute x16, waiting for transfers between devices, send(): return lax.ppermute(block, AXES, pairs)  14.3 us
    pallas_call x6, Pallas kernels, call(): pl.pallas_call(kernel, in_specs=[SMEM] + [VMEM] * len(arrays), out_specs=...  7.22 us
    pallas_call x1, Pallas kernels, shards(): pl.pallas_call(same_kernel(cols), in_specs=[SMEM] + [VMEM] * 5, out_specs...  2.46 us
  transfers between devices with their start and end apart: 16, of which 9 were waited for; matrix products, arithmetic and copies ran while one was open for 0% of the time, Pallas kernels for 21%

profile of v6, /device:TPU:2, one launch (start us, length us, event | category | flops | bytes accessed | tf_op | source)
XLA Modules:
  0.0 90.8 jit_solution(3156822803545767436)
XLA Ops:
  0.1 22.1 %crossed.1 = (f32[2,960,256]{2,1,0:T(8,128)S(1)}, f32[2,960,256]{2,1,0:T(8,128)S(1)}, bf16[2,14,960,240]{3,2,1,0:T(8,128)(2,1)S(1)}, bf16[53760,128]{1,0:T(8,128)(2,1)S(1)}) custom-call(s32[6]{0:T(128)S(1)} %stack.27.index, bf16[2,14,960,240]{3,2,1,0:T(8,128)(2,1)} %u_hbm.1, bf16[14,240,2,960]{3,2,1,0:T(2,128)(2,1)} %w_hbm.1), custom_call_target="tpu_custom_call" | custom-call | flops 12386304000 | bytes 25804800 | tf_op jit(solution)/shard_map/crossed/pallas_call | solution.py:300
  22.3 4.2 %first_square.1.p00 = f32[480,960]{1,0:T(8,128)S(1)} custom-call(s32[6]{0:T(128)S(1)} %stack.27.index, bf16[2,14,960,240]{3,2,1,0:T(8,128)(2,1)S(1)} %get-tuple-element.47.u, bf16[53760,128]{1,0:T(8,128)(2,1)S(1)} %get-tuple-element.48.w), custom_call_target="tpu_custom_call" | custom-call | flops 3096576000 | bytes 1048576 | tf_op jit(solution)/shard_map/first_square/pallas_call | solution.py:283
  27.2 1.3 %chip_sum.2 = (f32[4,120,256]{2,1,0:T(8,128)S(1)}, bf16[4,120,256]{2,1,0:T(8,128)(2,1)S(1)}, bf16[4,120,256]{2,1,0:T(8,128)(2,1)S(1)}, bf16[4,120,256]{2,1,0:T(8,128)(2,1)S(1)}) custom-call(s32[6]{0:T(128)S(1)} %stack.27.index, f32[2,4,2,120,256]{4,3,2,1,0:T(8,128)S(1)} %bitcast.13, f32[2,4,2,120,256]{4,3,2,1,0:T(8,128)S(1)} %bitcast.12), custom_call_target="tpu_custom_call" | custom-call | flops 6193152000 | bytes 1048576 | tf_op jit(solution)/shard_map/chip_sum/pallas_call | solution.py:70
  28.5 1.6 %collective-permute-start.1 = (bf16[4,120,256]{2,1,0:T(8,128)(2,1)S(1)}, bf16[4,120,256]{2,1,0:T(8,128)(2,1)S(1)}, u32[]{:S(2)}, u32[]{:S(2)}) collective-permute-start(bf16[4,120,256]{2,1,0:T(8,128)(2,1)S(1)} %get-tuple-element.54), channel_id=1, source_target_pairs={{0,6},{1,7},{2,4},{3,5},{4,2},{5,3},{6,0},{7,1},{8,14},{9,15},{10,... | collective-permute-start | bytes 737288 | tf_op jit(solution)/shard_map/ppermute | solution.py:362
  30.0 1.5 %collective-permute-start.2 = (bf16[4,120,256]{2,1,0:T(8,128)(2,1)S(1)}, bf16[4,120,256]{2,1,0:T(8,128)(2,1)S(1)}, u32[]{:S(2)}, u32[]{:S(2)}) collective-permute-start(bf16[4,120,256]{2,1,0:T(8,128)(2,1)S(1)} %get-tuple-element.55), channel_id=1, source_target_pairs={{0,2},{1,3},{2,0},{3,1},{4,6},{5,7},{6,4},{7,5},{8,10},{9,11},{10,... | collective-permute-start | bytes 737288 | tf_op jit(solution)/shard_map/ppermute | solution.py:362
  32.1 12.1 %other_squares.1 = (f32[480,960]{1,0:T(8,128)S(1)}, f32[960,960]{1,0:T(8,128)S(1)}, f32[4,960,256]{2,1,0:T(8,128)S(1)}, f32[1,240]{1,0:T(1,128)S(1)}) custom-call(s32[6]{0:T(128)S(1)} %stack.27.index, bf16[2,14,960,240]{3,2,1,0:T(8,128)(2,1)S(1)} %get-tuple-element.47.u, bf16[53760,128]{1,0:T(8,128)(2,1)S(1)} %copy-done.1, f32[480,960]{1,0:T(8,128)S(1)} %first_square.1.p00), custom_call_target="tpu_custom_call" | custom-call | flops 9289728000 | bytes 1048576 | tf_op jit(solution)/shard_map/other_squares/pallas_call | solution.py:283
  44.2 2.5 %same.1 = (f32[2,960,256]{2,1,0:T(8,128)S(1)}, f32[2,960,256]{2,1,0:T(8,128)S(1)}, f32[4,960,256]{2,1,0:T(8,128)S(1)}) custom-call(s32[6]{0:T(128)S(1)} %stack.27.index, f32[4,960,256]{2,1,0:T(8,128)S(1)} %get-tuple-element.58.out, f32[480,960]{1,0:T(8,128)S(1)} %first_square.1.p00, ...), custom_call_target="tpu_custom_call", output_to_operand_aliasing={{2}: (1, {})} | custom-call | flops 3096576000 | bytes 1048576 | tf_op jit(solution)/shard_map/same/pallas_call | solution.py:503
  46.8 1.4 %plane_sum.2 = (f32[120,256]{1,0:T(8,128)S(1)}, bf16[120,256]{1,0:T(8,128)(2,1)S(1)}, bf16[120,256]{1,0:T(8,128)(2,1)S(1)}, bf16[120,256]{1,0:T(8,128)(2,1)S(1)}) custom-call(s32[6]{0:T(128)S(1)} %stack.27.index, f32[4,120,256]{2,1,0:T(8,128)S(1)} %get-tuple-element.51.refs_0_, bf16[4,120,256]{2,1,0:T(8,128)(2,1)S(1)} %collective-permute-done.1.refs_1_, ...), custom_call_target="tpu_custom_call" | custom-call | flops 12386304000 | bytes 1048576 | tf_op jit(solution)/shard_map/plane_sum/pallas_call | solution.py:70
  48.3 2.5 %collective-permute-done.4 = f32[2,960,256]{2,1,0:T(8,128)S(1)} collective-permute-done((f32[2,960,256]{2,1,0:T(8,128)S(1)}, f32[2,960,256]{2,1,0:T(8,128)S(1)}, u32[]{:S(2)}, u32[]{:S(2)}) %collective-permute-start.4) | collective-permute-done | bytes 1966112 | tf_op jit(solution)/shard_map/ppermute | solution.py:362
  52.0 1.6 %collective-permute-start.8 = (bf16[4,120,256]{2,1,0:T(8,128)(2,1)S(1)}, bf16[4,120,256]{2,1,0:T(8,128)(2,1)S(1)}, u32[]{:S(2)}, u32[]{:S(2)}) collective-permute-start(bf16[4,120,256]{2,1,0:T(8,128)(2,1)S(1)} %get-tuple-element.73), channel_id=1, source_target_pairs={{0,6},{1,7},{2,4},{3,5},{4,2},{5,3},{6,0},{7,1},{8,14},{9,15},{10,... | collective-permute-start | bytes 737288 | tf_op jit(solution)/shard_map/ppermute | solution.py:362
  53.6 1.5 %collective-permute-start.9 = (bf16[4,120,256]{2,1,0:T(8,128)(2,1)S(1)}, bf16[4,120,256]{2,1,0:T(8,128)(2,1)S(1)}, u32[]{:S(2)}, u32[]{:S(2)}) collective-permute-start(bf16[4,120,256]{2,1,0:T(8,128)(2,1)S(1)} %get-tuple-element.74), channel_id=1, source_target_pairs={{0,2},{1,3},{2,0},{3,1},{4,6},{5,7},{6,4},{7,5},{8,10},{9,11},{10,... | collective-permute-start | bytes 737288 | tf_op jit(solution)/shard_map/ppermute | solution.py:362
  55.6 1.6 %collective-permute-start.5 = (bf16[120,256]{1,0:T(8,128)(2,1)S(1)}, bf16[120,256]{1,0:T(8,128)(2,1)S(1)}, u32[]{:S(2)}, u32[]{:S(2)}) collective-permute-start(bf16[120,256]{1,0:T(8,128)(2,1)S(1)} %get-tuple-element.68), channel_id=1, source_target_pairs={{0,8},{1,9},{2,10},{3,11},{4,12},{5,13},{6,14},{7,15},{8,0},{9,1},... | collective-permute-start | bytes 184328 | tf_op jit(solution)/shard_map/ppermute | solution.py:362
  57.2 2.6 %collective-permute-start.6 = (bf16[120,256]{1,0:T(8,128)(2,1)S(1)}, bf16[120,256]{1,0:T(8,128)(2,1)S(1)}, u32[]{:S(2)}, u32[]{:S(2)}) collective-permute-start(bf16[120,256]{1,0:T(8,128)(2,1)S(1)} %get-tuple-element.69), channel_id=1, source_target_pairs={{0,16},{1,17},{2,18},{3,19},{4,20},{5,21},{6,22},{7,23},{8,24},{9,... | collective-permute-start | bytes 184328 | tf_op jit(solution)/shard_map/ppermute | solution.py:362
  60.4 3.1 %collective-permute-start.7 = (bf16[120,256]{1,0:T(8,128)(2,1)S(1)}, bf16[120,256]{1,0:T(8,128)(2,1)S(1)}, u32[]{:S(2)}, u32[]{:S(2)}) collective-permute-start(bf16[120,256]{1,0:T(8,128)(2,1)S(1)} %get-tuple-element.70), channel_id=1, source_target_pairs={{0,24},{1,25},{2,26},{3,27},{4,28},{5,29},{6,30},{7,31},{8,16},{9,... | collective-permute-start | bytes 184328 | tf_op jit(solution)/shard_map/ppermute | solution.py:362
  64.0 2.4 %collective-permute-done.7.refs_3_ = bf16[120,256]{1,0:T(8,128)(2,1)S(1)} collective-permute-done((bf16[120,256]{1,0:T(8,128)(2,1)S(1)}, bf16[120,256]{1,0:T(8,128)(2,1)S(1)}, u32[]{:S(2)}, u32[]{:S(2)}) %collective-permute-start.7) | collective-permute-done | bytes 61472 | tf_op jit(solution)/shard_map/ppermute | solution.py:362
  67.4 1.4 %plane_sum.3 = (f32[120,256]{1,0:T(8,128)S(1)}, bf16[120,256]{1,0:T(8,128)(2,1)S(1)}, bf16[120,256]{1,0:T(8,128)(2,1)S(1)}, bf16[120,256]{1,0:T(8,128)(2,1)S(1)}) custom-call(s32[6]{0:T(128)S(1)} %stack.27.index, f32[4,120,256]{2,1,0:T(8,128)S(1)} %get-tuple-element.66.refs_0_, bf16[4,120,256]{2,1,0:T(8,128)(2,1)S(1)} %collective-permute-done.8.refs_1_, ...), custom_call_target="tpu_custom_call" | custom-call | flops 12386304000 | bytes 1048576 | tf_op jit(solution)/shard_map/plane_sum/pallas_call | solution.py:70
  69.4 3.1 %collective-permute-start.12 = (bf16[120,256]{1,0:T(8,128)(2,1)S(1)}, bf16[120,256]{1,0:T(8,128)(2,1)S(1)}, u32[]{:S(2)}, u32[]{:S(2)}) collective-permute-start(bf16[120,256]{1,0:T(8,128)(2,1)S(1)} %get-tuple-element.78), channel_id=1, source_target_pairs={{0,16},{1,17},{2,18},{3,19},{4,20},{5,21},{6,22},{7,23},{8,24},{9,... | collective-permute-start | bytes 184328 | tf_op jit(solution)/shard_map/ppermute | solution.py:362
  73.7 2.9 %collective-permute-done.12.refs_2_ = bf16[120,256]{1,0:T(8,128)(2,1)S(1)} collective-permute-done((bf16[120,256]{1,0:T(8,128)(2,1)S(1)}, bf16[120,256]{1,0:T(8,128)(2,1)S(1)}, u32[]{:S(2)}, u32[]{:S(2)}) %collective-permute-start.12) | collective-permute-done | bytes 61472 | tf_op jit(solution)/shard_map/ppermute | solution.py:362
  76.5 2.0 %collective-permute-done.13.refs_3_ = bf16[120,256]{1,0:T(8,128)(2,1)S(1)} collective-permute-done((bf16[120,256]{1,0:T(8,128)(2,1)S(1)}, bf16[120,256]{1,0:T(8,128)(2,1)S(1)}, u32[]{:S(2)}, u32[]{:S(2)}) %collective-permute-start.13) | collective-permute-done | bytes 61472 | tf_op jit(solution)/shard_map/ppermute | solution.py:362
  79.4 2.8 %collective-permute-start.14 = (bf16[2,120,128]{2,1,0:T(8,128)(2,1)S(1)}, bf16[2,120,128]{2,1,0:T(8,128)(2,1)S(1)}, u32[]{:S(2)}, u32[]{:S(2)}) collective-permute-start(bf16[2,120,128]{2,1,0:T(8,128)(2,1)S(1)} %get-tuple-element.83), channel_id=1, source_target_pairs={{0,0},{1,8},{2,16},{3,24},{4,4},{5,12},{6,20},{7,28},{8,1},{9,9},{... | collective-permute-start | bytes 184328 | tf_op jit(solution)/shard_map/ppermute | solution.py:362
  82.2 4.0 %collective-permute-start.15 = (bf16[2,120,128]{2,1,0:T(8,128)(2,1)S(1)}, bf16[2,120,128]{2,1,0:T(8,128)(2,1)S(1)}, u32[]{:S(2)}, u32[]{:S(2)}) collective-permute-start(bf16[2,120,128]{2,1,0:T(8,128)(2,1)S(1)} %get-tuple-element.84), channel_id=1, source_target_pairs={{0,4},{1,12},{2,20},{3,28},{4,0},{5,8},{6,16},{7,24},{8,5},{9,13},... | collective-permute-start | bytes 184328 | tf_op jit(solution)/shard_map/ppermute | solution.py:362
  86.2 1.4 %collective-permute-done.14.refs_2_ = bf16[2,120,128]{2,1,0:T(8,128)(2,1)S(1)} collective-permute-done((bf16[2,120,128]{2,1,0:T(8,128)(2,1)S(1)}, bf16[2,120,128]{2,1,0:T(8,128)(2,1)S(1)}, u32[]{:S(2)}, u32[]{:S(2)}) %collective-permute-start.14) | collective-permute-done | bytes 61472 | tf_op jit(solution)/shard_map/ppermute | solution.py:362
  87.5 1.6 %collective-permute-done.15.refs_3_ = bf16[2,120,128]{2,1,0:T(8,128)(2,1)S(1)} collective-permute-done((bf16[2,120,128]{2,1,0:T(8,128)(2,1)S(1)}, bf16[2,120,128]{2,1,0:T(8,128)(2,1)S(1)}, u32[]{:S(2)}, u32[]{:S(2)}) %collective-permute-start.15) | collective-permute-done | bytes 61472 | tf_op jit(solution)/shard_map/ppermute | solution.py:362
  89.2 1.7 %outcome.1 = f32[2,120,2,240]{3,2,1,0:T(2,128)} custom-call(s32[6]{0:T(128)S(1)} %stack.27.index, f32[120,256]{1,0:T(8,128)S(1)} %get-tuple-element.71.refs_0_, f32[120,256]{1,0:T(8,128)S(1)} %get-tuple-element.82.refs_1_, bf16[2,120,128]{2,1,0:T(8,128)(2,1)S(1)} %collective-permute-done.14.refs_2_, bf16[2,120,128]{2,1,0:T(8,128)(2,1)S(1)} %collective-permute-done.15.refs_3_), custom_call_target="tpu_custom_call" | custom-call | tf_op jit(solution)/shard_map/outcome/pallas_call | solution.py:529
  (24 shorter events, 8.1 us)
Async XLA Ops:
  22.2 4.9 %copy-start = (bf16[53760,128]{1,0:T(8,128)(2,1)}, bf16[53760,128]{1,0:T(8,128)(2,1)S(1)}, u32[]{:S(2)}) copy-start(bf16[53760,128]{1,0:T(8,128)(2,1)S(1)} %get-tuple-element.48.w) | copy-start | bytes 41287684
  22.2 4.9 %collective-permute-start = (f32[2,960,256]{2,1,0:T(8,128)S(1)}, f32[2,960,256]{2,1,0:T(8,128)S(1)}, u32[]{:S(2)}, u32[]{:S(2)}) collective-permute-start(f32[2,960,256]{2,1,0:T(8,128)S(1)} %get-tuple-element.50), channel_id=1, source_target_pairs={{0,1},{1,0},{2,3},{3,2},{4,5},{5,4},{6,7},{7,6},{8,9},{9,8},{10,11... | collective-permute-start | bytes 5898248 | tf_op jit(solution)/shard_map/ppermute | solution.py:362
  27.2 4.9 %copy-start.1 = (bf16[53760,128]{1,0:T(8,128)(2,1)S(1)}, bf16[53760,128]{1,0:T(8,128)(2,1)}, u32[]{:S(2)}) copy-start(bf16[53760,128]{1,0:T(8,128)(2,1)} %copy-done) | copy-start | bytes 41287684
  28.5 15.7 %collective-permute-start.1 = (bf16[4,120,256]{2,1,0:T(8,128)(2,1)S(1)}, bf16[4,120,256]{2,1,0:T(8,128)(2,1)S(1)}, u32[]{:S(2)}, u32[]{:S(2)}) collective-permute-start(bf16[4,120,256]{2,1,0:T(8,128)(2,1)S(1)} %get-tuple-element.54), channel_id=1, source_target_pairs={{0,6},{1,7},{2,4},{3,5},{4,2},{5,3},{6,0},{7,1},{8,14},{9,15},{10,... | collective-permute-start | bytes 737288 | tf_op jit(solution)/shard_map/ppermute | solution.py:362
  30.0 14.2 %collective-permute-start.2 = (bf16[4,120,256]{2,1,0:T(8,128)(2,1)S(1)}, bf16[4,120,256]{2,1,0:T(8,128)(2,1)S(1)}, u32[]{:S(2)}, u32[]{:S(2)}) collective-permute-start(bf16[4,120,256]{2,1,0:T(8,128)(2,1)S(1)} %get-tuple-element.55), channel_id=1, source_target_pairs={{0,2},{1,3},{2,0},{3,1},{4,6},{5,7},{6,4},{7,5},{8,10},{9,11},{10,... | collective-permute-start | bytes 737288 | tf_op jit(solution)/shard_map/ppermute | solution.py:362
  31.5 12.7 %collective-permute-start.3 = (bf16[4,120,256]{2,1,0:T(8,128)(2,1)S(1)}, bf16[4,120,256]{2,1,0:T(8,128)(2,1)S(1)}, u32[]{:S(2)}, u32[]{:S(2)}) collective-permute-start(bf16[4,120,256]{2,1,0:T(8,128)(2,1)S(1)} %get-tuple-element.56), channel_id=1, source_target_pairs={{0,4},{1,5},{2,6},{3,7},{4,0},{5,1},{6,2},{7,3},{8,12},{9,13},{10,... | collective-permute-start | bytes 737288 | tf_op jit(solution)/shard_map/ppermute | solution.py:362
  46.7 4.0 %collective-permute-start.4 = (f32[2,960,256]{2,1,0:T(8,128)S(1)}, f32[2,960,256]{2,1,0:T(8,128)S(1)}, u32[]{:S(2)}, u32[]{:S(2)}) collective-permute-start(f32[2,960,256]{2,1,0:T(8,128)S(1)} %get-tuple-element.65), channel_id=1, source_target_pairs={{0,1},{1,0},{2,3},{3,2},{4,5},{5,4},{6,7},{7,6},{8,9},{9,8},{10,11... | collective-permute-start | bytes 5898248 | tf_op jit(solution)/shard_map/ppermute | solution.py:362
  52.0 15.3 %collective-permute-start.8 = (bf16[4,120,256]{2,1,0:T(8,128)(2,1)S(1)}, bf16[4,120,256]{2,1,0:T(8,128)(2,1)S(1)}, u32[]{:S(2)}, u32[]{:S(2)}) collective-permute-start(bf16[4,120,256]{2,1,0:T(8,128)(2,1)S(1)} %get-tuple-element.73), channel_id=1, source_target_pairs={{0,6},{1,7},{2,4},{3,5},{4,2},{5,3},{6,0},{7,1},{8,14},{9,15},{10,... | collective-permute-start | bytes 737288 | tf_op jit(solution)/shard_map/ppermute | solution.py:362
  53.6 13.8 %collective-permute-start.9 = (bf16[4,120,256]{2,1,0:T(8,128)(2,1)S(1)}, bf16[4,120,256]{2,1,0:T(8,128)(2,1)S(1)}, u32[]{:S(2)}, u32[]{:S(2)}) collective-permute-start(bf16[4,120,256]{2,1,0:T(8,128)(2,1)S(1)} %get-tuple-element.74), channel_id=1, source_target_pairs={{0,2},{1,3},{2,0},{3,1},{4,6},{5,7},{6,4},{7,5},{8,10},{9,11},{10,... | collective-permute-start | bytes 737288 | tf_op jit(solution)/shard_map/ppermute | solution.py:362
  55.1 12.3 %collective-permute-start.10 = (bf16[4,120,256]{2,1,0:T(8,128)(2,1)S(1)}, bf16[4,120,256]{2,1,0:T(8,128)(2,1)S(1)}, u32[]{:S(2)}, u32[]{:S(2)}) collective-permute-start(bf16[4,120,256]{2,1,0:T(8,128)(2,1)S(1)} %get-tuple-element.75), channel_id=1, source_target_pairs={{0,4},{1,5},{2,6},{3,7},{4,0},{5,1},{6,2},{7,3},{8,12},{9,13},{10,... | collective-permute-start | bytes 737288 | tf_op jit(solution)/shard_map/ppermute | solution.py:362
  55.6 4.8 %collective-permute-start.5 = (bf16[120,256]{1,0:T(8,128)(2,1)S(1)}, bf16[120,256]{1,0:T(8,128)(2,1)S(1)}, u32[]{:S(2)}, u32[]{:S(2)}) collective-permute-start(bf16[120,256]{1,0:T(8,128)(2,1)S(1)} %get-tuple-element.68), channel_id=1, source_target_pairs={{0,8},{1,9},{2,10},{3,11},{4,12},{5,13},{6,14},{7,15},{8,0},{9,1},... | collective-permute-start | bytes 184328 | tf_op jit(solution)/shard_map/ppermute | solution.py:362
  57.2 6.9 %collective-permute-start.6 = (bf16[120,256]{1,0:T(8,128)(2,1)S(1)}, bf16[120,256]{1,0:T(8,128)(2,1)S(1)}, u32[]{:S(2)}, u32[]{:S(2)}) collective-permute-start(bf16[120,256]{1,0:T(8,128)(2,1)S(1)} %get-tuple-element.69), channel_id=1, source_target_pairs={{0,16},{1,17},{2,18},{3,19},{4,20},{5,21},{6,22},{7,23},{8,24},{9,... | collective-permute-start | bytes 184328 | tf_op jit(solution)/shard_map/ppermute | solution.py:362
  60.4 6.0 %collective-permute-start.7 = (bf16[120,256]{1,0:T(8,128)(2,1)S(1)}, bf16[120,256]{1,0:T(8,128)(2,1)S(1)}, u32[]{:S(2)}, u32[]{:S(2)}) collective-permute-start(bf16[120,256]{1,0:T(8,128)(2,1)S(1)} %get-tuple-element.70), channel_id=1, source_target_pairs={{0,24},{1,25},{2,26},{3,27},{4,28},{5,29},{6,30},{7,31},{8,16},{9,... | collective-permute-start | bytes 184328 | tf_op jit(solution)/shard_map/ppermute | solution.py:362
  68.8 4.9 %collective-permute-start.11 = (bf16[120,256]{1,0:T(8,128)(2,1)S(1)}, bf16[120,256]{1,0:T(8,128)(2,1)S(1)}, u32[]{:S(2)}, u32[]{:S(2)}) collective-permute-start(bf16[120,256]{1,0:T(8,128)(2,1)S(1)} %get-tuple-element.77), channel_id=1, source_target_pairs={{0,8},{1,9},{2,10},{3,11},{4,12},{5,13},{6,14},{7,15},{8,0},{9,1},... | collective-permute-start | bytes 184328 | tf_op jit(solution)/shard_map/ppermute | solution.py:362
  69.4 7.1 %collective-permute-start.12 = (bf16[120,256]{1,0:T(8,128)(2,1)S(1)}, bf16[120,256]{1,0:T(8,128)(2,1)S(1)}, u32[]{:S(2)}, u32[]{:S(2)}) collective-permute-start(bf16[120,256]{1,0:T(8,128)(2,1)S(1)} %get-tuple-element.78), channel_id=1, source_target_pairs={{0,16},{1,17},{2,18},{3,19},{4,20},{5,21},{6,22},{7,23},{8,24},{9,... | collective-permute-start | bytes 184328 | tf_op jit(solution)/shard_map/ppermute | solution.py:362
  72.5 6.0 %collective-permute-start.13 = (bf16[120,256]{1,0:T(8,128)(2,1)S(1)}, bf16[120,256]{1,0:T(8,128)(2,1)S(1)}, u32[]{:S(2)}, u32[]{:S(2)}) collective-permute-start(bf16[120,256]{1,0:T(8,128)(2,1)S(1)} %get-tuple-element.79), channel_id=1, source_target_pairs={{0,24},{1,25},{2,26},{3,27},{4,28},{5,29},{6,30},{7,31},{8,16},{9,... | collective-permute-start | bytes 184328 | tf_op jit(solution)/shard_map/ppermute | solution.py:362
  79.4 8.1 %collective-permute-start.14 = (bf16[2,120,128]{2,1,0:T(8,128)(2,1)S(1)}, bf16[2,120,128]{2,1,0:T(8,128)(2,1)S(1)}, u32[]{:S(2)}, u32[]{:S(2)}) collective-permute-start(bf16[2,120,128]{2,1,0:T(8,128)(2,1)S(1)} %get-tuple-element.83), channel_id=1, source_target_pairs={{0,0},{1,8},{2,16},{3,24},{4,4},{5,12},{6,20},{7,28},{8,1},{9,9},{... | collective-permute-start | bytes 184328 | tf_op jit(solution)/shard_map/ppermute | solution.py:362
  82.2 7.0 %collective-permute-start.15 = (bf16[2,120,128]{2,1,0:T(8,128)(2,1)S(1)}, bf16[2,120,128]{2,1,0:T(8,128)(2,1)S(1)}, u32[]{:S(2)}, u32[]{:S(2)}) collective-permute-start(bf16[2,120,128]{2,1,0:T(8,128)(2,1)S(1)} %get-tuple-element.84), channel_id=1, source_target_pairs={{0,4},{1,12},{2,20},{3,28},{4,0},{5,8},{6,16},{7,24},{8,5},{9,13},... | collective-permute-start | bytes 184328 | tf_op jit(solution)/shard_map/ppermute | solution.py:362
